TPU v7x, 32 devices: a whole 2x2x4 slice. The times are simulated.
32 devices in a mesh: fsdp: 4 (over y, x), dp: 8 (over z, core).
Axes of the slice: x: 2, y: 2, z: 4, core: 2. Of those that a mesh axis runs over, the one named last changes fastest.
Arguments:
- tokens: bfloat16 [32768, 1024], P(('fsdp', 'dp')), may hold values from -6 to 6
- clip_frames: int32 [32, 4], P(('fsdp', 'dp')), may hold values from 0 to 3, as said below
- clip_patches: int32 [32, 4], P(('fsdp', 'dp')), may hold values from 256 to 576, as said below
- qkv_weight: bfloat16 [1024, 3072], P(('fsdp', 'dp')), may hold values from -0.1875 to 0.1875
- qkv_bias: bfloat16 [3072], P(('fsdp', 'dp')), may hold values from -3 to 3
- out_weight: bfloat16 [1024, 1024], P(('fsdp', 'dp')), may hold values from -1.5 to 1.5
- out_bias: bfloat16 [1024], P(('fsdp', 'dp')), may hold values from -2 to 2
- up_weight: bfloat16 [1024, 4096], P(('fsdp', 'dp')), may hold values from -0.1875 to 0.1875
- up_bias: bfloat16 [4096], P(('fsdp', 'dp')), may hold values from -3 to 3
- down_weight: bfloat16 [4096, 1024], P(('fsdp', 'dp')), may hold values from -0.09375 to 0.09375
- down_bias: bfloat16 [1024], P(('fsdp', 'dp')), may hold values from -2 to 2
- norm1_gain: bfloat16 [1024], P(('fsdp', 'dp')), may hold values from 0.099609375 to 1.8984375
- norm1_shift: bfloat16 [1024], P(('fsdp', 'dp')), may hold values from -2 to 2
- norm2_gain: bfloat16 [1024], P(('fsdp', 'dp')), may hold values from 0.099609375 to 1.8984375
- norm2_shift: bfloat16 [1024], P(('fsdp', 'dp')), may hold values from -2 to 2
- cotangent: bfloat16 [32768, 1024], P(('fsdp', 'dp')), may hold values from -6 to 6
Outputs:
- output: bfloat16 [32768, 1024], P(('fsdp', 'dp'))
- grad_tokens: bfloat16 [32768, 1024], P(('fsdp', 'dp'))
- grad_qkv_weight: float32 [1024, 3072], P(('fsdp', 'dp'))
- grad_qkv_bias: float32 [3072], P(('fsdp', 'dp'))
- grad_out_weight: float32 [1024, 1024], P(('fsdp', 'dp'))
- grad_out_bias: float32 [1024], P(('fsdp', 'dp'))
- grad_up_weight: float32 [1024, 4096], P(('fsdp', 'dp'))
- grad_up_bias: float32 [4096], P(('fsdp', 'dp'))
- grad_down_weight: float32 [4096, 1024], P(('fsdp', 'dp'))
- grad_down_bias: float32 [1024], P(('fsdp', 'dp'))
- grad_norm1_gain: float32 [1024], P(('fsdp', 'dp'))
- grad_norm1_shift: float32 [1024], P(('fsdp', 'dp'))
- grad_norm2_gain: float32 [1024], P(('fsdp', 'dp'))
- grad_norm2_shift: float32 [1024], P(('fsdp', 'dp'))
Inputs may be any that keep to these rules, and one draw needn't show every extreme that they name: `clip_frames`: per device, the slots' frames times (patches + 2) add up to at most 1024; 0 marks an empty slot, every device has a clip in slot 0. `clip_patches`: each entry is 256 or 576.
All inputs are finite; a program needn't handle non-finite values.
Results may differ from a plain program's by a relative error of at most 0.0077.
Values may be sent and summed in bfloat16 or wider, within the bound.
No kernel may reach another device: no remote copies, remote signals or barrier semaphores. Data moves between devices by JAX's collectives and lax.ppermute only.
A program may use at most 256 MiB of HBM per device.

v0:
```python
import jax
import jax.numpy as jnp
import numpy as np
from jax import lax
from jax.sharding import PartitionSpec as P

D = 1024
HEADS = 16
HEAD = 64
SIDE_SMALL = 16
SIDE_LARGE = 24
TOK_DEV = 1024


EPSILON = 1e-06
MASKED = -1e30


def layout(frames, patches):
    frame_tokens = patches + 2
    clip_tokens = frames * frame_tokens
    clip_starts = jnp.cumsum(clip_tokens) - clip_tokens
    positions = jnp.arange(TOK_DEV, dtype=jnp.int32)
    inside = (
        (positions[None, :] >= clip_starts[:, None])
        & (positions[None, :] < (clip_starts + clip_tokens)[:, None])
    ).astype(jnp.int32)
    slot_ids = jnp.arange(frames.shape[0], dtype=jnp.int32)
    present = jnp.sum(inside, axis=0) > 0
    segment = jnp.where(present, jnp.sum(inside * slot_ids[:, None], axis=0), -1)
    begins = jnp.sum(inside * clip_starts[:, None], axis=0)
    widths = jnp.maximum(jnp.sum(inside * frame_tokens[:, None], axis=0), 1)
    clip_sides = jnp.where(patches == SIDE_SMALL * SIDE_SMALL, SIDE_SMALL, SIDE_LARGE).astype(
        jnp.int32
    )
    sides_rows = jnp.maximum(jnp.sum(inside * clip_sides[:, None], axis=0), 1)
    offsets = positions - begins
    frame_index = offsets // widths
    within = offsets % widths
    patch_index = jnp.maximum(within - 2, 0)
    row_index = jnp.where(within >= 2, patch_index // sides_rows, 0)
    col_index = jnp.where(within >= 2, patch_index % sides_rows, 0)
    return (segment, frame_index, row_index, col_index)


def rotary_tables(frame_index, row_index, col_index):
    pair_count = HEAD // 2
    time_pairs = pair_count // 3
    row_pairs = (pair_count - time_pairs) // 2
    pair_ranks = np.arange(pair_count)
    group_ids = np.where(
        pair_ranks < time_pairs, 0, np.where(pair_ranks < time_pairs + row_pairs, 1, 2)
    )
    group_first = np.array([0, time_pairs, time_pairs + row_pairs])[group_ids]
    group_sizes = np.array([time_pairs, row_pairs, pair_count - time_pairs - row_pairs])[group_ids]
    rate_table = 10000.0 ** (-(pair_ranks - group_first) / group_sizes)
    angles = jnp.zeros((TOK_DEV, pair_count), jnp.float32)
    for group_id, place in enumerate((frame_index, row_index, col_index)):
        table = jnp.asarray(np.where(group_ids == group_id, rate_table, 0.0), jnp.float32)
        angles = angles + place.astype(jnp.float32)[:, None] * table[None, :]
    return (jnp.cos(angles), jnp.sin(angles))


def rotate(inputs, cosine, sine):
    half_size = inputs.shape[-1] // 2
    first_half = inputs[..., :half_size]
    second_half = inputs[..., half_size:]
    cos_rows = cosine[:, None, :]
    sin_rows = sine[:, None, :]
    return jnp.concatenate(
        [
            first_half * cos_rows - second_half * sin_rows,
            second_half * cos_rows + first_half * sin_rows,
        ],
        axis=-1,
    )


def layer_norm(inputs, gain, shift):
    average = jnp.mean(inputs, axis=-1, keepdims=True)
    centred = inputs - average
    variance = jnp.mean(centred * centred, axis=-1, keepdims=True)
    return centred * lax.rsqrt(variance + EPSILON) * gain + shift


def allowed(begin, row_count, segment, frame_index):
    positions = jnp.arange(TOK_DEV, dtype=jnp.int32)
    row_ids = begin + jnp.arange(row_count, dtype=jnp.int32)
    row_segment = lax.dynamic_slice_in_dim(segment, begin, row_count, 0)
    row_frame = lax.dynamic_slice_in_dim(frame_index, begin, row_count, 0)
    same_clip = (
        (row_segment[:, None] == segment[None, :])
        & (row_segment[:, None] >= 0)
        & (frame_index[None, :] <= row_frame[:, None])
    )
    return same_clip | (row_ids[:, None] == positions[None, :])


def block_scores(block_rows, keys_head, begin, row_count, segment, frame_index):
    scores = jnp.einsum(
        "qd,kd->qk", block_rows, keys_head, preferred_element_type=jnp.float32
    ) * HEAD ** (-0.5)
    return jnp.where(allowed(begin, row_count, segment, frame_index), scores, MASKED)


def attend(queries, keys_rot, values_in, segment, frame_index):
    row_count = min(512, TOK_DEV)

    def one_head(item):
        query_head, keys_head, values_head = item

        def one_block(number):
            begin = number * row_count
            block_rows = lax.dynamic_slice_in_dim(query_head, begin, row_count, 0)
            scores = block_scores(block_rows, keys_head, begin, row_count, segment, frame_index)
            highest = jnp.max(scores, axis=1, keepdims=True)
            expo = jnp.exp(scores - highest)
            totals = jnp.sum(expo, axis=1, keepdims=True)
            probs = (expo / totals).astype(jnp.bfloat16)
            result = jnp.dot(probs, values_head, preferred_element_type=jnp.float32)
            return (result, (highest + jnp.log(totals))[:, 0])

        results, log_totals = lax.map(one_block, jnp.arange(TOK_DEV // row_count, dtype=jnp.int32))
        return (results.reshape(TOK_DEV, HEAD), log_totals.reshape(TOK_DEV))

    return lax.map(one_head, (queries, keys_rot, values_in))


def attend_back(queries, keys_rot, values_in, log_totals, grad_heads, segment, frame_index):
    row_count = min(512, TOK_DEV)
    scale = HEAD ** (-0.5)

    def one_head(item):
        query_head, keys_head, values_head, log_head, grad_head = item

        def one_block(carry, number):
            grad_keys, grad_values = carry
            begin = number * row_count
            block_rows = lax.dynamic_slice_in_dim(query_head, begin, row_count, 0)
            block_grads = lax.dynamic_slice_in_dim(grad_head, begin, row_count, 0)
            block_logs = lax.dynamic_slice_in_dim(log_head, begin, row_count, 0)
            scores = block_scores(block_rows, keys_head, begin, row_count, segment, frame_index)
            probs = jnp.exp(scores - block_logs[:, None])
            grad_probs = jnp.einsum(
                "qd,kd->qk", block_grads, values_head, preferred_element_type=jnp.float32
            )
            inner = jnp.sum(probs * grad_probs, axis=1, keepdims=True)
            grad_scores = (probs * (grad_probs - inner)).astype(jnp.bfloat16)
            grad_rows = jnp.dot(grad_scores, keys_head, preferred_element_type=jnp.float32) * scale
            grad_keys = (
                grad_keys
                + jnp.einsum(
                    "qk,qd->kd", grad_scores, block_rows, preferred_element_type=jnp.float32
                )
                * scale
            )
            grad_values = grad_values + jnp.einsum(
                "qk,qd->kd",
                probs.astype(jnp.bfloat16),
                block_grads,
                preferred_element_type=jnp.float32,
            )
            return ((grad_keys, grad_values), grad_rows)

        zeros_head = jnp.zeros((TOK_DEV, HEAD), jnp.float32)
        (grad_keys, grad_values), grad_rows = lax.scan(
            one_block, (zeros_head, zeros_head), jnp.arange(TOK_DEV // row_count, dtype=jnp.int32)
        )
        return (grad_rows.reshape(TOK_DEV, HEAD), grad_keys, grad_values)

    return lax.map(one_head, (queries, keys_rot, values_in, log_totals, grad_heads))


def forward(tokens, weights, segment, frame_index, cosine, sine):
    (
        qkv_w,
        qkv_b,
        out_w,
        out_b,
        up_w,
        up_b,
        down_w,
        down_b,
        gain_one,
        shift_one,
        gain_two,
        shift_two,
    ) = weights
    inputs = tokens.astype(jnp.float32)
    normed_one = layer_norm(
        inputs, gain_one.astype(jnp.float32), shift_one.astype(jnp.float32)
    ).astype(jnp.bfloat16)
    projected = (
        jnp.dot(normed_one, qkv_w, preferred_element_type=jnp.float32) + qkv_b.astype(jnp.float32)
    ).reshape(TOK_DEV, 3, HEADS, HEAD)
    queries = rotate(projected[:, 0], cosine, sine).astype(jnp.bfloat16).transpose(1, 0, 2)
    keys_rot = rotate(projected[:, 1], cosine, sine).astype(jnp.bfloat16).transpose(1, 0, 2)
    values_in = projected[:, 2].astype(jnp.bfloat16).transpose(1, 0, 2)
    heads, log_totals = attend(queries, keys_rot, values_in, segment, frame_index)
    mixed = heads.transpose(1, 0, 2).reshape(TOK_DEV, D).astype(jnp.bfloat16)
    resid = inputs + (
        jnp.dot(mixed, out_w, preferred_element_type=jnp.float32) + out_b.astype(jnp.float32)
    )
    normed_two = layer_norm(
        resid, gain_two.astype(jnp.float32), shift_two.astype(jnp.float32)
    ).astype(jnp.bfloat16)
    pre_act = jnp.dot(normed_two, up_w, preferred_element_type=jnp.float32) + up_b.astype(
        jnp.float32
    )
    activ = jax.nn.gelu(pre_act, approximate=False).astype(jnp.bfloat16)
    final = resid + (
        jnp.dot(activ, down_w, preferred_element_type=jnp.float32) + down_b.astype(jnp.float32)
    )
    return (
        normed_one,
        queries,
        keys_rot,
        values_in,
        log_totals,
        mixed,
        resid,
        normed_two,
        pre_act,
        activ,
        final,
    )


def reduce_grads(grads):
    return lax.psum_scatter(grads, ("fsdp", "dp"), scatter_dimension=0, tiled=True)


def local(
    tokens,
    clip_frames,
    clip_patches,
    qkv_weight,
    qkv_bias,
    out_weight,
    out_bias,
    up_weight,
    up_bias,
    down_weight,
    down_bias,
    norm1_gain,
    norm1_shift,
    norm2_gain,
    norm2_shift,
    cotangent,
):
    segment, frame_index, row_index, col_index = layout(clip_frames[0], clip_patches[0])
    cosine, sine = rotary_tables(frame_index, row_index, col_index)
    weights = (
        lax.all_gather(qkv_weight, ("fsdp", "dp"), axis=0, tiled=True),
        lax.all_gather(qkv_bias, ("fsdp", "dp"), axis=0, tiled=True),
        lax.all_gather(out_weight, ("fsdp", "dp"), axis=0, tiled=True),
        lax.all_gather(out_bias, ("fsdp", "dp"), axis=0, tiled=True),
        lax.all_gather(up_weight, ("fsdp", "dp"), axis=0, tiled=True),
        lax.all_gather(up_bias, ("fsdp", "dp"), axis=0, tiled=True),
        lax.all_gather(down_weight, ("fsdp", "dp"), axis=0, tiled=True),
        lax.all_gather(down_bias, ("fsdp", "dp"), axis=0, tiled=True),
        lax.all_gather(norm1_gain, ("fsdp", "dp"), axis=0, tiled=True),
        lax.all_gather(norm1_shift, ("fsdp", "dp"), axis=0, tiled=True),
        lax.all_gather(norm2_gain, ("fsdp", "dp"), axis=0, tiled=True),
        lax.all_gather(norm2_shift, ("fsdp", "dp"), axis=0, tiled=True),
    )
    stored = forward(tokens, weights, segment, frame_index, cosine, sine)
    output = stored[-1].astype(jnp.bfloat16)
    back_weights = (
        lax.all_gather(qkv_weight, ("fsdp", "dp"), axis=0, tiled=True),
        lax.all_gather(qkv_bias, ("fsdp", "dp"), axis=0, tiled=True),
        lax.all_gather(out_weight, ("fsdp", "dp"), axis=0, tiled=True),
        lax.all_gather(out_bias, ("fsdp", "dp"), axis=0, tiled=True),
        lax.all_gather(up_weight, ("fsdp", "dp"), axis=0, tiled=True),
        lax.all_gather(up_bias, ("fsdp", "dp"), axis=0, tiled=True),
        lax.all_gather(down_weight, ("fsdp", "dp"), axis=0, tiled=True),
        lax.all_gather(down_bias, ("fsdp", "dp"), axis=0, tiled=True),
        lax.all_gather(norm1_gain, ("fsdp", "dp"), axis=0, tiled=True),
        lax.all_gather(norm1_shift, ("fsdp", "dp"), axis=0, tiled=True),
        lax.all_gather(norm2_gain, ("fsdp", "dp"), axis=0, tiled=True),
        lax.all_gather(norm2_shift, ("fsdp", "dp"), axis=0, tiled=True),
    )
    saved = forward(tokens, back_weights, segment, frame_index, cosine, sine)
    (
        qkv_w,
        qkv_b,
        out_w,
        out_b,
        up_w,
        up_b,
        down_w,
        down_b,
        gain_one,
        shift_one,
        gain_two,
        shift_two,
    ) = back_weights
    (
        normed_one,
        queries,
        keys_rot,
        values_in,
        log_totals,
        mixed,
        resid,
        normed_two,
        pre_act,
        activ,
        final,
    ) = saved
    grad_final = cotangent.astype(jnp.float32)
    grad_down_bias = jnp.sum(grad_final, axis=0)
    grad_down_weight = jnp.einsum("tf,td->fd", activ, cotangent, preferred_element_type=jnp.float32)
    grad_activ = jnp.einsum("td,fd->tf", cotangent, down_w, preferred_element_type=jnp.float32)
    gelu_out, gelu_pull = jax.vjp(lambda inner: jax.nn.gelu(inner, approximate=False), pre_act)
    grad_pre = gelu_pull(grad_activ)[0].astype(jnp.bfloat16)
    grad_up_bias = jnp.sum(grad_pre.astype(jnp.float32), axis=0)
    grad_up_weight = jnp.einsum(
        "td,tf->df", normed_two, grad_pre, preferred_element_type=jnp.float32
    )
    grad_normed_two = jnp.einsum("tf,df->td", grad_pre, up_w, preferred_element_type=jnp.float32)
    norm_out, second_pull = jax.vjp(
        layer_norm, resid, gain_two.astype(jnp.float32), shift_two.astype(jnp.float32)
    )
    grad_resid_part, grad_gain_two, grad_shift_two = second_pull(grad_normed_two)
    grad_resid = grad_final + grad_resid_part
    grad_branch = grad_resid.astype(jnp.bfloat16)
    grad_out_bias = jnp.sum(grad_branch.astype(jnp.float32), axis=0)
    grad_out_weight = jnp.einsum(
        "td,te->de", mixed, grad_branch, preferred_element_type=jnp.float32
    )
    grad_mixed = jnp.einsum(
        "te,de->td", grad_branch, out_w, preferred_element_type=jnp.float32
    ).astype(jnp.bfloat16)
    grad_heads = grad_mixed.reshape(TOK_DEV, HEADS, HEAD).transpose(1, 0, 2)
    grad_queries, grad_keys, grad_values = attend_back(
        queries, keys_rot, values_in, log_totals, grad_heads, segment, frame_index
    )
    grad_queries = rotate(grad_queries.transpose(1, 0, 2), cosine, -sine)
    grad_keys = rotate(grad_keys.transpose(1, 0, 2), cosine, -sine)
    grad_values = grad_values.transpose(1, 0, 2)
    grad_projected = (
        jnp.stack([grad_queries, grad_keys, grad_values], axis=1)
        .reshape(TOK_DEV, 3 * D)
        .astype(jnp.bfloat16)
    )
    grad_qkv_bias = jnp.sum(grad_projected.astype(jnp.float32), axis=0)
    grad_qkv_weight = jnp.einsum(
        "td,te->de", normed_one, grad_projected, preferred_element_type=jnp.float32
    )
    grad_normed_one = jnp.einsum(
        "te,de->td", grad_projected, qkv_w, preferred_element_type=jnp.float32
    )
    first_out, first_pull = jax.vjp(
        layer_norm,
        tokens.astype(jnp.float32),
        gain_one.astype(jnp.float32),
        shift_one.astype(jnp.float32),
    )
    grad_input_part, grad_gain_one, grad_shift_one = first_pull(grad_normed_one)
    grad_tokens = (grad_resid + grad_input_part).astype(jnp.bfloat16)
    summed = reduce_grads(
        (
            grad_qkv_weight,
            grad_qkv_bias,
            grad_out_weight,
            grad_out_bias,
            grad_up_weight,
            grad_up_bias,
            grad_down_weight,
            grad_down_bias,
            grad_gain_one,
            grad_shift_one,
            grad_gain_two,
            grad_shift_two,
        )
    )
    return (
        output,
        grad_tokens,
        summed[0],
        summed[1],
        summed[2],
        summed[3],
        summed[4],
        summed[5],
        summed[6],
        summed[7],
        summed[8],
        summed[9],
        summed[10],
        summed[11],
    )


def solution(mesh):
    placed = (
        P(("fsdp", "dp"), None),
        P(("fsdp", "dp"), None),
        P(("fsdp", "dp"), None),
        P(("fsdp", "dp"), None),
        P(("fsdp", "dp")),
        P(("fsdp", "dp"), None),
        P(("fsdp", "dp")),
        P(("fsdp", "dp"), None),
        P(("fsdp", "dp")),
        P(("fsdp", "dp"), None),
        P(("fsdp", "dp")),
        P(("fsdp", "dp")),
        P(("fsdp", "dp")),
        P(("fsdp", "dp")),
        P(("fsdp", "dp")),
        P(("fsdp", "dp"), None),
    )
    return jax.shard_map(
        local,
        mesh=mesh,
        in_specs=placed,
        out_specs=(
            P(("fsdp", "dp"), None),
            P(("fsdp", "dp"), None),
            P(("fsdp", "dp"), None),
            P(("fsdp", "dp")),
            P(("fsdp", "dp"), None),
            P(("fsdp", "dp")),
            P(("fsdp", "dp"), None),
            P(("fsdp", "dp")),
            P(("fsdp", "dp"), None),
            P(("fsdp", "dp")),
            P(("fsdp", "dp")),
            P(("fsdp", "dp")),
            P(("fsdp", "dp")),
            P(("fsdp", "dp")),
        ),
        check_vma=False,
    )
```

profile of v0, /device:TPU:0, one launch (start us, length us, event | category | flops | bytes accessed | tf_op | source)
XLA Modules:
  0.0 1574.5 jit_solution(12183455633189355191)
XLA Ops:
  14.7 42.8 %all-reduce.16 = (bf16[1024]{0:T(1024)(128)(2,1)S(1)}, bf16[3072]{0:T(1024)(128)(2,1)S(1)}, bf16[1024]{0:T(1024)(128)(2,1)S(1)}, bf16[1024]{0:T(1024)(128)(2,1)S...) all-reduce(bf16[1024]{0:T(1024)(128)(2,1)S(1)} %dynamic-update-slic, ...), channel_id=1, replica_groups=mesh['fsdp'=4,'dp'=8] {'fsdp','dp'}, use_global_device_ids=true, to_apply=%add.3 | all-reduce | flops 9216 | bytes 36864
  62.7 40.7 %all-gather = bf16[32,1,128]{2,1,0:T(2,128)(2,1)S(1)} all-gather(bf16[1,1,128]{2,1,0:T(2,128)(2,1)S(1)} %bitcast.229), channel_id=1, replica_groups=mesh['fsdp'=4,'dp'=8] {'fsdp','dp'}, dimensions={0}, use_global_device_ids=true | all-gather | bytes 8448 | tf_op jit(solution)/shard_map/all_gather | solution.py:259
  166.4 192.2 %while.85 = (s32[]{:T(128)}, bf16[16,1024,64]{1,2,0:T(8,128)(2,1)}, f32[16,1024]{1,0:T(8,128)}, bf16[16,1024,64]{2,1,0:T(8,128)(2,1)}, bf16[16,1024,64]{2,1,0:T(...) while((s32[]{:T(128)}, bf16[16,1024,64]{1,2,0:T(8,128)(2,1)}, ...), condition=%wide.region_21.22_spmd.clone, body=%wide.region_16.21_spmd.sunk.clone | while | flops 141558272 | bytes 8713692 | solution.py:126
  383.8 51.8 %convert_reduce_fusion = (f32[4096]{0:T(1024)}, bf16[1024,4096]{1,0:T(8,128)(2,1)S(1)}, f32[1024,4096]{1,0:T(8,128)}) fusion(f32[1024,4096]{1,0:T(8,128)} %fusion.120, f32[4096]{0:T(1024)S(1)} %bitcast.225, bf16[1024,1024]{1,0:T(8,128)(2,1)S(1)} %copy-done.22, bf16[4096,1024]{1,0:T(8,128)(2,1)} %all-gather.12.cloned.1.call-done), kind=kOutput, calls=%fused_computation.71 | convolution fusion | flops 8904503296 | bytes 52461568 | tf_op jit(solution)/shard_map/td,fd->tf/dot_general | solution.py:314
  479.5 538.1 %while.87 = (s32[]{:T(128)}, f32[16,1024,64]{1,2,0:T(8,128)}, f32[16,1024,64]{1,2,0:T(8,128)}, bf16[16,1024,64]{1,2,0:T(8,128)(2,1)}, bf16[16,1024,64]{2,1,0:T(8...) while((s32[]{:T(128)}, f32[16,1024,64]{1,2,0:T(8,128)}, ...), condition=%wide.region_30.31_spmd.clone, body=%wide.region_26.30_spmd.sunk.clone | while | flops 343769600 | bytes 23899788 | solution.py:171
  487.4 22.4 %while.86 = (s32[]{:T(128)}, f32[1024,64]{0,1:T(8,128)}, f32[1024,64]{0,1:T(8,128)S(1)}, f32[2,512,64]{1,2,0:T(8,128)}, s32[2]{0:T(128)S(1)}, /*index=5*/s32[102...) while((s32[]{:T(128)}, f32[1024,64]{0,1:T(8,128)}, ...), condition=%wide.region_29.29_spmd.clone, body=%wide.region_27.28_spmd.clone.sunk | while | flops 343769600 | bytes 20221244 | solution.py:166
  521.0 22.4 %while.86 = (s32[]{:T(128)}, f32[1024,64]{0,1:T(8,128)}, f32[1024,64]{0,1:T(8,128)S(1)}, f32[2,512,64]{1,2,0:T(8,128)}, s32[2]{0:T(128)S(1)}, /*index=5*/s32[102...) while((s32[]{:T(128)}, f32[1024,64]{0,1:T(8,128)}, ...), condition=%wide.region_29.29_spmd.clone, body=%wide.region_27.28_spmd.clone.sunk | while | flops 343769600 | bytes 20221244 | solution.py:166
  554.7 22.4 %while.86 = (s32[]{:T(128)}, f32[1024,64]{0,1:T(8,128)}, f32[1024,64]{0,1:T(8,128)S(1)}, f32[2,512,64]{1,2,0:T(8,128)}, s32[2]{0:T(128)S(1)}, /*index=5*/s32[102...) while((s32[]{:T(128)}, f32[1024,64]{0,1:T(8,128)}, ...), condition=%wide.region_29.29_spmd.clone, body=%wide.region_27.28_spmd.clone.sunk | while | flops 343769600 | bytes 20221244 | solution.py:166
  588.3 22.4 %while.86 = (s32[]{:T(128)}, f32[1024,64]{0,1:T(8,128)}, f32[1024,64]{0,1:T(8,128)S(1)}, f32[2,512,64]{1,2,0:T(8,128)}, s32[2]{0:T(128)S(1)}, /*index=5*/s32[102...) while((s32[]{:T(128)}, f32[1024,64]{0,1:T(8,128)}, ...), condition=%wide.region_29.29_spmd.clone, body=%wide.region_27.28_spmd.clone.sunk | while | flops 343769600 | bytes 20221244 | solution.py:166
  621.9 22.4 %while.86 = (s32[]{:T(128)}, f32[1024,64]{0,1:T(8,128)}, f32[1024,64]{0,1:T(8,128)S(1)}, f32[2,512,64]{1,2,0:T(8,128)}, s32[2]{0:T(128)S(1)}, /*index=5*/s32[102...) while((s32[]{:T(128)}, f32[1024,64]{0,1:T(8,128)}, ...), condition=%wide.region_29.29_spmd.clone, body=%wide.region_27.28_spmd.clone.sunk | while | flops 343769600 | bytes 20221244 | solution.py:166
  655.5 22.4 %while.86 = (s32[]{:T(128)}, f32[1024,64]{0,1:T(8,128)}, f32[1024,64]{0,1:T(8,128)S(1)}, f32[2,512,64]{1,2,0:T(8,128)}, s32[2]{0:T(128)S(1)}, /*index=5*/s32[102...) while((s32[]{:T(128)}, f32[1024,64]{0,1:T(8,128)}, ...), condition=%wide.region_29.29_spmd.clone, body=%wide.region_27.28_spmd.clone.sunk | while | flops 343769600 | bytes 20221244 | solution.py:166
  689.1 22.4 %while.86 = (s32[]{:T(128)}, f32[1024,64]{0,1:T(8,128)}, f32[1024,64]{0,1:T(8,128)S(1)}, f32[2,512,64]{1,2,0:T(8,128)}, s32[2]{0:T(128)S(1)}, /*index=5*/s32[102...) while((s32[]{:T(128)}, f32[1024,64]{0,1:T(8,128)}, ...), condition=%wide.region_29.29_spmd.clone, body=%wide.region_27.28_spmd.clone.sunk | while | flops 343769600 | bytes 20221244 | solution.py:166
  722.7 22.4 %while.86 = (s32[]{:T(128)}, f32[1024,64]{0,1:T(8,128)}, f32[1024,64]{0,1:T(8,128)S(1)}, f32[2,512,64]{1,2,0:T(8,128)}, s32[2]{0:T(128)S(1)}, /*index=5*/s32[102...) while((s32[]{:T(128)}, f32[1024,64]{0,1:T(8,128)}, ...), condition=%wide.region_29.29_spmd.clone, body=%wide.region_27.28_spmd.clone.sunk | while | flops 343769600 | bytes 20221244 | solution.py:166
  756.2 22.4 %while.86 = (s32[]{:T(128)}, f32[1024,64]{0,1:T(8,128)}, f32[1024,64]{0,1:T(8,128)S(1)}, f32[2,512,64]{1,2,0:T(8,128)}, s32[2]{0:T(128)S(1)}, /*index=5*/s32[102...) while((s32[]{:T(128)}, f32[1024,64]{0,1:T(8,128)}, ...), condition=%wide.region_29.29_spmd.clone, body=%wide.region_27.28_spmd.clone.sunk | while | flops 343769600 | bytes 20221244 | solution.py:166
  789.8 22.4 %while.86 = (s32[]{:T(128)}, f32[1024,64]{0,1:T(8,128)}, f32[1024,64]{0,1:T(8,128)S(1)}, f32[2,512,64]{1,2,0:T(8,128)}, s32[2]{0:T(128)S(1)}, /*index=5*/s32[102...) while((s32[]{:T(128)}, f32[1024,64]{0,1:T(8,128)}, ...), condition=%wide.region_29.29_spmd.clone, body=%wide.region_27.28_spmd.clone.sunk | while | flops 343769600 | bytes 20221244 | solution.py:166
  857.0 22.4 %while.86 = (s32[]{:T(128)}, f32[1024,64]{0,1:T(8,128)}, f32[1024,64]{0,1:T(8,128)S(1)}, f32[2,512,64]{1,2,0:T(8,128)}, s32[2]{0:T(128)S(1)}, /*index=5*/s32[102...) while((s32[]{:T(128)}, f32[1024,64]{0,1:T(8,128)}, ...), condition=%wide.region_29.29_spmd.clone, body=%wide.region_27.28_spmd.clone.sunk | while | flops 343769600 | bytes 20221244 | solution.py:166
  890.6 22.4 %while.86 = (s32[]{:T(128)}, f32[1024,64]{0,1:T(8,128)}, f32[1024,64]{0,1:T(8,128)S(1)}, f32[2,512,64]{1,2,0:T(8,128)}, s32[2]{0:T(128)S(1)}, /*index=5*/s32[102...) while((s32[]{:T(128)}, f32[1024,64]{0,1:T(8,128)}, ...), condition=%wide.region_29.29_spmd.clone, body=%wide.region_27.28_spmd.clone.sunk | while | flops 343769600 | bytes 20221244 | solution.py:166
  924.2 22.4 %while.86 = (s32[]{:T(128)}, f32[1024,64]{0,1:T(8,128)}, f32[1024,64]{0,1:T(8,128)S(1)}, f32[2,512,64]{1,2,0:T(8,128)}, s32[2]{0:T(128)S(1)}, /*index=5*/s32[102...) while((s32[]{:T(128)}, f32[1024,64]{0,1:T(8,128)}, ...), condition=%wide.region_29.29_spmd.clone, body=%wide.region_27.28_spmd.clone.sunk | while | flops 343769600 | bytes 20221244 | solution.py:166
  957.8 22.4 %while.86 = (s32[]{:T(128)}, f32[1024,64]{0,1:T(8,128)}, f32[1024,64]{0,1:T(8,128)S(1)}, f32[2,512,64]{1,2,0:T(8,128)}, s32[2]{0:T(128)S(1)}, /*index=5*/s32[102...) while((s32[]{:T(128)}, f32[1024,64]{0,1:T(8,128)}, ...), condition=%wide.region_29.29_spmd.clone, body=%wide.region_27.28_spmd.clone.sunk | while | flops 343769600 | bytes 20221244 | solution.py:166
  991.4 22.4 %while.86 = (s32[]{:T(128)}, f32[1024,64]{0,1:T(8,128)}, f32[1024,64]{0,1:T(8,128)S(1)}, f32[2,512,64]{1,2,0:T(8,128)}, s32[2]{0:T(128)S(1)}, /*index=5*/s32[102...) while((s32[]{:T(128)}, f32[1024,64]{0,1:T(8,128)}, ...), condition=%wide.region_29.29_spmd.clone, body=%wide.region_27.28_spmd.clone.sunk | while | flops 343769600 | bytes 20221244 | solution.py:166
  1078.3 168.5 %while.83 = (s32[]{:T(128)}, bf16[16,1024,64]{1,2,0:T(8,128)(2,1)}, bf16[16,1024,64]{2,1,0:T(8,128)(2,1)}, bf16[16,1024,64]{2,1,0:T(8,128)(2,1)}, bf16[16,1024,6...) while((s32[]{:T(128)}, bf16[16,1024,64]{1,2,0:T(8,128)(2,1)}, ...), condition=%wide.region_13.14_spmd.clone, body=%wide.region_8.13_spmd.sunk.clone | while | flops 141557760 | bytes 8687036 | solution.py:126
  1254.0 48.2 %fusion.169 = bf16[1024,4096]{1,0:T(8,128)(2,1)} fusion(f32[4096]{0:T(1024)S(1)} %bitcast.227, bf16[1024,4096]{1,0:T(8,128)(2,1)S(1)} %bitcast.231, f32[1024,1024]{0,1:T(8,128)S(1)} %get-tuple-element.705, f32[1024]{0:T(1024)S(1)} %copy-done.60, f32[1024]{0:T(1024)S(1)} %copy-done.44, f32[1024]{0:T(1024)S(1)} %add_rsqrt_fusion, ...), kind=kOutput, calls=%fused_computation.68.clone.clone.clone.clone.1 | convolution fusion | flops 8872001536 | bytes 21004288 | tf_op jit(solution)/shard_map/dot_general | solution.py:207
  1351.0 39.1 %all-reduce.15 = (f32[3072]{0:T(1024)S(1)}, f32[1024]{0:T(1024)S(1)}, f32[4096]{0:T(1024)S(1)}, f32[1024]{0:T(1024)S(1)}, f32[1024]{0:T(1024)S(1)}, /*index=5*/f...) all-reduce(f32[3072]{0:T(1024)S(1)} %reduce_sum.262, ...), channel_id=3, replica_groups=mesh['fsdp'=4,'dp'=8] {'fsdp','dp'}, use_global_device_ids=true, to_apply=%region_35.36.clone | all-reduce | flops 13312 | bytes 106496
  1394.8 172.7 %reduce-scatter.11.cloned.1.call-done = f32[128,1024]{1,0:T(8,128)} async-done(((f32[4096,1024]{1,0:T(8,128)}), f32[128,1024]{1,0:T(8,128)}) %reduce-scatter.11.cloned.1.call-update) | async-done | bytes 524304 | tf_op jit(solution)/shard_map/reduce_scatter | solution.py:230
  (1786 shorter events, 1358.0 us)
Async XLA Ops:
  7.2 103.6 %all-gather.6.cloned.1.call-start = ((), (), s32[]{:S(2)}) async-start(), calls=%async_computation.4 | async-start | bytes 6488064 | tf_op jit(solution)/shard_map/all_gather | solution.py:254
  7.9 350.7 %all-gather.8.cloned.1.call-start = ((), (), s32[]{:S(2)}) async-start(), calls=%async_computation.5 | async-start | bytes 2162688 | tf_op jit(solution)/shard_map/all_gather | solution.py:256
  8.7 358.1 %all-gather.10.cloned.1.call-start = ((), (), s32[]{:S(2)}) async-start(), calls=%async_computation.6 | async-start | bytes 8650752 | tf_op jit(solution)/shard_map/all_gather | solution.py:258
  9.4 374.4 %all-gather.12.cloned.1.call-start = ((), (), s32[]{:S(2)}) async-start(), calls=%async_computation.7 | async-start | bytes 8650752 | tf_op jit(solution)/shard_map/all_gather | solution.py:260
  10.0 1384.8 %reduce-scatter.7.cloned.1.call-start = ((), (), s32[]{:S(2)}) async-start(), calls=%async_computation.9 | async-start | bytes 4325376 | tf_op jit(solution)/shard_map/reduce_scatter | solution.py:230
  61.0 297.6 %copy-start = (bf16[1024,1024]{0,1:T(8,128)(2,1)}, bf16[1024,1024]{0,1:T(8,128)(2,1)S(1)}, u32[]{:S(2)}) copy-start(bf16[1024,1024]{0,1:T(8,128)(2,1)S(1)} %copy.117) | copy-start | bytes 6291460
  61.1 49.8 %copy-start.61 = (f32[1024]{0:T(1024)}, f32[1024]{0:T(1024)S(1)}, u32[]{:S(2)}) copy-start(f32[1024]{0:T(1024)S(1)} %convert_element_type.154) | copy-start | bytes 12292
  61.1 49.7 %copy-start.31 = (f32[1024]{0:T(1024)}, f32[1024]{0:T(1024)S(1)}, u32[]{:S(2)}) copy-start(f32[1024]{0:T(1024)S(1)} %convert_element_type.153) | copy-start | bytes 12292
  61.1 48.5 %copy-start.68 = (f32[32]{0:T(128)S(1)}, f32[32]{0:T(128)}, u32[]{:S(2)}) copy-start(f32[32]{0:T(128)} %constant.243.clone) | copy-start | bytes 388
  61.1 48.5 %copy-start.69 = (f32[32]{0:T(128)S(1)}, f32[32]{0:T(128)}, u32[]{:S(2)}) copy-start(f32[32]{0:T(128)} %constant.242.clone) | copy-start | bytes 388
  61.1 48.5 %copy-start.70 = (f32[32]{0:T(128)S(1)}, f32[32]{0:T(128)}, u32[]{:S(2)}) copy-start(f32[32]{0:T(128)} %constant.241.clone) | copy-start | bytes 388
  61.5 62.1 %copy-start.27 = (f32[1024]{0:T(1024)}, f32[1024]{0:T(1024)S(1)}, u32[]{:S(2)}) copy-start(f32[1024]{0:T(1024)S(1)} %broadcast_multiply_fusion.2) | copy-start | bytes 12292
  62.2 61.5 %copy-start.39 = (f32[1024]{0:T(1024)}, f32[1024]{0:T(1024)S(1)}, u32[]{:S(2)}) copy-start(f32[1024]{0:T(1024)S(1)} %fusion.81) | copy-start | bytes 12292
  110.8 33.8 %copy-start.25 = (f32[1024,32]{0,1:T(8,128)}, f32[1024,32]{0,1:T(8,128)S(1)}, u32[]{:S(2)}) copy-start(f32[1024,32]{0,1:T(8,128)S(1)} %get-tuple-element.696) | copy-start | bytes 393220
  166.4 192.2 %copy-start.57 = (f32[1024]{0:T(1024)S(1)}, f32[1024]{0:T(1024)}, u32[]{:S(2)}) copy-start(f32[1024]{0:T(1024)} %convert_element_type.165) | copy-start | bytes 12292
  363.7 20.0 %copy-start.34 = (f32[1024]{0:T(1024)}, f32[1024]{0:T(1024)S(1)}, u32[]{:S(2)}) copy-start(f32[1024]{0:T(1024)S(1)} %broadcast_multiply_fusion) | copy-start | bytes 12292
  383.8 51.8 %copy-start.72 = (bf16[1024,4096]{1,0:T(8,128)(2,1)S(1)}, bf16[1024,4096]{1,0:T(8,128)(2,1)}, u32[]{:S(2)}) copy-start(bf16[1024,4096]{1,0:T(8,128)(2,1)} %all-gather.10.cloned.1.call-done) | copy-start | bytes 25165828
  476.9 917.9 %reduce-scatter.5.cloned.1.call-start = ((), (), s32[]{:S(2)}) async-start(), calls=%async_computation.8 | async-start | bytes 12976128 | tf_op jit(solution)/shard_map/reduce_scatter | solution.py:230
  479.5 538.1 %copy-start.26 = (f32[1024,32]{0,1:T(8,128)S(1)}, f32[1024,32]{0,1:T(8,128)}, u32[]{:S(2)}) copy-start(f32[1024,32]{0,1:T(8,128)} %copy-done.25) | copy-start | bytes 393220
  1037.8 357.0 %reduce-scatter.9.cloned.1.call-start = ((), (), s32[]{:S(2)}) async-start(), calls=%async_computation.10 | async-start | bytes 17301504 | tf_op jit(solution)/shard_map/reduce_scatter | solution.py:230
  1055.6 511.9 %reduce-scatter.11.cloned.1.call-start = ((), (), s32[]{:S(2)}) async-start(), calls=%async_computation.11 | async-start | bytes 17301504 | tf_op jit(solution)/shard_map/reduce_scatter | solution.py:230
  1078.2 168.6 %copy-start.2 = (bf16[1024,1024]{0,1:T(8,128)(2,1)S(1)}, bf16[1024,1024]{0,1:T(8,128)(2,1)}, u32[]{:S(2)}) copy-start(bf16[1024,1024]{0,1:T(8,128)(2,1)} %copy-done) | copy-start | bytes 6291460
  1078.2 168.6 %copy-start.58 = (f32[1024]{0:T(1024)S(1)}, f32[1024]{0:T(1024)}, u32[]{:S(2)}) copy-start(f32[1024]{0:T(1024)} %convert_element_type.165) | copy-start | bytes 12292
  1254.0 48.2 %copy-start.63 = (f32[1024]{0:T(1024)S(1)}, f32[1024]{0:T(1024)}, u32[]{:S(2)}) copy-start(f32[1024]{0:T(1024)} %convert_element_type.171) | copy-start | bytes 12292
  (129 other events, 403.2 us)
Sparse Core Ops, SparseCore 0:
  11.0 72.5 all-gather.5
  86.5 55.0 all-gather.7
  144.7 76.1 all-gather.9
  223.6 76.2 all-gather.11
  477.0 139.4 reduce-scatter.6
  1037.9 152.9 reduce-scatter.4
  1193.9 186.5 reduce-scatter.8
  1383.5 183.9 reduce-scatter.10
where the time goes:
time: 1590 us; the launch traced here: 1570 us
  matrix products  627 us (39%)
  local copies, waits for them, and re-layouts  478 us (30%)
  waiting for transfers between devices  175 us (11%)
  blocking collectives  123 us (8%)
  other arithmetic  87.5 us (6%)
  loops' own time  69 us (4%)
    reduce_scatter x4, waiting for transfers between devices, reduce_grads(): lax.psum_scatter(grads, ('fsdp', 'dp'), scatter_dimension=0, tiled=True)  173 us
    squeeze x128, local copies, waits for them, and re-layouts, attend(): return lax.map(one_head, (queries, keys_rot, values_in))  172 us
    dot_general x96, matrix products, block_scores(): jnp.einsum('qd,kd->qk', block_rows, keys_head, preferred_element_type=jnp...  154 us
    dynamic_update_slice x128, local copies, waits for them, and re-layouts, attend(): return lax.map(one_head, (queries, keys_rot, values_in))  89.7 us
    unnamed x2, blocking collectives  81.9 us
    dot_general x32, matrix products, one_block(): jnp.einsum('qk,qd->kd', grad_scores, block_rows, preferred_element_type=j...  65.6 us
    dot_general x2, matrix products, forward(): jnp.dot(normed_two, up_w, preferred_element_type=jnp.float32)  65.1 us
    dynamic_slice x96, local copies, waits for them, and re-layouts, one_head(): lax.map(one_block, jnp.arange(TOK_DEV // row_count, dtype=jnp.int32))  56.2 us
  transfers between devices with their start and end apart: 8, of which 1 were waited for; matrix products, arithmetic and copies ran while one was open for 68% of the time, Pallas kernels for 0%

commit v1 on v0

v1 whole, which is shorter than its diff:
```python
import functools

import jax
import jax.numpy as jnp
import numpy as np
from jax import lax
from jax.experimental import pallas as pl
from jax.experimental.pallas import tpu as pltpu
from jax.sharding import PartitionSpec as P

D = 1024
HEADS = 16
HEAD = 64
FF = 4096
SIDE_SMALL = 16
SIDE_LARGE = 24
TOK_DEV = 1024
AXES = ("fsdp", "dp")
EPSILON = 1e-06
MASKED = -1e30
BQ = 256
BK = 128
LANES = 128
TILE = 512
ROWS = 256
F32 = jnp.float32
BF = jnp.bfloat16
VMEM_BYTES = 56 << 20
WEIGHT = 1.15e10


def cost(microseconds):
    return pl.CostEstimate(flops=int(microseconds * WEIGHT), bytes_accessed=0, transcendentals=0)


def nt(left, right):
    return lax.dot_general(left, right, (((1,), (1,)), ((), ())), preferred_element_type=F32)


def nn(left, right):
    return jnp.dot(left, right, preferred_element_type=F32)


SMEM = pl.BlockSpec(memory_space=pltpu.SMEM)
ANY = pl.BlockSpec(memory_space=pl.ANY)


def fixed(*shape):
    return pl.BlockSpec(shape, lambda *_: (0,) * len(shape))


def pallas(kernel, operands, in_specs, after=(), **kept):
    given = len(operands)

    def body(*refs):
        kernel(*refs[:given], *refs[given + len(after) :])

    return pl.pallas_call(
        body,
        in_specs=list(in_specs) + [ANY] * len(after),
        compiler_params=pltpu.CompilerParams(vmem_limit_bytes=VMEM_BYTES),
        **kept,
    )(*operands, *after)


class Relay:
    def __init__(self):
        self.inputs, self.outs, self.jobs = [], [], []

    def take(self, array):
        for place, known in enumerate(self.inputs):
            if known is array:
                return place
        self.inputs.append(array)
        return len(self.inputs) - 1

    def make(self, rows, columns, dtype):
        self.outs.append(((rows, columns), dtype))
        return len(self.outs) - 1

    def put(self, out, row, column, rows, columns, terms):
        self.jobs.append((out, row, column, rows, columns, [(self.take(array), *at) for array, *at in terms]))

    def run(self, after=(), name="relay"):
        jobs, given = self.jobs, len(self.inputs)

        def kernel(*refs):
            sources, targets = refs[:given], refs[given:]
            for out, row, column, rows, columns, terms in jobs:
                step = next(size for size in (64, 32, 16) if rows % size == 0)

                @pl.loop(0, rows // step)
                def _(index):
                    def part(ref, row, column):
                        begin = pl.multiple_of(row + index * step, 16)
                        return ref.at[pl.ds(begin, step), column : column + columns]

                    total = part(sources[terms[0][0]], *terms[0][1:])[...]
                    for source, *at in terms[1:]:
                        total = total.astype(F32) + part(sources[source], *at)[...].astype(F32)
                    part(targets[out], row, column)[...] = total.astype(targets[out].dtype)

        moved = sum(2 * shape[0] * shape[1] * 3 for shape, _ in self.outs)
        return pallas(
            kernel,
            self.inputs,
            [fixed(*array.shape) for array in self.inputs],
            after,
            out_specs=[fixed(*shape) for shape, _ in self.outs],
            out_shape=[jax.ShapeDtypeStruct(shape, dtype) for shape, dtype in self.outs],
            cost_estimate=cost(1 + moved * 0.4e-6),
            name=name,
        )


BLOCKS = 32
UPPER = ((16, 8), (8, 16))


class Net:
    def __init__(self, count):
        self.count, self.share = count, max(count // BLOCKS, 1)
        self.number = lax.axis_index(AXES).astype(jnp.int32)
        self.me = self.number // self.share

    def swap(self, value, mask):
        return self.permute(value, mask * self.share)

    def permute(self, value, mask):
        return lax.ppermute(value, AXES, [(number, number ^ mask) for number in range(self.count)])

    def bits(self):
        return [1 << place for place in range(self.share.bit_length() - 1)]

    def widen(self, shard):
        for bit in self.bits():
            other = self.permute(shard, bit)
            shard = jnp.where(
                self.number & bit, jnp.concatenate([other, shard], 0), jnp.concatenate([shard, other], 0)
            )
        return shard

    def narrow(self, total):
        for bit in self.bits()[::-1]:
            low, high = jnp.split(total, 2, 0)
            own = jnp.where(self.number & bit, high, low)
            total = own + self.permute(jnp.where(self.number & bit, low, high), bit)
        return total

    def over_all(self, value):
        for place in range(self.count.bit_length() - 1):
            value = value + self.permute(value, 1 << place)
        return value


def runs_of(places):
    runs = []
    for position, place in enumerate(places):
        if runs and runs[-1][1] + runs[-1][2] == place:
            runs[-1][2] += 1
        else:
            runs.append([position, place, 1])
    return runs


def parted(places, mask):
    return [[position for position, place in enumerate(places) if bool(place & mask) == with_it] for with_it in (False, True)]


class Gather:
    def __init__(self, net, shard):
        self.net, self.rows, self.half = net, shard.shape[0], shard.shape[1] // 2
        self.blocks = [[0]] * 2
        self.stage = 0
        self.held = [(shard, net.swap(shard, 2))]

    def join(self, relay):
        rows, half = self.rows, self.half
        self.made = []
        if self.stage == 0:
            self.made.append(relay.make(2 * rows, 2 * half, BF))
            for place, array in enumerate(self.held[0]):
                relay.put(self.made[0], place * rows, 0, rows, 2 * half, [(array, 0, 0)])
            self.blocks = [[0, 2]] * 2
        elif self.stage == 1:
            for side in range(2):
                self.made.append(relay.make(4 * rows, half, BF))
                for place, array in enumerate(self.held[0]):
                    relay.put(self.made[side], 2 * place * rows, 0, 2 * rows, half, [(array, 0, side * half)])
            self.blocks = [[0, 2, 4, 6]] * 2
        elif self.stage == 2:
            for side in range(2):
                self.made.append(relay.make(8 * rows, half, BF))
                for place, array in enumerate(self.held[side]):
                    relay.put(self.made[side], 4 * place * rows, 0, 4 * rows, half, [(array, 0, 0)])
                self.blocks[side] = self.blocks[side] + [block ^ UPPER[side][0] for block in self.blocks[side]]

    def follow(self, made):
        arrays = [made[place] for place in self.made]
        self.stage += 1
        if self.stage == 1:
            self.held = [(arrays[0], self.net.swap(arrays[0], 4))]
            return
        self.held = [(array, self.net.swap(array, UPPER[side][self.stage - 2])) for side, array in enumerate(arrays)]
        if self.stage == 3:
            self.pieces = []
            for side in range(2):
                own, come = self.held[side]
                blocks = self.blocks[side]
                others = [block ^ UPPER[side][1] for block in blocks]
                for here, array in ((blocks, own), (others, come)):
                    self.pieces += [(side, here, array), (side, [block ^ 1 for block in here], self.net.swap(array, 1))]

    def arrivals(self):
        return [come for _, come in self.held]


class Scatter:
    def __init__(self, net, sides):
        self.net = net
        self.stage = 0
        self.half = sides[0][0].shape[1]
        self.rows = sides[0][0].shape[0] // 8
        self.held = [(stays, net.swap(leaves, UPPER[side][0])) for side, (stays, leaves) in enumerate(sides)]

    def join(self, relay):
        rows, half = self.rows, self.half
        self.made = []
        if self.stage == 0:
            for side, (own, come) in enumerate(self.held):
                for leaving in range(2):
                    self.made.append(relay.make(4 * rows, half, BF if leaving else F32))
                    first = 4 * rows * leaving
                    relay.put(self.made[-1], 0, 0, 4 * rows, half, [(own, first, 0), (come, first, 0)])
        elif self.stage == 1:
            for leaving in range(2):
                self.made.append(relay.make(2 * rows, 2 * half, BF if leaving else F32))
                first = 2 * rows * leaving
                for side, (own, come) in enumerate(self.held):
                    relay.put(self.made[-1], 0, side * half, 2 * rows, half, [(own, first, 0), (come, first, 0)])
        elif self.stage == 2:
            own, come = self.held[0]
            for leaving in range(2):
                self.made.append(relay.make(rows, 2 * half, BF if leaving else F32))
                first = rows * leaving
                relay.put(self.made[-1], 0, 0, rows, 2 * half, [(own, first, 0), (come, first, 0)])

    def follow(self, made):
        arrays = [made[place] for place in self.made]
        self.stage += 1
        if self.stage == 1:
            self.held = [(arrays[2 * side], self.net.swap(arrays[2 * side + 1], UPPER[side][1])) for side in range(2)]
        elif self.stage == 2:
            self.held = [(arrays[0], self.net.swap(arrays[1], 4))]
        else:
            self.result = self.net.narrow(arrays[0] + self.net.swap(arrays[1], 2).astype(F32))


class Sum:
    def __init__(self, net, value):
        self.net, self.value, self.stage = net, value, 0
        self.send()

    def send(self):
        self.come = self.net.permute(self.value, 1 << self.stage)

    def join(self, relay):
        self.made = relay.make(*self.value.shape, self.value.dtype)
        relay.put(self.made, 0, 0, *self.value.shape, [(self.value, 0, 0), (self.come, 0, 0)])

    def follow(self, made):
        self.value = made[self.made]
        self.stage += 1
        self.send()

    def finish(self):
        for place in range(self.stage + 1, self.net.count.bit_length()):
            self.value = self.value + self.come
            if place < self.net.count.bit_length() - 1:
                self.come = self.net.permute(self.value, 1 << place)
        return self.value


def advance(moving, after=(), name="relay", extra=None):
    relay = Relay()
    if extra is not None:
        extra(relay)
    for each in moving:
        each.join(relay)
    made = relay.run(after, name)
    for each in moving:
        each.follow(made)
    return made


def fetch(me, pieces, refs, columns, target, sem):
    first, last = columns
    for (side, blocks, width, rows), ref in zip(pieces, refs):
        begin, end = max(first, side * width), min(last, (side + 1) * width)
        if begin >= end:
            continue
        for place, block in enumerate(blocks):
            row = pl.multiple_of((me ^ block) * rows, rows)
            pltpu.make_async_copy(
                ref.at[pl.ds(place * rows, rows), pl.ds(begin - side * width, end - begin)],
                target.at[pl.ds(row, rows), pl.ds(begin - first, end - begin)],
                sem,
            ).start()


def arrive(target, sem):
    pltpu.make_async_copy(target, target, sem).wait()


def describe(pieces):
    return [(side, tuple(blocks), array.shape[1], array.shape[0] // len(blocks)) for side, blocks, array in pieces]


def normed(inputs):
    average = jnp.mean(inputs, axis=-1, keepdims=True)
    centred = inputs - average
    scale = lax.rsqrt(jnp.mean(centred * centred, axis=-1, keepdims=True) + EPSILON)
    return centred * scale, scale


def norm_back(inputs, gain, upstream):
    unit, scale = normed(inputs)
    scaled = gain * upstream
    back = scale * (
        scaled
        - jnp.mean(scaled, axis=-1, keepdims=True)
        - unit * jnp.mean(scaled * unit, axis=-1, keepdims=True)
    )
    return back, jnp.sum(upstream * unit, axis=0, keepdims=True), jnp.sum(upstream, axis=0, keepdims=True)


def partner(values):
    half = HEAD // 2
    lane = lax.broadcasted_iota(jnp.int32, values.shape, 1)
    return jnp.where(
        lane % HEAD < half,
        pltpu.roll(values, values.shape[1] - half, 1),
        pltpu.roll(values, half, 1),
    )


def wide(table, width):
    return jnp.concatenate([table] * (width // LANES), 1)


def turn_out(me, values, kept, sent):
    turned = values.T
    rows = D // BLOCKS
    for number in range(BLOCKS):
        place = (number ^ me) >> 1
        block = turned[number * rows : (number + 1) * rows, :]
        own = ((number ^ me) & 1) == 0
        begin = pl.multiple_of(place * rows, rows)

        @pl.when(own)
        def _():
            kept[pl.ds(begin, rows), :] = block

        @pl.when(jnp.logical_not(own))
        def _():
            sent[pl.ds(begin, rows), :] = block


LINES = (3, 1, 1, 1, 1, 1, 1, 1)
LENGTHS = (96, 32, 128, 32, 32, 32, 32, 32)
QKV_B, OUT_B, UP_B, DOWN_B, GAIN_ONE, SHIFT_ONE, GAIN_TWO, SHIFT_TWO = 0, 3, 4, 8, 9, 10, 11, 12
TABLE = 16


def lines_of(me, small):
    flat = jnp.zeros((BLOCKS * LANES,), BF)
    line = 0
    for values, lines, length in zip(small, LINES, LENGTHS):
        place = line * LANES + (0 if length == LANES else (me % 4) * length)
        flat = lax.dynamic_update_slice(flat, values, (place,))
        line += lines
    return flat.reshape(BLOCKS, LANES)


def table_of(lines, table):
    row = line = 0
    values = lines.astype(F32)
    table[...] = jnp.zeros_like(table)
    for count, length in zip(LINES, LENGTHS):
        spans = []
        for group in range(BLOCKS // 4):
            blocks = [(4 * group + member) * BLOCKS + line for member in range(4)]
            if length == LANES:
                spans += [values[block : block + 1, :] for block in blocks]
            else:
                for part in range(count):
                    spans.append(sum((values[block + part : block + part + 1, :] for block in blocks[1:]), values[blocks[0] + part : blocks[0] + part + 1, :]))
        for begin in range(0, len(spans), D // LANES):
            table[row : row + 1, :] = jnp.concatenate(spans[begin : begin + D // LANES], 1)
            row += 1
        line += count


def project_kernel(layout_of, me_ref, tokens, cosine, sine, *rest):
    refs = rest[: len(layout_of)]
    normed_kept, normed_sent, qkv_out, table, weight, lines, normed_out, sem, lines_sem = rest[len(layout_of) :]
    step = pl.program_id(0)

    @pl.when(step == 0)
    def _():
        fetch(me_ref[0], layout_of, refs, (3 * D, 3 * D + LANES), lines, lines_sem)
        fetch(me_ref[0], layout_of, refs, (0, 3 * D), weight, sem)
        arrive(lines, lines_sem)
        table_of(lines[...], table)
        gain, shift = table[GAIN_ONE : GAIN_ONE + 1, :], table[SHIFT_ONE : SHIFT_ONE + 1, :]
        for begin in range(0, tokens.shape[0], ROWS):
            part = slice(begin, begin + ROWS)
            unit, _ = normed(tokens[part, :].astype(F32))
            normed_out[part, :] = (unit * gain + shift).astype(BF)
        turn_out(me_ref[0], normed_out[...], normed_kept, normed_sent)
        arrive(weight, sem)

    column = pl.multiple_of(step * TILE, TILE)
    heads_tiles = D // TILE
    bias = table[pl.ds(QKV_B + step // heads_tiles, 1), pl.ds(pl.multiple_of(step % heads_tiles * TILE, TILE), TILE)]

    @pl.when(step < 2 * heads_tiles)
    def _():
        scale = jnp.where(step < heads_tiles, HEAD**-0.5, 1.0).astype(F32)
        for begin in range(0, tokens.shape[0], ROWS):
            part = slice(begin, begin + ROWS)
            product = nn(normed_out[part, :], weight[:, pl.ds(column, TILE)]) + bias
            turned = product * wide(cosine[part, :], TILE) + partner(product) * wide(sine[part, :], TILE)
            qkv_out[part, :] = (turned * scale).astype(BF)

    @pl.when(step >= 2 * heads_tiles)
    def _():
        product = nn(normed_out[...], weight[:, pl.ds(column, TILE)]) + bias
        qkv_out[...] = product.astype(BF)


def project(me, tokens, cosine, sine, pieces, after=()):
    count = tokens.shape[0]
    layout_of = describe(pieces)
    return pallas(
        functools.partial(project_kernel, layout_of),
        grid=(3 * D // TILE,),
        in_specs=[SMEM, fixed(count, D), fixed(count, LANES), fixed(count, LANES)] + [ANY] * len(pieces),
        out_specs=[fixed(D // 2, count)] * 2 + [pl.BlockSpec((count, TILE), lambda step: (0, step)), fixed(TABLE, D)],
        out_shape=[jax.ShapeDtypeStruct((D // 2, count), BF)] * 2
        + [jax.ShapeDtypeStruct((count, 3 * D), BF), jax.ShapeDtypeStruct((TABLE, D), F32)],
        scratch_shapes=[
            pltpu.VMEM((D, 3 * D), BF),
            pltpu.VMEM((D, LANES), BF),
            pltpu.VMEM((count, D), BF),
            pltpu.SemaphoreType.DMA,
            pltpu.SemaphoreType.DMA,
        ],
        cost_estimate=cost(16),
        name="project",
        operands=(me, tokens, cosine, sine, *[array for _, _, array in pieces]),
        after=after,
    )


def line_of(table, line):
    return table[line : line + 1, :]


def branch_kernel(layout_of, me_ref, mixed, tokens, table, *rest):
    refs = rest[: len(layout_of)]
    resid, normed_two, normed_kept, normed_sent, mixed_kept, mixed_sent, weight, sem = rest[len(layout_of) :]

    @pl.when(pl.program_id(0) == 0)
    def _():
        fetch(me_ref[0], layout_of, refs, (0, D), weight, sem)
        arrive(weight, sem)

    value = tokens[...].astype(F32) + (nn(mixed[...], weight[...]) + line_of(table, OUT_B))
    resid[...] = value
    unit, _ = normed(value)
    low = (unit * line_of(table, GAIN_TWO) + line_of(table, SHIFT_TWO)).astype(BF)
    normed_two[...] = low
    turn_out(me_ref[0], low, normed_kept, normed_sent)
    turn_out(me_ref[0], mixed[...], mixed_kept, mixed_sent)


def branch(me, mixed, tokens, table, pieces, after=()):
    count = tokens.shape[0]
    layout_of = describe(pieces)
    rows = pl.BlockSpec((ROWS, D), lambda step: (step, 0))
    return pallas(
        functools.partial(branch_kernel, layout_of),
        grid=(count // ROWS,),
        in_specs=[SMEM, rows, rows, fixed(TABLE, D)] + [ANY] * len(pieces),
        out_specs=[rows, rows] + [pl.BlockSpec((D // 2, ROWS), lambda step: (0, step))] * 4,
        out_shape=[jax.ShapeDtypeStruct((count, D), F32), jax.ShapeDtypeStruct((count, D), BF)]
        + [jax.ShapeDtypeStruct((D // 2, count), BF)] * 4,
        scratch_shapes=[pltpu.VMEM((D, D), BF), pltpu.SemaphoreType.DMA],
        cost_estimate=cost(12),
        name="branch",
            operands=(me, mixed, tokens, table, *[array for _, _, array in pieces],),
        after=after,
    )


def gelu_parts(value):
    decay = jnp.exp(-0.5 * value * value)
    point = 1.0 / (1.0 + (0.3275911 * 2.0**-0.5) * jnp.abs(value))
    series = 0.5 * 1.061405429
    for factor in (-1.453152027, 1.421413741, -0.284496736, 0.254829592):
        series = series * point + 0.5 * factor
    tail = series * point * decay
    return jnp.where(value >= 0, 1.0 - tail, tail), decay * (2.0 * np.pi) ** -0.5


def up_kernel(layout_of, me_ref, normed_two, table, *rest):
    refs = rest[: len(layout_of)]
    activ, slope, activ_kept, activ_sent, weight, sem = rest[len(layout_of) :]
    step = pl.program_id(0)

    @pl.when(step == 0)
    def _():
        fetch(me_ref[0], layout_of, refs, (D, D + FF), weight, sem)
        arrive(weight, sem)

    column = pl.multiple_of(step * TILE, TILE)
    tiles = D // TILE
    bias = table[pl.ds(UP_B + step // tiles, 1), pl.ds(pl.multiple_of(step % tiles * TILE, TILE), TILE)]
    for begin in range(0, normed_two.shape[0], ROWS):
        part = slice(begin, begin + ROWS)
        value = nn(normed_two[part, :], weight[:, pl.ds(column, TILE)]) + bias
        share, density = gelu_parts(value)
        activ[part, :] = (value * share).astype(BF)
        slope[part, :] = (share + value * density).astype(BF)
        turned = activ[part, :].T
        rows = FF // BLOCKS
        parity = me_ref[0] & 1
        for block in range(TILE // rows):
            here = slice(block // 2 * rows, (block // 2 + 1) * rows)

            @pl.when(parity == block % 2)
            def _():
                activ_kept[here, part] = turned[block * rows : (block + 1) * rows, :]

            @pl.when(parity != block % 2)
            def _():
                activ_sent[here, part] = turned[block * rows : (block + 1) * rows, :]


def up(me, normed_two, table, pieces, after=()):
    count = normed_two.shape[0]
    layout_of = describe(pieces)
    tile = pl.BlockSpec((count, TILE), lambda step: (0, step))
    return pallas(
        functools.partial(up_kernel, layout_of),
        grid=(FF // TILE,),
        in_specs=[SMEM, fixed(count, D), fixed(TABLE, D)] + [ANY] * len(pieces),
        out_specs=[tile, tile] + [pl.BlockSpec((TILE // 2, count), lambda step: (step, 0))] * 2,
        out_shape=[jax.ShapeDtypeStruct((count, FF), BF)] * 2 + [jax.ShapeDtypeStruct((FF // 2, count), BF)] * 2,
        scratch_shapes=[pltpu.VMEM((D, FF), BF), pltpu.SemaphoreType.DMA],
        cost_estimate=cost(35),
        name="up",
            operands=(me, normed_two, table, *[array for _, _, array in pieces],),
        after=after,
    )


def down_kernel(layout_of, me_ref, activ, slope, cotangent, resid, table, *rest):
    refs = rest[: len(layout_of)]
    output, grad_pre, grad_bias, weight, total, sem = rest[len(layout_of) :]
    step = pl.program_id(0)

    @pl.when(step == 0)
    def _():
        fetch(me_ref[0], layout_of, refs, (0, D), weight, sem)
        total[...] = resid[...] + line_of(table, DOWN_B)
        arrive(weight, sem)

    rows = weight[pl.ds(pl.multiple_of(step * TILE, TILE), TILE), :]
    sums = jnp.zeros((1, TILE), F32)
    for begin in range(0, activ.shape[0], ROWS):
        part = slice(begin, begin + ROWS)
        total[part, :] += nn(activ[part, :], rows)
        back = (nt(cotangent[part, :], rows) * slope[part, :].astype(F32)).astype(BF)
        grad_pre[part, :] = back
        sums += jnp.sum(back.astype(F32), axis=0, keepdims=True)
    grad_bias[...] = sums

    @pl.when(step == pl.num_programs(0) - 1)
    def _():
        output[...] = total[...].astype(BF)


def down(me, activ, slope, cotangent, resid, table, pieces, after=()):
    count = activ.shape[0]
    layout_of = describe(pieces)
    tile = pl.BlockSpec((count, TILE), lambda step: (0, step))
    return pallas(
        functools.partial(down_kernel, layout_of),
        grid=(FF // TILE,),
        in_specs=[SMEM, tile, tile, fixed(count, D), fixed(count, D), fixed(TABLE, D)] + [ANY] * len(pieces),
        out_specs=[fixed(count, D), tile, pl.BlockSpec((1, TILE), lambda step: (0, step))],
        out_shape=[
            jax.ShapeDtypeStruct((count, D), BF),
            jax.ShapeDtypeStruct((count, FF), BF),
            jax.ShapeDtypeStruct((1, FF), F32),
        ],
        scratch_shapes=[pltpu.VMEM((FF, D), BF), pltpu.VMEM((count, D), F32), pltpu.SemaphoreType.DMA],
        cost_estimate=cost(29),
        name="down",
            operands=(me, activ, slope, cotangent, resid, table, *[array for _, _, array in pieces],),
        after=after,
    )


def outer_rows_kernel(me_ref, left, left_other, right, right_other, *rest):
    sides, grad_bias = rest[:4], rest[4]
    step = pl.program_id(0)
    rows = FF // BLOCKS
    half = right.shape[1] // 2

    def group(ref):
        places = [(4 * step + z) ^ (me_ref[0] >> 1) for z in range(4)]
        return jnp.concatenate([ref[pl.ds(pl.multiple_of(place * rows, rows), rows), :] for place in places], 0)

    product = nn(group(left), right[...]) + nn(group(left_other), right_other[...])
    for side in range(2):
        bit = (step >> (1 - side)) & 1
        values = product[:, side * half : (side + 1) * half]

        @pl.when(bit == 0)
        def _():
            sides[2 * side][...] = values

        @pl.when(bit == 1)
        def _():
            sides[2 * side + 1][...] = values.astype(BF)

    @pl.when(step == 0)
    def _():
        grad_bias[...] = jnp.sum(right[...].astype(F32), axis=0, keepdims=True)


def outer_rows(me, left, left_other, right, right_other, after=()):
    size, count = left.shape
    width = right.shape[1]
    block = (4 * FF // BLOCKS, width // 2)
    return pallas(
        outer_rows_kernel,
        grid=(4,),
        in_specs=[SMEM] + [fixed(size, count)] * 2 + [fixed(count, width)] * 2,
        out_specs=[
            pl.BlockSpec(block, lambda step: (jnp.minimum(step, 1), 0)),
            pl.BlockSpec(block, lambda step: (jnp.maximum(step - 2, 0), 0)),
            pl.BlockSpec(block, lambda step: (step // 2, 0)),
            pl.BlockSpec(block, lambda step: (step // 2, 0)),
            fixed(1, width),
        ],
        out_shape=[jax.ShapeDtypeStruct((size // 2, width // 2), kind) for kind in (F32, BF, F32, BF)]
        + [jax.ShapeDtypeStruct((1, width), F32)],
        cost_estimate=cost(17),
        name="outer_rows",
        operands=(me, left, left_other, right, right_other),
        after=after,
    )


def outer_kernel(tiles, parts, *refs):
    sides = refs[4 * len(parts) : 4 * len(parts) + 4]
    grad_bias = refs[4 * len(parts) + 4]
    step = pl.program_id(0)
    for number, (begin, end) in enumerate(parts):
        left, left_other, right, right_other = refs[4 * number : 4 * number + 4]
        rows = left.shape[0] // (BLOCKS // 2)

        @pl.when((step >= begin) & (step < end))
        def _():
            product = nn(left[...], right[...]) + nn(left_other[...], right_other[...])
            for side in range(2):

                @pl.when((step >= tiles // 2) == bool(side))
                def _():
                    for which, positions in enumerate(parted(list(range(BLOCKS // 2)), UPPER[side][0] >> 1)):
                        target = sides[2 * side + which]
                        for position, first, length in runs_of(positions):
                            part = product[first * rows : (first + length) * rows, :]
                            target[position * rows : (position + length) * rows, :] = part.astype(target.dtype)

            grad_bias[...] = jnp.sum(right[...].astype(F32), axis=0, keepdims=True)


def outer(sets, tile_width, after=()):
    size, count = sets[0][0].shape
    parts, tiles, in_specs = [], 0, []
    for _, _, right, _ in sets:
        begin, end = tiles, tiles + right.shape[1] // tile_width
        parts.append((begin, end))
        tiles = end

        def place(step, begin=begin, end=end):
            return 0, jnp.clip(step - begin, 0, end - begin - 1)

        in_specs += [fixed(size, count)] * 2 + [pl.BlockSpec((count, tile_width), place)] * 2
    width = tiles * tile_width
    block = (size // 2, tile_width)
    firsts = pl.BlockSpec(block, lambda step: (0, jnp.minimum(step, tiles // 2 - 1)))
    seconds = pl.BlockSpec(block, lambda step: (0, jnp.maximum(step - tiles // 2, 0)))
    return pallas(
        functools.partial(outer_kernel, tiles, parts),
        grid=(tiles,),
        in_specs=in_specs,
        out_specs=[firsts, firsts, seconds, seconds, pl.BlockSpec((1, tile_width), lambda step: (0, step))],
        out_shape=[jax.ShapeDtypeStruct((size // 2, width // 2), kind) for kind in (F32, BF, F32, BF)]
        + [jax.ShapeDtypeStruct((1, width), F32)],
        cost_estimate=cost(4 * count * size * width / 0.55e9),
        name="outer",
        operands=tuple(array for each in sets for array in each),
        after=after,
    )


def branch_back_kernel(layout_of, me_ref, grad_pre, resid, cotangent, table, *rest):
    refs = rest[: len(layout_of)]
    grad_resid, grad_branch, grad_mixed, grad_gain, grad_shift, grad_bias, up_weight, out_weight, up_sem, out_sem = rest[
        len(layout_of) :
    ]

    @pl.when(pl.program_id(0) == 0)
    def _():
        fetch(me_ref[0], layout_of, refs, (D, D + FF), up_weight, up_sem)
        fetch(me_ref[0], layout_of, refs, (0, D), out_weight, out_sem)
        grad_gain[...] = jnp.zeros_like(grad_gain)
        grad_shift[...] = jnp.zeros_like(grad_shift)
        grad_bias[...] = jnp.zeros_like(grad_bias)
        arrive(up_weight, up_sem)
        arrive(out_weight, out_sem)

    upstream = nt(grad_pre[...], up_weight[...])
    back, gain_part, shift_part = norm_back(resid[...], line_of(table, GAIN_TWO), upstream)
    total = cotangent[...].astype(F32) + back
    low = total.astype(BF)
    grad_resid[...] = total
    grad_branch[...] = low
    grad_gain[...] += gain_part
    grad_shift[...] += shift_part
    grad_bias[...] += jnp.sum(low.astype(F32), axis=0, keepdims=True)
    grad_mixed[...] = nt(low, out_weight[...]).astype(BF)


def branch_back(me, grad_pre, resid, cotangent, table, pieces, after=()):
    count = resid.shape[0]
    layout_of = describe(pieces)
    rows = pl.BlockSpec((ROWS, D), lambda step: (step, 0))
    vector = jax.ShapeDtypeStruct((1, D), F32)
    return pallas(
        functools.partial(branch_back_kernel, layout_of),
        grid=(count // ROWS,),
        in_specs=[SMEM, pl.BlockSpec((ROWS, FF), lambda step: (step, 0)), rows, rows, fixed(TABLE, D)]
        + [ANY] * len(pieces),
        out_specs=[rows, rows, rows] + [fixed(1, D)] * 3,
        out_shape=[
            jax.ShapeDtypeStruct((count, D), F32),
            jax.ShapeDtypeStruct((count, D), BF),
            jax.ShapeDtypeStruct((count, D), BF),
            vector,
            vector,
            vector,
        ],
        scratch_shapes=[
            pltpu.VMEM((D, FF), BF),
            pltpu.VMEM((D, D), BF),
            pltpu.SemaphoreType.DMA,
            pltpu.SemaphoreType.DMA,
        ],
        cost_estimate=cost(21),
        name="branch_back",
            operands=(me, grad_pre, resid, cotangent, table, *[array for _, _, array in pieces],),
        after=after,
    )


def tokens_back_kernel(layout_of, chunks, me_ref, *rest):
    grads, rest = rest[:chunks], rest[chunks:]
    tokens, grad_resid, table = rest[:3]
    refs = rest[3 : 3 + len(layout_of)]
    grad_tokens, grad_gain, grad_shift, weight, sem = rest[3 + len(layout_of) :]

    @pl.when(pl.program_id(0) == 0)
    def _():
        fetch(me_ref[0], layout_of, refs, (0, 3 * D), weight, sem)
        grad_gain[...] = jnp.zeros_like(grad_gain)
        grad_shift[...] = jnp.zeros_like(grad_shift)
        arrive(weight, sem)

    quads = [
        (ref, begin) for ref in grads for begin in range(0, ref.shape[1], 3 * QUAD)
    ]
    ordered = jnp.concatenate(
        [ref[:, begin + part * QUAD : begin + (part + 1) * QUAD] for part in range(3) for ref, begin in quads], 1
    )
    back, gain_part, shift_part = norm_back(
        tokens[...].astype(F32), line_of(table, GAIN_ONE), nt(ordered, weight[...])
    )
    grad_tokens[...] = (grad_resid[...] + back).astype(BF)
    grad_gain[...] += gain_part
    grad_shift[...] += shift_part


def tokens_back(me, grads, tokens, grad_resid, table, pieces, after=()):
    count = tokens.shape[0]
    layout_of = describe(pieces)
    rows = pl.BlockSpec((ROWS, D), lambda step: (step, 0))
    vector = jax.ShapeDtypeStruct((1, D), F32)
    return pallas(
        functools.partial(tokens_back_kernel, layout_of, len(grads)),
        grid=(count // ROWS,),
        in_specs=[SMEM]
        + [pl.BlockSpec((ROWS, part.shape[1]), lambda step: (step, 0)) for part in grads]
        + [rows, rows, fixed(TABLE, D)]
        + [ANY] * len(pieces),
        out_specs=[rows, fixed(1, D), fixed(1, D)],
        out_shape=[jax.ShapeDtypeStruct((count, D), BF), vector, vector],
        scratch_shapes=[pltpu.VMEM((D, 3 * D), BF), pltpu.SemaphoreType.DMA],
        cost_estimate=cost(15),
        name="tokens_back",
            operands=(me, *grads, tokens, grad_resid, table, *[array for _, _, array in pieces],),
        after=after,
    )


def key_runs(positions, frames, patches):
    first, last = positions, positions + 1
    start = jnp.int32(0)
    for slot in range(frames.shape[1]):
        width = patches[0, slot] + 2
        size = frames[0, slot] * width
        offset = positions - start
        inside = (offset >= 0) & (offset < size)
        end = start + width + jnp.where(offset >= width, width, 0) + jnp.where(offset >= 2 * width, width, 0)
        first = jnp.where(inside, start, first)
        last = jnp.where(inside, end, last)
        start = start + size
    return first, last


def fill_mask(frames, patches, mask, runs):
    count = mask.shape[0]
    first, last = key_runs(lax.broadcasted_iota(jnp.int32, (1, count), 1), frames, patches)
    keys = lax.broadcasted_iota(jnp.int32, (count, count), 0)
    mask[...] = jnp.where((keys >= first) & (keys < last), 0.0, MASKED)
    for block in range(count // BQ):
        part = slice(block * BQ, (block + 1) * BQ)
        begin = jnp.min(first[:, part]) // BK
        runs[0, block] = begin
        runs[1, block] = (jnp.max(last[:, part]) + (BK - 1)) // BK - begin


def each_block(count, runs, work):
    blocks = count // BQ

    @pl.loop(0, 2 * blocks)
    def _(index):
        block = lax.rem(index, blocks)
        pair = index // blocks
        for size in range(1, count // BK + 1):

            @pl.when(runs[1, block] == size)
            def _():
                work(
                    pair,
                    pl.multiple_of(block * BQ, BQ),
                    pl.multiple_of(runs[0, block] * BK, BK),
                    size * BK,
                )


def one_head(pair_values, head):
    lane = lax.broadcasted_iota(jnp.int32, pair_values.shape, 1)
    return jnp.where(lane // HEAD == head, pair_values, jnp.zeros_like(pair_values))


def attend_kernel(frames, patches, queries, keys, values, *rest):
    mixed, log_totals, mask, turned, runs = rest[-5:]
    count = queries.shape[0]

    @pl.when(pl.program_id(0) == 0)
    def _():
        fill_mask(frames, patches, mask, runs)

    turned[...] = values[...].T

    def work(pair, row, key, size):
        lanes = pl.ds(pl.multiple_of(pair * LANES, LANES), LANES)
        rows = queries[pl.ds(row, BQ), lanes]
        these = keys[pl.ds(key, size), lanes]
        bias = mask[pl.ds(key, size), pl.ds(row, BQ)]
        scores = [nt(these, one_head(rows, head)) + bias for head in range(2)]
        results = []
        for head in range(2):
            highest = jnp.max(scores[head], axis=0, keepdims=True)
            expo = jnp.exp(scores[head] - highest)
            totals = jnp.sum(expo, axis=0, keepdims=True)
            place = pl.multiple_of(pair * LANES + head * HEAD, HEAD)
            result = nn(turned[pl.ds(place, HEAD), pl.ds(key, size)], expo.astype(BF))
            results.append(result * (1.0 / totals))
            log_totals[pl.ds(2 * pair + head, 1), pl.ds(row, BQ)] = highest + jnp.log(totals)
        mixed[pl.ds(row, BQ), lanes] = jnp.concatenate(results, 0).T.astype(BF)

    each_block(count, runs, work)


QUAD = 4 * HEAD
QUADS = HEADS // 4


def attend(frames, patches, qkv, begin, quads, before=(), after=()):
    count = qkv.shape[0]

    def columns(part):
        return pl.BlockSpec((count, QUAD), lambda step: (0, part * QUADS + begin + step))

    return pallas(
        attend_kernel,
        grid=(quads,),
        in_specs=[SMEM, SMEM, columns(0), columns(1), columns(2)] + [ANY] * len(before),
        out_specs=[columns(0), pl.BlockSpec((None, 4, count), lambda step: (begin + step, 0, 0))],
        out_shape=[jax.ShapeDtypeStruct((count, D), BF), jax.ShapeDtypeStruct((QUADS, 4, count), F32)],
        scratch_shapes=[
            pltpu.VMEM((count, count), F32),
            pltpu.VMEM((QUAD, count), BF),
            pltpu.SMEM((2, count // BQ), jnp.int32),
        ],
        input_output_aliases={5 + place: place for place in range(len(before))},
        cost_estimate=cost(9 * quads),
        name="attend",
            operands=(frames, patches, qkv, qkv, qkv, *before,),
        after=after,
    )


def attend_back_kernel(
    frames,
    patches,
    queries,
    keys,
    values,
    mixed,
    grads,
    log_totals,
    cosine,
    sine,
    grad_projected,
    mask,
    turned,
    grad_keys,
    grad_values,
    inner,
    runs,
):
    count = queries.shape[0]

    @pl.when(pl.program_id(0) == 0)
    def _():
        fill_mask(frames, patches, mask, runs)

    turned[...] = keys[...].T
    grad_keys[...] = jnp.zeros_like(grad_keys)
    grad_values[...] = jnp.zeros_like(grad_values)
    product = mixed[...].astype(F32) * grads[...].astype(F32)
    own = (
        lax.broadcasted_iota(jnp.int32, (8, QUAD), 1) // HEAD == lax.broadcasted_iota(jnp.int32, (8, QUAD), 0)
    ).astype(F32)
    inner[...] = lax.dot_general(
        own, product, (((1,), (1,)), ((), ())), precision=lax.Precision.HIGHEST, preferred_element_type=F32
    )

    def work(pair, row, key, size):
        lanes = pl.ds(pl.multiple_of(pair * LANES, LANES), LANES)
        block = pl.ds(row, BQ)
        span = pl.ds(key, size)
        bias = mask[span, block]
        these, those = keys[span, lanes], values[span, lanes]
        rows = [one_head(queries[block, lanes], head) for head in range(2)]
        rows_grads = [one_head(grads[block, lanes], head) for head in range(2)]
        probs, grad_scores, grad_rows = [], [], []
        for head in range(2):
            here = pl.ds(2 * pair + head, 1)
            share = jnp.exp(nt(these, rows[head]) + bias - log_totals[here, block])
            change = (share * (nt(those, rows_grads[head]) - inner[here, block])).astype(BF)
            place = pl.multiple_of(pair * LANES + head * HEAD, HEAD)
            grad_rows.append(nn(turned[pl.ds(place, HEAD), span], change))
            probs.append(share.astype(BF))
            grad_scores.append(change)
        grad_values[span, lanes] += nn(jnp.concatenate(probs, 1), jnp.concatenate(rows_grads, 0))
        grad_keys[span, lanes] += nn(jnp.concatenate(grad_scores, 1), jnp.concatenate(rows, 0))
        turned_back = jnp.concatenate(grad_rows, 0).T * HEAD**-0.5
        turned_back = turned_back * cosine[block, :] - partner(turned_back) * sine[block, :]
        grad_projected[block, lanes] = turned_back.astype(BF)

    each_block(count, runs, work)
    back = grad_keys[...] * wide(cosine[...], QUAD) - partner(grad_keys[...]) * wide(sine[...], QUAD)
    grad_projected[:, QUAD : 2 * QUAD] = back.astype(BF)
    grad_projected[:, 2 * QUAD :] = grad_values[...].astype(BF)


def attend_back(frames, patches, qkv, mixed, grads, log_totals, cosine, sine, begin, quads, after=()):
    count = qkv.shape[0]

    def columns(part):
        return pl.BlockSpec((count, QUAD), lambda step: (0, part * QUADS + begin + step))

    return pallas(
        attend_back_kernel,
        grid=(quads,),
        in_specs=[
            SMEM,
            SMEM,
            columns(0),
            columns(1),
            columns(2),
            columns(0),
            columns(0),
            pl.BlockSpec((None, 4, count), lambda step: (begin + step, 0, 0)),
            fixed(count, LANES),
            fixed(count, LANES),
        ],
        out_specs=pl.BlockSpec((count, 3 * QUAD), lambda step: (0, step)),
        out_shape=jax.ShapeDtypeStruct((count, 3 * QUAD * quads), BF),
        scratch_shapes=[
            pltpu.VMEM((count, count), F32),
            pltpu.VMEM((QUAD, count), BF),
            pltpu.VMEM((count, QUAD), F32),
            pltpu.VMEM((count, QUAD), F32),
            pltpu.VMEM((8, count), F32),
            pltpu.SMEM((2, count // BQ), jnp.int32),
        ],
        cost_estimate=cost(15 * quads),
        name="attend_back",
            operands=(frames, patches, qkv, qkv, qkv, mixed, grads, log_totals, cosine, sine,),
        after=after,
    )


def positions_of(frames, patches):
    frame_tokens = patches + 2
    clip_tokens = frames * frame_tokens
    clip_starts = jnp.cumsum(clip_tokens) - clip_tokens
    positions = jnp.arange(TOK_DEV, dtype=jnp.int32)
    inside = (
        (positions[None, :] >= clip_starts[:, None])
        & (positions[None, :] < (clip_starts + clip_tokens)[:, None])
    ).astype(jnp.int32)
    begins = jnp.sum(inside * clip_starts[:, None], axis=0)
    widths = jnp.maximum(jnp.sum(inside * frame_tokens[:, None], axis=0), 1)
    clip_sides = jnp.where(patches == SIDE_SMALL * SIDE_SMALL, SIDE_SMALL, SIDE_LARGE).astype(jnp.int32)
    sides_rows = jnp.maximum(jnp.sum(inside * clip_sides[:, None], axis=0), 1)
    offsets = positions - begins
    frame_index = offsets // widths
    within = offsets % widths
    patch_index = jnp.maximum(within - 2, 0)
    row_index = jnp.where(within >= 2, patch_index // sides_rows, 0)
    col_index = jnp.where(within >= 2, patch_index % sides_rows, 0)
    return frame_index, row_index, col_index


def rotary_tables(places):
    pair_count = HEAD // 2
    time_pairs = pair_count // 3
    row_pairs = (pair_count - time_pairs) // 2
    pair_ranks = np.arange(pair_count)
    group_ids = np.where(pair_ranks < time_pairs, 0, np.where(pair_ranks < time_pairs + row_pairs, 1, 2))
    group_first = np.array([0, time_pairs, time_pairs + row_pairs])[group_ids]
    group_sizes = np.array([time_pairs, row_pairs, pair_count - time_pairs - row_pairs])[group_ids]
    rate_table = 10000.0 ** (-(pair_ranks - group_first) / group_sizes)
    angles = jnp.zeros((TOK_DEV, pair_count), F32)
    for group_id, place in enumerate(places):
        table = jnp.asarray(np.where(group_ids == group_id, rate_table, 0.0), F32)
        angles = angles + place.astype(F32)[:, None] * table[None, :]
    cosine, sine = jnp.cos(angles), jnp.sin(angles)
    return jnp.concatenate([cosine] * 4, 1), jnp.concatenate([-sine, sine] * 2, 1)


def by_side(made):
    return (made[0], made[1]), (made[2], made[3])


def local(
    count,
    tokens,
    clip_frames,
    clip_patches,
    qkv_weight,
    qkv_bias,
    out_weight,
    out_bias,
    up_weight,
    up_bias,
    down_weight,
    down_bias,
    norm1_gain,
    norm1_shift,
    norm2_gain,
    norm2_shift,
    cotangent,
):
    net = Net(count)
    me_ref = net.me.reshape(1)
    small = (qkv_bias, out_bias, up_bias, down_bias, norm1_gain, norm1_shift, norm2_gain, norm2_shift)
    sizes = [item.shape[0] * count for item in small]
    ends = list(np.cumsum(sizes))
    clips = (clip_frames, clip_patches)

    shard = net.widen(qkv_weight)
    lines = lines_of(net.me, [net.widen(values) for values in small])
    first = Gather(net, jnp.concatenate([shard, lines, jnp.zeros_like(lines)], 1))
    middle_shard = net.widen(jnp.concatenate([out_weight, up_weight], 1))
    final_shard = net.widen(down_weight)
    cosine, sine = rotary_tables(positions_of(clip_frames[0], clip_patches[0]))

    def copy_of(shard):
        def put(relay):
            relay.put(relay.make(*shard.shape, BF), 0, 0, *shard.shape, [(shard, 0, 0)])

        return put

    made = advance([first], extra=copy_of(middle_shard))
    middle = Gather(net, made[0])
    made = advance([first])
    made = advance([first, middle])
    made = advance([middle], after=first.arrivals(), extra=copy_of(final_shard))
    final = Gather(net, made[0])
    normed_kept, normed_sent, qkv, table = project(me_ref, tokens, cosine, sine, first.pieces, after=made)
    made = advance([middle, final], after=[qkv])
    attended = attend(*clips, qkv, 0, QUADS // 2, after=made)
    made = advance([final], after=[*attended, *middle.arrivals()])
    normed_other = net.swap(normed_sent, 1)
    mixed, log_totals = attend(*clips, qkv, QUADS // 2, QUADS // 2, attended, after=made)
    made = advance([final], after=[mixed])
    resid, normed_two, two_kept, two_sent, mixed_kept, mixed_sent = branch(
        me_ref, mixed, tokens, table, middle.pieces, after=made
    )
    two_other, mixed_other = net.swap(two_sent, 1), net.swap(mixed_sent, 1)
    cotangent_other = net.swap(cotangent, 1)
    activ, slope, activ_kept, activ_sent = up(
        me_ref, normed_two, table, middle.pieces, after=[*final.arrivals(), normed_other]
    )
    activ_other = net.swap(activ_sent, 1)
    output, grad_pre, grad_up_bias = down(
        me_ref,
        activ,
        slope,
        cotangent,
        resid,
        table,
        final.pieces,
        after=[activ_kept, two_other, mixed_other, cotangent_other],
    )
    grad_pre_other = net.swap(grad_pre, 1)
    *made, grad_down_bias = outer_rows(
        me_ref, activ_kept, activ_other, cotangent, cotangent_other, after=[grad_pre]
    )
    moving_down = Scatter(net, by_side(made))
    grad_resid, grad_branch, grad_mixed, grad_gain_two, grad_shift_two, grad_out_bias = branch_back(
        me_ref, grad_pre, resid, cotangent, table, middle.pieces, after=[*made, grad_pre_other]
    )
    grad_branch_other = net.swap(grad_branch, 1)
    made = advance([moving_down], after=[grad_branch])
    *made, _ = outer(
        [(mixed_kept, mixed_other, grad_branch, grad_branch_other), (two_kept, two_other, grad_pre, grad_pre_other)],
        TILE,
        after=made,
    )
    moving_up = Scatter(net, by_side(made))
    parts, others, grad_qkv_bias, moving_qkv = [], [], [], []

    def back(quad, after):
        parts.append(attend_back(*clips, qkv, mixed, grad_mixed, log_totals, cosine, sine, quad, 1, after=after))
        others.append(net.swap(parts[-1], 1))
        return [parts[-1]]

    def weigh(quads, after):
        sets = [(normed_kept, normed_other, parts[quad], others[quad]) for quad in quads]
        *made, bias = outer(sets, 3 * QUAD // 2, after=after)
        grad_qkv_bias.append(bias)
        moving_qkv.append(Scatter(net, by_side(made)))
        return made

    made = back(0, made)
    made = advance([moving_down], after=made)
    made = back(1, made)
    made = advance([moving_down, moving_up], after=made)
    made = weigh([0, 1], made)
    made = back(2, made)
    made = advance([moving_up, moving_qkv[0]], after=[*made, moving_down.result])
    made = back(3, made)
    made = advance([moving_up, moving_qkv[0]], after=made)
    made = weigh([2, 3], made)
    grad_tokens, grad_gain_one, grad_shift_one = tokens_back(
        me_ref, parts, tokens, grad_resid, table, first.pieces, after=made
    )

    def by_part(parts):
        whole = jnp.concatenate(parts, 1)
        return whole.reshape(-1, QUADS, 3, QUAD).transpose(0, 2, 1, 3).reshape(-1, 3 * D)

    grads = [by_part(grad_qkv_bias), grad_out_bias, grad_up_bias, grad_down_bias]
    grads += [grad_gain_one, grad_shift_one, grad_gain_two, grad_shift_two]
    total = Sum(net, jnp.pad(jnp.concatenate(grads, 1).reshape(-1, D), ((0, TABLE - 13), (0, 0))))
    made = advance([moving_qkv[1], moving_qkv[0], total], after=[grad_tokens])
    made = advance([moving_qkv[1], total], after=made[:1])
    made = advance([moving_qkv[1], total], after=made[:1])
    summed = total.finish().reshape(-1)
    own = [
        lax.dynamic_slice_in_dim(summed, end - size + net.number * (size // count), size // count)
        for size, end in zip(sizes, ends)
    ]
    out_up = moving_up.result
    return (
        output,
        grad_tokens,
        by_part([each.result for each in moving_qkv]),
        own[0],
        out_up[:, :D],
        own[1],
        out_up[:, D:],
        own[2],
        moving_down.result,
        own[3],
        own[4],
        own[5],
        own[6],
        own[7],
    )


def solution(mesh):
    count = mesh.shape["fsdp"] * mesh.shape["dp"]
    rows, vector = P(AXES, None), P(AXES)
    placed = (rows, rows, rows, rows, vector, rows, vector, rows, vector, rows, vector) + (vector,) * 4 + (rows,)
    given = (rows, rows, rows, vector, rows, vector, rows, vector, rows) + (vector,) * 5
    return jax.shard_map(
        functools.partial(local, count), mesh=mesh, in_specs=placed, out_specs=given, check_vma=False
    )
```

time: 1590 us -> 571 us (0.36)
  matrix products: 627 us -> 0 us
  local copies, waits for them, and re-layouts: 478 us -> 27.8 us
  Pallas kernels: 0 us -> 344 us
  blocking collectives: 123 us -> 0 us
  other arithmetic: 87.5 us -> 13.1 us
  loops' own time: 69 us -> 0 us
  starting transfers between devices: 0.31 us -> 64.7 us
  waiting for transfers between devices: 175 us -> 111 us
    dot_general x302 -> x0, matrix products: 627 us -> none  [the longest x96 154 us: block_scores(): jnp.einsum('qd,kd->qk', block_rows, keys_head, preferred_element_type=jnp...]
    pallas_call x0 -> x31, Pallas kernels: none -> 344 us  [pallas(): pl.pallas_call(body, in_specs=list(in_specs) + [ANY] * len(after), compil...]
    squeeze x129 -> x0, local copies, waits for them, and re-layouts: 177 us -> none  [the longest x128 172 us: attend(): return lax.map(one_head, (queries, keys_rot, values_in))]
    reduce_scatter x4 -> x0, waiting for transfers between devices: 173 us -> none  [reduce_grads(): lax.psum_scatter(grads, ('fsdp', 'dp'), scatter_dimension=0, tiled=True)]
    ppermute x0 -> x70, waiting for transfers between devices: none -> 111 us  [permute(): lax.ppermute(value, AXES, [(number, number ^ mask) for number in range(se...]
    dynamic_update_slice x160 -> x8, local copies, waits for them, and re-layouts: 91.1 us -> 6.69 us  [lines_of(): flat = lax.dynamic_update_slice(flat, values, (place,))]
    unnamed x2 -> x0, blocking collectives: 81.9 us -> none
    dynamic_slice x240 -> x3, local copies, waits for them, and re-layouts: 78.3 us -> 1.78 us  [local(): lax.dynamic_slice_in_dim(summed, end - size + net.number * (size // count...]
  transfers between devices with their start and end apart: 8 -> 70, of which waited for: 1 -> 21; matrix products, arithmetic and copies ran while one was open for 68% -> 4% of each run, Pallas kernels for 0% -> 60%
where the time goes in v1:
time: 571 us; the launch traced here: 562 us
  Pallas kernels  344 us (60%)
  waiting for transfers between devices  111 us (19%)
  starting transfers between devices  64.7 us (11%)
  local copies, waits for them, and re-layouts  27.8 us (5%)
  other arithmetic  13.1 us (2%)
    pallas_call x31, Pallas kernels, pallas(): pl.pallas_call(body, in_specs=list(in_specs) + [ANY] * len(after), compil...  344 us
    ppermute x70, waiting for transfers between devices, permute(): lax.ppermute(value, AXES, [(number, number ^ mask) for number in range(se...  111 us
    ppermute x70, starting transfers between devices, permute(): lax.ppermute(value, AXES, [(number, number ^ mask) for number in range(se...  64.7 us
    unnamed x102, local copies, waits for them, and re-layouts  15.3 us
  transfers between devices with their start and end apart: 70, of which 21 were waited for; matrix products, arithmetic and copies ran while one was open for 4% of the time, Pallas kernels for 60%

profile of v1, /device:TPU:0, one launch (start us, length us, event | category | flops | bytes accessed | tf_op | source)
XLA Modules:
  0.0 562.0 jit_solution(15740178114267800770)
XLA Ops:
  22.3 18.5 %collective-permute-done.1.refs_1_ = bf16[64,3328]{1,0:T(8,128)(2,1)S(1)} collective-permute-done((bf16[64,3328]{1,0:T(8,128)(2,1)}, bf16[64,3328]{1,0:T(8,128)(2,1)S(1)}, u32[]{:S(2)}, u32[]{:S(2)}) %collective-permute-start.1) | collective-permute-done | bytes 426016 | tf_op jit(solution)/shard_map/ppermute | solution.py:130
  47.5 7.1 %collective-permute-done.4.refs_5_ = bf16[32,5120]{1,0:T(8,128)(2,1)S(1)} collective-permute-done((bf16[32,5120]{1,0:T(8,128)(2,1)S(1)}, bf16[32,5120]{1,0:T(8,128)(2,1)S(1)}, u32[]{:S(2)}, u32[]{:S(2)}) %collective-permute-start.4) | collective-permute-done | bytes 327712 | tf_op jit(solution)/shard_map/ppermute | solution.py:130
  67.9 23.3 %collective-permute-done.11.refs_2_ = bf16[64,5120]{1,0:T(8,128)(2,1)S(1)} collective-permute-done((bf16[64,5120]{1,0:T(8,128)(2,1)}, bf16[64,5120]{1,0:T(8,128)(2,1)S(1)}, u32[]{:S(2)}, u32[]{:S(2)}) %collective-permute-start.11) | collective-permute-done | bytes 655392 | tf_op jit(solution)/shard_map/ppermute | solution.py:130
  99.9 17.6 %project.1 = (bf16[512,1024]{1,0:T(8,128)(2,1)}, bf16[512,1024]{1,0:T(8,128)(2,1)}, bf16[1024,3072]{1,0:T(8,128)(2,1)}, f32[16,1024]{1,0:T(8,128)}) custom-call(s32[1]{0:T(128)} %bitcast.refs_0_, bf16[1024,1024]{1,0:T(8,128)(2,1)} %refs_5_.1, f32[1024,128]{1,0:T(8,128)} %get-tuple-element.234.refs_2_.refs_8_, ...), custom_call_target="tpu_custom_call" | custom-call | flops 184000004096 | tf_op jit(solution)/shard_map/project/pallas_call | solution.py:58
  125.5 18.6 %attend.2 = (bf16[1024,1024]{1,0:T(8,128)(2,1)}, f32[4,4,1024]{2,1,0:T(4,128)}) custom-call(s32[1,4]{1,0:T(1,128)} %refs_0_.13, s32[1,4]{1,0:T(1,128)} %refs_1_.13, bf16[1024,3072]{1,0:T(8,128)(2,1)} %get-tuple-element.125.refs_6_.refs_2_.refs_3_.refs_4_, bf16[1024,3072]{1,0:T(8,128)(2,1)} %get-tuple-element.125.refs_6_.refs_2_.refs_3_.refs_4_, ...), custom_call_target="tpu_custom_call" | custom-call | flops 206999994368 | tf_op jit(solution)/shard_map/attend/pallas_call | solution.py:58
  156.2 18.8 %attend.3 = (bf16[1024,1024]{1,0:T(8,128)(2,1)}, f32[4,4,1024]{2,1,0:T(4,128)}) custom-call(s32[1,4]{1,0:T(1,128)} %refs_0_.13, s32[1,4]{1,0:T(1,128)} %refs_1_.13, bf16[1024,3072]{1,0:T(8,128)(2,1)} %get-tuple-element.125.refs_6_.refs_2_.refs_3_.refs_4_, ...), custom_call_target="tpu_custom_call", output_to_operand_aliasing={{0}: (5, {}), {1}: (6, {})} | custom-call | flops 206999994368 | tf_op jit(solution)/shard_map/attend/pallas_call | solution.py:58
  182.4 12.2 %branch.1 = (f32[1024,1024]{1,0:T(8,128)}, bf16[1024,1024]{1,0:T(8,128)(2,1)}, bf16[512,1024]{1,0:T(8,128)(2,1)}, bf16[512,1024]{1,0:T(8,128)(2,1)}, bf16[512,10...) custom-call(s32[1]{0:T(128)} %bitcast.refs_0_, bf16[1024,1024]{1,0:T(8,128)(2,1)} %get-tuple-element.133.refs_4_.refs_1_.refs_5_, ...), custom_call_target="tpu_custom_call" | custom-call | flops 138000007168 | tf_op jit(solution)/shard_map/branch/pallas_call | solution.py:58
  195.2 9.8 %collective-permute-done.24.refs_11_.refs_8_ = bf16[1024,512]{1,0:T(8,128)(2,1)} collective-permute-done((bf16[1024,512]{1,0:T(8,128)(2,1)}, bf16[1024,512]{1,0:T(8,128)(2,1)}, u32[]{:S(2)}, u32[]{:S(2)}) %collective-permute-start.24) | collective-permute-done | bytes 1048608 | tf_op jit(solution)/shard_map/ppermute | solution.py:130
  207.4 37.4 %up.1 = (bf16[1024,4096]{1,0:T(8,128)(2,1)}, bf16[1024,4096]{1,0:T(8,128)(2,1)}, bf16[2048,1024]{1,0:T(8,128)(2,1)}, bf16[2048,1024]{1,0:T(8,128)(2,1)}) custom-call(s32[1]{0:T(128)} %bitcast.refs_0_, bf16[1024,1024]{1,0:T(8,128)(2,1)} %get-tuple-element.137.refs_1_, f32[16,1024]{1,0:T(8,128)} %get-tuple-element.134.refs_3_.refs_2_.refs_5_.refs_4_.refs_7_, ...), custom_call_target="tpu_custom_call" | custom-call | flops 402499993600 | tf_op jit(solution)/shard_map/up/pallas_call | solution.py:58
  245.3 28.6 %down.1 = (bf16[1024,1024]{1,0:T(8,128)(2,1)}, bf16[1024,4096]{1,0:T(8,128)(2,1)}, f32[1,4096]{1,0:T(1,128)}) custom-call(s32[1]{0:T(128)} %bitcast.refs_0_, bf16[1024,4096]{1,0:T(8,128)(2,1)} %get-tuple-element.139.refs_1_, bf16[1024,4096]{1,0:T(8,128)(2,1)} %get-tuple-element.140.refs_2_, bf16[1024,1024]{1,0:T(8,128)(2,1)} %refs_3_.5, ...), custom_call_target="tpu_custom_call" | custom-call | flops 333499990016 | tf_op jit(solution)/shard_map/down/pallas_call | solution.py:58
  274.1 16.9 %outer_rows.1 = (f32[1024,512]{1,0:T(8,128)}, bf16[1024,512]{1,0:T(8,128)(2,1)}, f32[1024,512]{1,0:T(8,128)}, bf16[1024,512]{1,0:T(8,128)(2,1)}, f32[1,1024]{1,0:T(1,128)}) custom-call(s32[1]{0:T(128)} %bitcast.refs_0_, bf16[2048,1024]{1,0:T(8,128)(2,1)} %get-tuple-element.142.refs_14_.refs_1_, bf16[2048,1024]{1,0:T(8,128)(2,1)} %collective-permute-done.34.refs_2_, ...), custom_call_target="tpu_custom_call" | custom-call | flops 195499999232 | tf_op jit(solution)/shard_map/outer_rows/pallas_call | solution.py:58
  293.2 21.4 %branch_back.1 = (f32[1024,1024]{1,0:T(8,128)}, bf16[1024,1024]{1,0:T(8,128)(2,1)}, bf16[1024,1024]{1,0:T(8,128)(2,1)}, f32[1,1024]{1,0:T(1,128)}, f32[1,1024]{1,0:T(1,128)}, /*index=5*/f32[1,1024]{1,0:T(1,128)}) custom-call(s32[1]{0:T(128)} %bitcast.refs_0_, bf16[1024,4096]{1,0:T(8,128)(2,1)} %get-tuple-element.146.refs_5_.refs_1_.refs_6_, ...), custom_call_target="tpu_custom_call" | custom-call | flops 241499996160 | tf_op jit(solution)/shard_map/branch_back/pallas_call | solution.py:58
  325.8 21.3 %outer.3 = (f32[256,2560]{1,0:T(8,128)}, bf16[256,2560]{1,0:T(8,128)(2,1)}, f32[256,2560]{1,0:T(8,128)}, bf16[256,2560]{1,0:T(8,128)(2,1)}, f32[1,5120]{1,0:T(1,128)}) custom-call(bf16[512,1024]{1,0:T(8,128)(2,1)} %get-tuple-element.154.refs_0_, bf16[512,1024]{1,0:T(8,128)(2,1)} %collective-permute-done.32.refs_16_.refs_1_, ...), custom_call_target="tpu_custom_call" | custom-call | flops 224509657088 | tf_op jit(solution)/shard_map/outer/pallas_call | solution.py:58
  349.3 16.4 %attend_back.4.refs_4_.refs_2_.refs_1_ = bf16[1024,768]{1,0:T(8,128)(2,1)} custom-call(s32[1,4]{1,0:T(1,128)} %refs_0_.13, s32[1,4]{1,0:T(1,128)} %refs_1_.13, bf16[1024,3072]{1,0:T(8,128)(2,1)} %get-tuple-element.125.refs_6_.refs_2_.refs_3_.refs_4_, bf16[1024,3072]{1,0:T(8,128)(2,1)} %get-tuple-element.125.refs_6_.refs_2_.refs_3_.refs_4_, ...), custom_call_target="tpu_custom_call" | custom-call | flops 172499992576 | tf_op jit(solution)/shard_map/attend_back/pallas_call | solution.py:58
  373.2 16.6 %attend_back.5.refs_6_.refs_2_ = bf16[1024,768]{1,0:T(8,128)(2,1)} custom-call(s32[1,4]{1,0:T(1,128)} %refs_0_.13, s32[1,4]{1,0:T(1,128)} %refs_1_.13, bf16[1024,3072]{1,0:T(8,128)(2,1)} %get-tuple-element.125.refs_6_.refs_2_.refs_3_.refs_4_, bf16[1024,3072]{1,0:T(8,128)(2,1)} %get-tuple-element.125.refs_6_.refs_2_.refs_3_.refs_4_, ...), custom_call_target="tpu_custom_call" | custom-call | flops 172499992576 | tf_op jit(solution)/shard_map/attend_back/pallas_call | solution.py:58
  390.5 6.8 %collective-permute-done.43.refs_1_ = bf16[256,1024]{1,0:T(8,128)(2,1)} collective-permute-done((bf16[256,1024]{1,0:T(8,128)(2,1)}, bf16[256,1024]{1,0:T(8,128)(2,1)}, u32[]{:S(2)}, u32[]{:S(2)}) %collective-permute-start.43) | collective-permute-done | bytes 524320 | tf_op jit(solution)/shard_map/ppermute | solution.py:130
  397.3 6.5 %relay.24 = (f32[128,1024]{1,0:T(8,128)}, bf16[128,1024]{1,0:T(8,128)(2,1)}, f32[128,2560]{1,0:T(8,128)}, bf16[128,2560]{1,0:T(8,128)(2,1)}, f32[128,2560]{1,0:T(8,128)}, /*index=5*/bf16[128,2560]{1,0:T(8,128)(2,1)}) custom-call(f32[256,1024]{1,0:T(8,128)} %get-tuple-element.165.refs_10_.refs_0_, bf16[256,1024]{1,0:T(8,128)(2,1)} %collective-permute-done.43.refs_1_, ...), custom_call_target="tpu_custom_call" | custom-call | flops 54911045632 | tf_op jit(solution)/shard_map/relay/pallas_call | solution.py:58
  406.8 11.0 %outer.4 = (f32[256,768]{1,0:T(8,128)}, bf16[256,768]{1,0:T(8,128)(2,1)}, f32[256,768]{1,0:T(8,128)}, bf16[256,768]{1,0:T(8,128)(2,1)}, f32[1,1536]{1,0:T(1,128)}) custom-call(bf16[512,1024]{1,0:T(8,128)(2,1)} %get-tuple-element.167.refs_0_.refs_4_, bf16[512,1024]{1,0:T(8,128)(2,1)} %copy-done.21, bf16[1024,768]{1,0:T(8,128)(2,1)} %attend_back.4.refs_4_.refs_2_.refs_1_, ...), custom_call_target="tpu_custom_call" | custom-call | flops 67352895488 | tf_op jit(solution)/shard_map/outer/pallas_call | solution.py:58
  420.0 16.4 %attend_back.6.refs_8_.refs_2_.refs_3_ = bf16[1024,768]{1,0:T(8,128)(2,1)} custom-call(s32[1,4]{1,0:T(1,128)} %refs_0_.13, s32[1,4]{1,0:T(1,128)} %refs_1_.13, bf16[1024,3072]{1,0:T(8,128)(2,1)} %get-tuple-element.125.refs_6_.refs_2_.refs_3_.refs_4_, bf16[1024,3072]{1,0:T(8,128)(2,1)} %get-tuple-element.125.refs_6_.refs_2_.refs_3_.refs_4_, ...), custom_call_target="tpu_custom_call" | custom-call | flops 172499992576 | tf_op jit(solution)/shard_map/attend_back/pallas_call | solution.py:58
  449.0 16.4 %attend_back.7.refs_6_.refs_4_ = bf16[1024,768]{1,0:T(8,128)(2,1)} custom-call(s32[1,4]{1,0:T(1,128)} %refs_0_.13, s32[1,4]{1,0:T(1,128)} %refs_1_.13, bf16[1024,3072]{1,0:T(8,128)(2,1)} %get-tuple-element.125.refs_6_.refs_2_.refs_3_.refs_4_, bf16[1024,3072]{1,0:T(8,128)(2,1)} %get-tuple-element.125.refs_6_.refs_2_.refs_3_.refs_4_, ...), custom_call_target="tpu_custom_call" | custom-call | flops 172499992576 | tf_op jit(solution)/shard_map/attend_back/pallas_call | solution.py:58
  465.6 10.3 %collective-permute-done.53.refs_1_ = bf16[64,5120]{1,0:T(8,128)(2,1)} collective-permute-done((bf16[64,5120]{1,0:T(8,128)(2,1)}, bf16[64,5120]{1,0:T(8,128)(2,1)}, u32[]{:S(2)}, u32[]{:S(2)}) %collective-permute-start.53) | collective-permute-done | bytes 655392 | tf_op jit(solution)/shard_map/ppermute | solution.py:130
  480.1 10.9 %outer.5 = (f32[256,768]{1,0:T(8,128)}, bf16[256,768]{1,0:T(8,128)(2,1)}, f32[256,768]{1,0:T(8,128)}, bf16[256,768]{1,0:T(8,128)(2,1)}, f32[1,1536]{1,0:T(1,128)}) custom-call(bf16[512,1024]{1,0:T(8,128)(2,1)} %get-tuple-element.167.refs_0_.refs_4_, bf16[512,1024]{1,0:T(8,128)(2,1)} %copy-done.21, bf16[1024,768]{1,0:T(8,128)(2,1)} %attend_back.6.refs_8_.refs_2_.refs_3_, ...), custom_call_target="tpu_custom_call" | custom-call | flops 67352895488 | tf_op jit(solution)/shard_map/outer/pallas_call | solution.py:58
  497.1 15.0 %tokens_back.1 = (bf16[1024,1024]{1,0:T(8,128)(2,1)}, f32[1,1024]{1,0:T(1,128)}, f32[1,1024]{1,0:T(1,128)}) custom-call(s32[1]{0:T(128)} %bitcast.refs_0_, bf16[1024,768]{1,0:T(8,128)(2,1)} %attend_back.4.refs_4_.refs_2_.refs_1_, bf16[1024,768]{1,0:T(8,128)(2,1)} %attend_back.5.refs_6_.refs_2_, bf16[1024,768]{1,0:T(8,128)(2,1)} %attend_back.6.refs_8_.refs_2_.refs_3_, ...), custom_call_target="tpu_custom_call" | custom-call | flops 172499992576 | tf_op jit(solution)/shard_map/tokens_back/pallas_call | solution.py:58
  540.1 7.7 %collective-permute-done.65.refs_3_ = f32[16,1024]{1,0:T(8,128)S(1)} collective-permute-done((f32[16,1024]{1,0:T(8,128)}, f32[16,1024]{1,0:T(8,128)S(1)}, u32[]{:S(2)}, u32[]{:S(2)}) %collective-permute-start.65) | collective-permute-done | bytes 65568 | tf_op jit(solution)/shard_map/ppermute | solution.py:130
  (293 shorter events, 175.3 us)
Async XLA Ops:
  47.3 147.3 %collective-permute-start.33 = (bf16[1024,1024]{1,0:T(8,128)(2,1)}, bf16[1024,1024]{1,0:T(8,128)(2,1)}, u32[]{:S(2)}, u32[]{:S(2)}) collective-permute-start(bf16[1024,1024]{1,0:T(8,128)(2,1)} %refs_3_.5), channel_id=1, source_target_pairs={{0,1},{1,0},{2,3},{3,2},{4,5},{5,4},{6,7},{7,6},{8,9},{9,8},{10,11... | collective-permute-start | bytes 6291464 | tf_op jit(solution)/shard_map/ppermute | solution.py:130
  59.5 32.3 %collective-permute-start.6 = (bf16[256,1664]{1,0:T(8,128)(2,1)}, bf16[256,1664]{1,0:T(8,128)(2,1)S(1)}, u32[]{:S(2)}, u32[]{:S(2)}) collective-permute-start(bf16[256,1664]{1,0:T(8,128)(2,1)} %get-tuple-element.119.refs_4_.refs_8_), channel_id=1, source_target_pairs={{0,8},{1,9},{2,10},{3,11},{4,12},{5,13},{6,14},{7,15},{8,0},{9,1},... | collective-permute-start | bytes 2555912 | tf_op jit(solution)/shard_map/ppermute | solution.py:130
  61.0 30.3 %collective-permute-start.9 = (bf16[256,1664]{1,0:T(8,128)(2,1)}, bf16[256,1664]{1,0:T(8,128)(2,1)S(1)}, u32[]{:S(2)}, u32[]{:S(2)}) collective-permute-start(bf16[256,1664]{1,0:T(8,128)(2,1)} %get-tuple-element.120.refs_8_.refs_12_), channel_id=1, source_target_pairs={{0,16},{1,17},{2,18},{3,19},{4,20},{5,21},{6,22},{7,23},{8,24},{9,... | collective-permute-start | bytes 2555912 | tf_op jit(solution)/shard_map/ppermute | solution.py:130
  121.2 30.4 %collective-permute-start.16 = (bf16[256,2560]{1,0:T(8,128)(2,1)}, bf16[256,2560]{1,0:T(8,128)(2,1)}, u32[]{:S(2)}, u32[]{:S(2)}) collective-permute-start(bf16[256,2560]{1,0:T(8,128)(2,1)} %get-tuple-element.126.refs_5_.refs_4_.refs_3_), channel_id=1, source_target_pairs={{0,8},{1,9},{2,10},{3,11},{4,12},{5,13},{6,14},{7,15},{8,0},{9,1},... | collective-permute-start | bytes 3932168 | tf_op jit(solution)/shard_map/ppermute | solution.py:130
  121.7 30.2 %collective-permute-start.17 = (bf16[256,2560]{1,0:T(8,128)(2,1)}, bf16[256,2560]{1,0:T(8,128)(2,1)}, u32[]{:S(2)}, u32[]{:S(2)}) collective-permute-start(bf16[256,2560]{1,0:T(8,128)(2,1)} %get-tuple-element.127.refs_6_.refs_8_.refs_7_.refs_9_), channel_id=1, source_target_pairs={{0,16},{1,17},{2,18},{3,19},{4,20},{5,21},{6,22},{7,23},{8,24},{9,... | collective-permute-start | bytes 3932168 | tf_op jit(solution)/shard_map/ppermute | solution.py:130
  144.1 34.6 %collective-permute-start.18 = (bf16[256,2560]{1,0:T(8,128)(2,1)}, bf16[256,2560]{1,0:T(8,128)(2,1)}, u32[]{:S(2)}, u32[]{:S(2)}) collective-permute-start(bf16[256,2560]{1,0:T(8,128)(2,1)} %get-tuple-element.126.refs_5_.refs_4_.refs_3_), channel_id=1, source_target_pairs={{0,1},{1,0},{2,3},{3,2},{4,5},{5,4},{6,7},{7,6},{8,9},{9,8},{10,11... | collective-permute-start | bytes 3932168 | tf_op jit(solution)/shard_map/ppermute | solution.py:130
  148.0 30.9 %collective-permute-start.20 = (bf16[256,2560]{1,0:T(8,128)(2,1)}, bf16[256,2560]{1,0:T(8,128)(2,1)}, u32[]{:S(2)}, u32[]{:S(2)}) collective-permute-start(bf16[256,2560]{1,0:T(8,128)(2,1)} %get-tuple-element.127.refs_6_.refs_8_.refs_7_.refs_9_), channel_id=1, source_target_pairs={{0,1},{1,0},{2,3},{3,2},{4,5},{5,4},{6,7},{7,6},{8,9},{9,8},{10,11... | collective-permute-start | bytes 3932168 | tf_op jit(solution)/shard_map/ppermute | solution.py:130
  194.6 50.2 %collective-permute-start.29 = (bf16[1024,512]{1,0:T(8,128)(2,1)}, bf16[1024,512]{1,0:T(8,128)(2,1)}, u32[]{:S(2)}, u32[]{:S(2)}) collective-permute-start(bf16[1024,512]{1,0:T(8,128)(2,1)} %get-tuple-element.136.refs_13_.refs_10_), channel_id=1, source_target_pairs={{0,1},{1,0},{2,3},{3,2},{4,5},{5,4},{6,7},{7,6},{8,9},{9,8},{10,11... | collective-permute-start | bytes 3145736 | tf_op jit(solution)/shard_map/ppermute | solution.py:130
  194.8 50.5 %collective-permute-start.31 = (bf16[512,1024]{1,0:T(8,128)(2,1)}, bf16[512,1024]{1,0:T(8,128)(2,1)}, u32[]{:S(2)}, u32[]{:S(2)}) collective-permute-start(bf16[512,1024]{1,0:T(8,128)(2,1)} %get-tuple-element.143), channel_id=1, source_target_pairs={{0,1},{1,0},{2,3},{3,2},{4,5},{5,4},{6,7},{7,6},{8,9},{9,8},{10,11... | collective-permute-start | bytes 3145736 | tf_op jit(solution)/shard_map/ppermute | solution.py:130
  205.0 40.3 %collective-permute-start.32 = (bf16[512,1024]{1,0:T(8,128)(2,1)}, bf16[512,1024]{1,0:T(8,128)(2,1)}, u32[]{:S(2)}, u32[]{:S(2)}) collective-permute-start(bf16[512,1024]{1,0:T(8,128)(2,1)} %get-tuple-element.144), channel_id=1, source_target_pairs={{0,1},{1,0},{2,3},{3,2},{4,5},{5,4},{6,7},{7,6},{8,9},{9,8},{10,11... | collective-permute-start | bytes 3145736 | tf_op jit(solution)/shard_map/ppermute | solution.py:130
  206.9 38.4 %collective-permute-start.28 = (bf16[1024,512]{1,0:T(8,128)(2,1)}, bf16[1024,512]{1,0:T(8,128)(2,1)}, u32[]{:S(2)}, u32[]{:S(2)}) collective-permute-start(bf16[1024,512]{1,0:T(8,128)(2,1)} %collective-permute-done.24.refs_11_.refs_8_), channel_id=1, source_target_pairs={{0,1},{1,0},{2,3},{3,2},{4,5},{5,4},{6,7},{7,6},{8,9},{9,8},{10,11... | collective-permute-start | bytes 3145736 | tf_op jit(solution)/shard_map/ppermute | solution.py:130
  206.9 38.4 %collective-permute-start.30 = (bf16[1024,512]{1,0:T(8,128)(2,1)}, bf16[1024,512]{1,0:T(8,128)(2,1)}, u32[]{:S(2)}, u32[]{:S(2)}) collective-permute-start(bf16[1024,512]{1,0:T(8,128)(2,1)} %collective-permute-done.25.refs_12_), channel_id=1, source_target_pairs={{0,1},{1,0},{2,3},{3,2},{4,5},{5,4},{6,7},{7,6},{8,9},{9,8},{10,11... | collective-permute-start | bytes 3145736 | tf_op jit(solution)/shard_map/ppermute | solution.py:130
  244.8 29.3 %collective-permute-start.34 = (bf16[2048,1024]{1,0:T(8,128)(2,1)}, bf16[2048,1024]{1,0:T(8,128)(2,1)}, u32[]{:S(2)}, u32[]{:S(2)}) collective-permute-start(bf16[2048,1024]{1,0:T(8,128)(2,1)} %get-tuple-element.147), channel_id=1, source_target_pairs={{0,1},{1,0},{2,3},{3,2},{4,5},{5,4},{6,7},{7,6},{8,9},{9,8},{10,11... | collective-permute-start | bytes 12582920 | tf_op jit(solution)/shard_map/ppermute | solution.py:130
  322.6 43.1 %collective-permute-start.39 = (bf16[512,512]{1,0:T(8,128)(2,1)}, bf16[512,512]{1,0:T(8,128)(2,1)}, u32[]{:S(2)}, u32[]{:S(2)}) collective-permute-start(bf16[512,512]{1,0:T(8,128)(2,1)} %get-tuple-element.158.refs_9_), channel_id=1, source_target_pairs={{0,8},{1,9},{2,10},{3,11},{4,12},{5,13},{6,14},{7,15},{8,0},{9,1},... | collective-permute-start | bytes 1572872 | tf_op jit(solution)/shard_map/ppermute | solution.py:130
  323.7 42.0 %collective-permute-start.40 = (bf16[512,512]{1,0:T(8,128)(2,1)}, bf16[512,512]{1,0:T(8,128)(2,1)}, u32[]{:S(2)}, u32[]{:S(2)}) collective-permute-start(bf16[512,512]{1,0:T(8,128)(2,1)} %get-tuple-element.160.refs_11_), channel_id=1, source_target_pairs={{0,16},{1,17},{2,18},{3,19},{4,20},{5,21},{6,22},{7,23},{8,24},{9,... | collective-permute-start | bytes 1572872 | tf_op jit(solution)/shard_map/ppermute | solution.py:130
  347.0 50.3 %collective-permute-start.44 = (bf16[256,2560]{1,0:T(8,128)(2,1)}, bf16[256,2560]{1,0:T(8,128)(2,1)}, u32[]{:S(2)}, u32[]{:S(2)}) collective-permute-start(bf16[256,2560]{1,0:T(8,128)(2,1)} %get-tuple-element.162.refs_11_), channel_id=1, source_target_pairs={{0,16},{1,17},{2,18},{3,19},{4,20},{5,21},{6,22},{7,23},{8,24},{9,... | collective-permute-start | bytes 3932168 | tf_op jit(solution)/shard_map/ppermute | solution.py:130
  348.4 48.9 %collective-permute-start.45 = (bf16[256,2560]{1,0:T(8,128)(2,1)}, bf16[256,2560]{1,0:T(8,128)(2,1)}, u32[]{:S(2)}, u32[]{:S(2)}) collective-permute-start(bf16[256,2560]{1,0:T(8,128)(2,1)} %get-tuple-element.164.refs_13_), channel_id=1, source_target_pairs={{0,8},{1,9},{2,10},{3,11},{4,12},{5,13},{6,14},{7,15},{8,0},{9,1},... | collective-permute-start | bytes 3932168 | tf_op jit(solution)/shard_map/ppermute | solution.py:130
  365.7 40.0 %collective-permute-start.41 = (bf16[1024,768]{1,0:T(8,128)(2,1)}, bf16[1024,768]{1,0:T(8,128)(2,1)}, u32[]{:S(2)}, u32[]{:S(2)}) collective-permute-start(bf16[1024,768]{1,0:T(8,128)(2,1)} %attend_back.4.refs_4_.refs_2_.refs_1_), channel_id=1, source_target_pairs={{0,1},{1,0},{2,3},{3,2},{4,5},{5,4},{6,7},{7,6},{8,9},{9,8},{10,11... | collective-permute-start | bytes 4718600 | tf_op jit(solution)/shard_map/ppermute | solution.py:130
  403.8 32.7 %collective-permute-start.50 = (bf16[128,1024]{1,0:T(8,128)(2,1)}, bf16[128,1024]{1,0:T(8,128)(2,1)}, u32[]{:S(2)}, u32[]{:S(2)}) collective-permute-start(bf16[128,1024]{1,0:T(8,128)(2,1)} %get-tuple-element.169.refs_9_), channel_id=1, source_target_pairs={{0,2},{1,3},{2,0},{3,1},{4,6},{5,7},{6,4},{7,5},{8,10},{9,11},{10,... | collective-permute-start | bytes 786440 | tf_op jit(solution)/shard_map/ppermute | solution.py:130
  403.8 34.5 %collective-permute-start.46 = (bf16[128,2560]{1,0:T(8,128)(2,1)}, bf16[128,2560]{1,0:T(8,128)(2,1)}, u32[]{:S(2)}, u32[]{:S(2)}) collective-permute-start(bf16[128,2560]{1,0:T(8,128)(2,1)} %get-tuple-element.171.refs_11_), channel_id=1, source_target_pairs={{0,8},{1,9},{2,10},{3,11},{4,12},{5,13},{6,14},{7,15},{8,0},{9,1},... | collective-permute-start | bytes 1966088 | tf_op jit(solution)/shard_map/ppermute | solution.py:130
  404.7 33.6 %collective-permute-start.47 = (bf16[128,2560]{1,0:T(8,128)(2,1)}, bf16[128,2560]{1,0:T(8,128)(2,1)}, u32[]{:S(2)}, u32[]{:S(2)}) collective-permute-start(bf16[128,2560]{1,0:T(8,128)(2,1)} %get-tuple-element.173.refs_13_), channel_id=1, source_target_pairs={{0,16},{1,17},{2,18},{3,19},{4,20},{5,21},{6,22},{7,23},{8,24},{9,... | collective-permute-start | bytes 1966088 | tf_op jit(solution)/shard_map/ppermute | solution.py:130
  436.5 42.5 %collective-permute-start.51 = (bf16[1024,768]{1,0:T(8,128)(2,1)}, bf16[1024,768]{1,0:T(8,128)(2,1)}, u32[]{:S(2)}, u32[]{:S(2)}) collective-permute-start(bf16[1024,768]{1,0:T(8,128)(2,1)} %attend_back.6.refs_8_.refs_2_.refs_3_), channel_id=1, source_target_pairs={{0,1},{1,0},{2,3},{3,2},{4,5},{5,4},{6,7},{7,6},{8,9},{9,8},{10,11... | collective-permute-start | bytes 4718600 | tf_op jit(solution)/shard_map/ppermute | solution.py:130
  443.2 32.7 %collective-permute-start.53 = (bf16[64,5120]{1,0:T(8,128)(2,1)}, bf16[64,5120]{1,0:T(8,128)(2,1)}, u32[]{:S(2)}, u32[]{:S(2)}) collective-permute-start(bf16[64,5120]{1,0:T(8,128)(2,1)} %get-tuple-element.179.refs_11_), channel_id=1, source_target_pairs={{0,4},{1,5},{2,6},{3,7},{4,0},{5,1},{6,2},{7,3},{8,12},{9,13},{10,... | collective-permute-start | bytes 1966088 | tf_op jit(solution)/shard_map/ppermute | solution.py:130
  478.9 39.1 %collective-permute-start.58 = (bf16[64,1536]{1,0:T(8,128)(2,1)}, bf16[64,1536]{1,0:T(8,128)(2,1)}, u32[]{:S(2)}, u32[]{:S(2)}) collective-permute-start(bf16[64,1536]{1,0:T(8,128)(2,1)} %get-tuple-element.188.refs_11_), channel_id=1, source_target_pairs={{0,4},{1,5},{2,6},{3,7},{4,0},{5,1},{6,2},{7,3},{8,12},{9,13},{10,... | collective-permute-start | bytes 589832 | tf_op jit(solution)/shard_map/ppermute | solution.py:130
  (93 other events, 1110.9 us)

commit v2 on v1

--- a/solution.py
+++ b/solution.py
@@ -20,12 +20,14 @@
 MASKED = -1e30
 BQ = 256
 BK = 128
+LENGTHS_OF_RUNS = (3, 4, 5, 7, 8)
 LANES = 128
 TILE = 512
 ROWS = 256
 F32 = jnp.float32
 BF = jnp.bfloat16
-VMEM_BYTES = 56 << 20
+VMEM_BYTES = 28 << 20
+ATTEND_BYTES = 40 << 20
 WEIGHT = 1.15e10
 
 
@@ -49,18 +51,38 @@
     return pl.BlockSpec(shape, lambda *_: (0,) * len(shape))
 
 
-def pallas(kernel, operands, in_specs, after=(), **kept):
+def far(*arrays):
+    return [pltpu.with_memory_space_constraint(array, pltpu.HBM) for array in arrays]
+
+
+def pallas(kernel, operands, in_specs, after=(), vmem=VMEM_BYTES, near=(), far_in=(), **kept):
     given = len(operands)
+    shapes, specs = kept.pop("out_shape"), kept.pop("out_specs")
+    single = not isinstance(shapes, (list, tuple))
+    shapes, specs = ([shapes], [specs]) if single else (list(shapes), list(specs))
+    shapes = [
+        shape if near == "all" or number in near else pltpu.HBM(shape.shape, shape.dtype)
+        for number, shape in enumerate(shapes)
+    ]
+    operands = [
+        far(array)[0] if number in far_in else array for number, array in enumerate(operands)
+    ]
+    waited = [each if each.shape == (8, LANES) else far(each)[0] for each in after]
 
     def body(*refs):
-        kernel(*refs[:given], *refs[given + len(after) :])
-
-    return pl.pallas_call(
+        outs = given + len(after)
+        refs[outs + len(shapes)][...] = jnp.zeros((8, LANES), F32)
+        kernel(*refs[:given], *refs[outs : outs + len(shapes)], *refs[outs + len(shapes) + 1 :])
+
+    *made, token = pl.pallas_call(
         body,
         in_specs=list(in_specs) + [ANY] * len(after),
-        compiler_params=pltpu.CompilerParams(vmem_limit_bytes=VMEM_BYTES),
+        out_specs=specs + [fixed(8, LANES)],
+        out_shape=shapes + [jax.ShapeDtypeStruct((8, LANES), F32)],
+        compiler_params=pltpu.CompilerParams(vmem_limit_bytes=vmem),
         **kept,
-    )(*operands, *after)
+    )(*operands, *waited)
+    return (made[0] if single else made), token
 
 
 class Relay:
@@ -110,6 +132,7 @@
             out_shape=[jax.ShapeDtypeStruct(shape, dtype) for shape, dtype in self.outs],
             cost_estimate=cost(1 + moved * 0.4e-6),
             name=name,
+            near="all",
         )
 
 
@@ -170,57 +193,62 @@
 class Gather:
     def __init__(self, net, shard):
         self.net, self.rows, self.half = net, shard.shape[0], shard.shape[1] // 2
-        self.blocks = [[0]] * 2
+        self.blocks = [[0, 2, 4, 6]] * 2
         self.stage = 0
-        self.held = [(shard, net.swap(shard, 2))]
+        self.held = [[shard] + [net.swap(shard, mask) for mask in (2, 4, 6)]] * 2
 
     def join(self, relay):
-        rows, half = self.rows, self.half
         self.made = []
-        if self.stage == 0:
-            self.made.append(relay.make(2 * rows, 2 * half, BF))
-            for place, array in enumerate(self.held[0]):
-                relay.put(self.made[0], place * rows, 0, rows, 2 * half, [(array, 0, 0)])
-            self.blocks = [[0, 2]] * 2
-        elif self.stage == 1:
-            for side in range(2):
-                self.made.append(relay.make(4 * rows, half, BF))
-                for place, array in enumerate(self.held[0]):
-                    relay.put(self.made[side], 2 * place * rows, 0, 2 * rows, half, [(array, 0, side * half)])
-            self.blocks = [[0, 2, 4, 6]] * 2
-        elif self.stage == 2:
-            for side in range(2):
-                self.made.append(relay.make(8 * rows, half, BF))
-                for place, array in enumerate(self.held[side]):
-                    relay.put(self.made[side], 4 * place * rows, 0, 4 * rows, half, [(array, 0, 0)])
+        for side in range(2):
+            size = self.held[side][0].shape[0]
+            self.made.append(relay.make(len(self.held[side]) * size, self.half, BF))
+            column = side * self.half if self.stage == 0 else 0
+            for place, array in enumerate(self.held[side]):
+                relay.put(self.made[side], place * size, 0, size, self.half, [(array, 0, column)])
+            if self.stage == 1:
                 self.blocks[side] = self.blocks[side] + [block ^ UPPER[side][0] for block in self.blocks[side]]
 
     def follow(self, made):
         arrays = [made[place] for place in self.made]
+        self.held = [(array, self.net.swap(array, UPPER[side][self.stage])) for side, array in enumerate(arrays)]
         self.stage += 1
-        if self.stage == 1:
-            self.held = [(arrays[0], self.net.swap(arrays[0], 4))]
-            return
-        self.held = [(array, self.net.swap(array, UPPER[side][self.stage - 2])) for side, array in enumerate(arrays)]
-        if self.stage == 3:
-            self.pieces = []
-            for side in range(2):
-                own, come = self.held[side]
-                blocks = self.blocks[side]
-                others = [block ^ UPPER[side][1] for block in blocks]
-                for here, array in ((blocks, own), (others, come)):
-                    self.pieces += [(side, here, array), (side, [block ^ 1 for block in here], self.net.swap(array, 1))]
+        if self.stage == 2:
+            self.kept = [self.net.swap(array, 1) for array in arrays]
+
+    def finish(self, after=()):
+        sent = [come for _, come in self.held]
+        if after:
+            relay = Relay()
+            for array in sent:
+                relay.put(relay.make(*array.shape, BF), 0, 0, *array.shape, [(array, 0, 0)])
+            sent, token = relay.run(after, "hold")
+        self.pieces = []
+        for side in range(2):
+            blocks = self.blocks[side]
+            others = [block ^ UPPER[side][1] for block in blocks]
+            self.pieces += [
+                (side, blocks, self.held[side][0]),
+                (side, [block ^ 1 for block in blocks], self.kept[side]),
+                (side, others, self.held[side][1]),
+                (side, [block ^ 1 for block in others], self.net.swap(sent[side], 1)),
+            ]
+        return token if after else None
 
     def arrivals(self):
-        return [come for _, come in self.held]
+        return [array for held in self.held for array in held[1:]]
+
+
+def whole(array):
+    return [(0, None, array)]
 
 
 class Scatter:
-    def __init__(self, net, sides):
+    def __init__(self, net, sides, widths=()):
         self.net = net
         self.stage = 0
         self.half = sides[0][0].shape[1]
         self.rows = sides[0][0].shape[0] // 8
+        self.widths = widths or (2 * self.half,)
         self.held = [(stays, net.swap(leaves, UPPER[side][0])) for side, (stays, leaves) in enumerate(sides)]
 
     def join(self, relay):
@@ -233,17 +261,16 @@
                     first = 4 * rows * leaving
                     relay.put(self.made[-1], 0, 0, 4 * rows, half, [(own, first, 0), (come, first, 0)])
         elif self.stage == 1:
-            for leaving in range(2):
-                self.made.append(relay.make(2 * rows, 2 * half, BF if leaving else F32))
-                first = 2 * rows * leaving
+            for z in range(4):
+                self.made.append(relay.make(rows, 2 * half, BF if z else F32))
                 for side, (own, come) in enumerate(self.held):
-                    relay.put(self.made[-1], 0, side * half, 2 * rows, half, [(own, first, 0), (come, first, 0)])
-        elif self.stage == 2:
-            own, come = self.held[0]
-            for leaving in range(2):
-                self.made.append(relay.make(rows, 2 * half, BF if leaving else F32))
-                first = rows * leaving
-                relay.put(self.made[-1], 0, 0, rows, 2 * half, [(own, first, 0), (come, first, 0)])
+                    relay.put(self.made[-1], 0, side * half, rows, half, [(own, z * rows, 0), (come, z * rows, 0)])
+        else:
+            column = 0
+            for width in self.widths:
+                self.made.append(relay.make(rows, width, F32))
+                relay.put(self.made[-1], 0, 0, rows, width, [(array, 0, column) for array in self.held])
+                column += width
 
     def follow(self, made):
         arrays = [made[place] for place in self.made]
@@ -251,34 +278,34 @@
         if self.stage == 1:
             self.held = [(arrays[2 * side], self.net.swap(arrays[2 * side + 1], UPPER[side][1])) for side in range(2)]
         elif self.stage == 2:
-            self.held = [(arrays[0], self.net.swap(arrays[1], 4))]
+            self.held = [arrays[0]] + [self.net.swap(arrays[z], 2 * z) for z in range(1, 4)]
         else:
-            self.result = self.net.narrow(arrays[0] + self.net.swap(arrays[1], 2).astype(F32))
+            self.result = [self.net.narrow(array) for array in arrays]
 
 
 class Sum:
     def __init__(self, net, value):
-        self.net, self.value, self.stage = net, value, 0
+        self.net, self.value = net, value
+        bits = [1 << place for place in range(net.count.bit_length() - 1)]
+        self.groups = [(1,)] + [(bit,) for bit in bits[3:]] + [(2, 4, 6)]
         self.send()
 
     def send(self):
-        self.come = self.net.permute(self.value, 1 << self.stage)
+        self.come = [self.net.permute(self.value, mask) for mask in self.groups.pop(0)]
 
     def join(self, relay):
         self.made = relay.make(*self.value.shape, self.value.dtype)
-        relay.put(self.made, 0, 0, *self.value.shape, [(self.value, 0, 0), (self.come, 0, 0)])
+        relay.put(self.made, 0, 0, *self.value.shape, [(array, 0, 0) for array in (self.value, *self.come)])
 
     def follow(self, made):
         self.value = made[self.made]
-        self.stage += 1
         self.send()
 
     def finish(self):
-        for place in range(self.stage + 1, self.net.count.bit_length()):
-            self.value = self.value + self.come
-            if place < self.net.count.bit_length() - 1:
-                self.come = self.net.permute(self.value, 1 << place)
-        return self.value
+        while self.groups:
+            self.value = self.value + sum(self.come)
+            self.send()
+        return (self.value, *self.come)
 
 
 def advance(moving, after=(), name="relay", extra=None):
@@ -287,10 +314,10 @@
         extra(relay)
     for each in moving:
         each.join(relay)
-    made = relay.run(after, name)
+    made, token = relay.run(after, name)
     for each in moving:
         each.follow(made)
-    return made
+    return made, token
 
 
 def fetch(me, pieces, refs, columns, target, sem):
@@ -298,6 +325,9 @@
     for (side, blocks, width, rows), ref in zip(pieces, refs):
         begin, end = max(first, side * width), min(last, (side + 1) * width)
         if begin >= end:
+            continue
+        if blocks is None:
+            pltpu.make_async_copy(ref.at[:, pl.ds(begin, end - begin)], target, sem).start()
             continue
         for place, block in enumerate(blocks):
             row = pl.multiple_of((me ^ block) * rows, rows)
@@ -313,7 +343,10 @@
 
 
 def describe(pieces):
-    return [(side, tuple(blocks), array.shape[1], array.shape[0] // len(blocks)) for side, blocks, array in pieces]
+    return [
+        (side, blocks and tuple(blocks), array.shape[1], array.shape[0] // len(blocks or (0,)))
+        for side, blocks, array in pieces
+    ]
 
 
 def normed(inputs):
@@ -372,14 +405,37 @@
 TABLE = 16
 
 
-def lines_of(me, small):
-    flat = jnp.zeros((BLOCKS * LANES,), BF)
+def prepare_kernel(me_ref, shard, *rest):
+    small, (joined, row, rows) = rest[:-3], rest[-3:]
+    joined[:, : 3 * D] = shard[...]
+    rows[...] = jnp.zeros_like(rows)
     line = 0
     for values, lines, length in zip(small, LINES, LENGTHS):
-        place = line * LANES + (0 if length == LANES else (me % 4) * length)
-        flat = lax.dynamic_update_slice(flat, values, (place,))
+        row[...] = jnp.zeros_like(row)
+        row[0:1, :length] = values[...].astype(F32)
+        place = 0 if length == LANES else (me_ref[0] % 4) * length
+        turned = pltpu.roll(row[:, : lines * LANES], place, 1)
+        for part in range(lines):
+            rows[line + part : line + part + 1, :] = turned[0:1, part * LANES : (part + 1) * LANES]
         line += lines
-    return flat.reshape(BLOCKS, LANES)
+    joined[:, 3 * D : 3 * D + LANES] = rows[...].astype(BF)
+    joined[:, 3 * D + LANES :] = jnp.zeros((BLOCKS, LANES), BF)
+
+
+def prepare(me, shard, small):
+    small = [values.reshape(1, -1) for values in small]
+    return pallas(
+        prepare_kernel,
+        in_specs=[SMEM, fixed(*shard.shape)] + [fixed(*values.shape) for values in small],
+        out_specs=fixed(BLOCKS, 3 * D + 2 * LANES),
+        out_shape=jax.ShapeDtypeStruct((BLOCKS, 3 * D + 2 * LANES), BF),
+        scratch_shapes=[pltpu.VMEM((8, 3 * LANES), F32), pltpu.VMEM((BLOCKS, LANES), F32)],
+        cost_estimate=cost(2),
+        name="prepare",
+        near="all",
+        far_in=range(1, 10),
+        operands=(me, shard, *small),
+    )
 
 
 def table_of(lines, table):
@@ -456,8 +512,10 @@
             pltpu.SemaphoreType.DMA,
             pltpu.SemaphoreType.DMA,
         ],
-        cost_estimate=cost(16),
+        cost_estimate=cost(16 / 4),
         name="project",
+        far_in=(1, *range(4, 4 + len(pieces))),
+        near=(1, 3),
         operands=(me, tokens, cosine, sine, *[array for _, _, array in pieces]),
         after=after,
     )
@@ -497,8 +555,10 @@
         out_shape=[jax.ShapeDtypeStruct((count, D), F32), jax.ShapeDtypeStruct((count, D), BF)]
         + [jax.ShapeDtypeStruct((D // 2, count), BF)] * 4,
         scratch_shapes=[pltpu.VMEM((D, D), BF), pltpu.SemaphoreType.DMA],
-        cost_estimate=cost(12),
+        cost_estimate=cost(12 / 4),
         name="branch",
+        far_in=(1, 2, *range(4, 4 + len(pieces))),
+        near=(1, 3, 5),
             operands=(me, mixed, tokens, table, *[array for _, _, array in pieces],),
         after=after,
     )
@@ -516,7 +576,7 @@
 
 def up_kernel(layout_of, me_ref, normed_two, table, *rest):
     refs = rest[: len(layout_of)]
-    activ, slope, activ_kept, activ_sent, weight, sem = rest[len(layout_of) :]
+    activ, slope, activ_sent, weight, sem = rest[len(layout_of) :]
     step = pl.program_id(0)
 
     @pl.when(step == 0)
@@ -531,21 +591,14 @@
         part = slice(begin, begin + ROWS)
         value = nn(normed_two[part, :], weight[:, pl.ds(column, TILE)]) + bias
         share, density = gelu_parts(value)
-        activ[part, :] = (value * share).astype(BF)
+        low = (value * share).astype(BF)
+        activ[part, :] = low
         slope[part, :] = (share + value * density).astype(BF)
-        turned = activ[part, :].T
         rows = FF // BLOCKS
-        parity = me_ref[0] & 1
-        for block in range(TILE // rows):
-            here = slice(block // 2 * rows, (block // 2 + 1) * rows)
-
-            @pl.when(parity == block % 2)
-            def _():
-                activ_kept[here, part] = turned[block * rows : (block + 1) * rows, :]
-
-            @pl.when(parity != block % 2)
-            def _():
-                activ_sent[here, part] = turned[block * rows : (block + 1) * rows, :]
+        odd = (me_ref[0] & 1) == 1
+        pairs = [low[:, begin : begin + 2 * rows] for begin in range(0, TILE, 2 * rows)]
+        sent = [jnp.where(odd, pair[:, :rows], pair[:, rows:]) for pair in pairs]
+        activ_sent[part, :] = jnp.concatenate(sent, 1)
 
 
 def up(me, normed_two, table, pieces, after=()):
@@ -556,62 +609,88 @@
         functools.partial(up_kernel, layout_of),
         grid=(FF // TILE,),
         in_specs=[SMEM, fixed(count, D), fixed(TABLE, D)] + [ANY] * len(pieces),
-        out_specs=[tile, tile] + [pl.BlockSpec((TILE // 2, count), lambda step: (step, 0))] * 2,
-        out_shape=[jax.ShapeDtypeStruct((count, FF), BF)] * 2 + [jax.ShapeDtypeStruct((FF // 2, count), BF)] * 2,
+        out_specs=[tile, tile, pl.BlockSpec((count, TILE // 2), lambda step: (0, step))],
+        out_shape=[jax.ShapeDtypeStruct((count, FF), BF)] * 2 + [jax.ShapeDtypeStruct((count, FF // 2), BF)],
         scratch_shapes=[pltpu.VMEM((D, FF), BF), pltpu.SemaphoreType.DMA],
-        cost_estimate=cost(35),
+        cost_estimate=cost(35 / 4),
         name="up",
+        far_in=range(3, 3 + len(pieces)),
             operands=(me, normed_two, table, *[array for _, _, array in pieces],),
         after=after,
     )
 
 
-def down_kernel(layout_of, me_ref, activ, slope, cotangent, resid, table, *rest):
-    refs = rest[: len(layout_of)]
-    output, grad_pre, grad_bias, weight, total, sem = rest[len(layout_of) :]
-    step = pl.program_id(0)
-
-    @pl.when(step == 0)
-    def _():
-        fetch(me_ref[0], layout_of, refs, (0, D), weight, sem)
-        total[...] = resid[...] + line_of(table, DOWN_B)
-        arrive(weight, sem)
-
-    rows = weight[pl.ds(pl.multiple_of(step * TILE, TILE), TILE), :]
+def pre_kernel(slope, cotangent, weight, grad_pre, grad_bias):
     sums = jnp.zeros((1, TILE), F32)
-    for begin in range(0, activ.shape[0], ROWS):
+    for begin in range(0, slope.shape[0], ROWS):
         part = slice(begin, begin + ROWS)
-        total[part, :] += nn(activ[part, :], rows)
-        back = (nt(cotangent[part, :], rows) * slope[part, :].astype(F32)).astype(BF)
+        back = (nt(cotangent[part, :], weight[...]) * slope[part, :].astype(F32)).astype(BF)
         grad_pre[part, :] = back
         sums += jnp.sum(back.astype(F32), axis=0, keepdims=True)
     grad_bias[...] = sums
 
+
+def pre(slope, cotangent, weight, after=()):
+    count = slope.shape[0]
+    tile = pl.BlockSpec((count, TILE), lambda step: (0, step))
+    return pallas(
+        pre_kernel,
+        grid=(FF // TILE,),
+        in_specs=[tile, fixed(count, D), pl.BlockSpec((TILE, D), lambda step: (step, 0))],
+        out_specs=[tile, pl.BlockSpec((1, TILE), lambda step: (0, step))],
+        out_shape=[jax.ShapeDtypeStruct((count, FF), BF), jax.ShapeDtypeStruct((1, FF), F32)],
+        cost_estimate=cost(16),
+        name="pre",
+        far_in=(0, 1, 2),
+        operands=(slope, cotangent, weight),
+        after=after,
+    )
+
+
+def output_kernel(activ, resid, table, weight, *rest):
+    output, total = rest[-2:]
+    step = pl.program_id(0)
+
+    @pl.when(step == 0)
+    def _():
+        total[...] = resid[...] + line_of(table, DOWN_B)
+
+    total[...] += nn(activ[...], weight[...])
+
     @pl.when(step == pl.num_programs(0) - 1)
     def _():
         output[...] = total[...].astype(BF)
 
 
-def down(me, activ, slope, cotangent, resid, table, pieces, after=()):
+def output_rows(activ, resid, table, weight, part, parts, before=(), after=()):
     count = activ.shape[0]
-    layout_of = describe(pieces)
-    tile = pl.BlockSpec((count, TILE), lambda step: (0, step))
+    rows = count // parts
+    wide_tile = 2 * TILE
+    mine = pl.BlockSpec((rows, D), lambda step: (part, 0))
     return pallas(
-        functools.partial(down_kernel, layout_of),
-        grid=(FF // TILE,),
-        in_specs=[SMEM, tile, tile, fixed(count, D), fixed(count, D), fixed(TABLE, D)] + [ANY] * len(pieces),
-        out_specs=[fixed(count, D), tile, pl.BlockSpec((1, TILE), lambda step: (0, step))],
-        out_shape=[
-            jax.ShapeDtypeStruct((count, D), BF),
-            jax.ShapeDtypeStruct((count, FF), BF),
-            jax.ShapeDtypeStruct((1, FF), F32),
-        ],
-        scratch_shapes=[pltpu.VMEM((FF, D), BF), pltpu.VMEM((count, D), F32), pltpu.SemaphoreType.DMA],
-        cost_estimate=cost(29),
-        name="down",
-            operands=(me, activ, slope, cotangent, resid, table, *[array for _, _, array in pieces],),
+        output_kernel,
+        grid=(FF // wide_tile,),
+        in_specs=[
+            pl.BlockSpec((rows, wide_tile), lambda step: (part, step)),
+            mine,
+            fixed(TABLE, D),
+            pl.BlockSpec((wide_tile, D), lambda step: (step, 0)),
+        ]
+        + [ANY] * len(before),
+        out_specs=mine,
+        out_shape=jax.ShapeDtypeStruct((count, D), BF),
+        scratch_shapes=[pltpu.VMEM((rows, D), F32)],
+        input_output_aliases={4 + place: place for place in range(len(before))},
+        cost_estimate=cost(16 // parts),
+        name="output",
+        far_in=(0, 1, 3),
+        operands=(activ, resid, table, weight, *before),
         after=after,
     )
+
+
+def tn(left, right):
+    return lax.dot_general(left, right, (((0,), (0,)), ((), ())), preferred_element_type=F32)
 
 
 def outer_rows_kernel(me_ref, left, left_other, right, right_other, *rest):
@@ -620,11 +699,12 @@
     rows = FF // BLOCKS
     half = right.shape[1] // 2
 
-    def group(ref):
-        places = [(4 * step + z) ^ (me_ref[0] >> 1) for z in range(4)]
-        return jnp.concatenate([ref[pl.ds(pl.multiple_of(place * rows, rows), rows), :] for place in places], 0)
-
-    product = nn(group(left), right[...]) + nn(group(left_other), right_other[...])
+    def group(ref, places):
+        return jnp.concatenate([ref[:, pl.ds(pl.multiple_of(place * rows, rows), rows)] for place in places], 1)
+
+    own = group(left, [me_ref[0] ^ (2 * (4 * step + z)) for z in range(4)])
+    other = group(left_other, [(me_ref[0] >> 1) ^ (4 * step + z) for z in range(4)])
+    product = tn(own, right[...]) + tn(other, right_other[...])
     for side in range(2):
         bit = (step >> (1 - side)) & 1
         values = product[:, side * half : (side + 1) * half]
@@ -643,13 +723,13 @@
 
 
 def outer_rows(me, left, left_other, right, right_other, after=()):
-    size, count = left.shape
+    count, size = left_other.shape
     width = right.shape[1]
     block = (4 * FF // BLOCKS, width // 2)
     return pallas(
         outer_rows_kernel,
         grid=(4,),
-        in_specs=[SMEM] + [fixed(size, count)] * 2 + [fixed(count, width)] * 2,
+        in_specs=[SMEM, fixed(count, 2 * size), fixed(count, size)] + [fixed(count, width)] * 2,
         out_specs=[
             pl.BlockSpec(block, lambda step: (jnp.minimum(step, 1), 0)),
             pl.BlockSpec(block, lambda step: (jnp.maximum(step - 2, 0), 0)),
@@ -659,19 +739,20 @@
         ],
         out_shape=[jax.ShapeDtypeStruct((size // 2, width // 2), kind) for kind in (F32, BF, F32, BF)]
         + [jax.ShapeDtypeStruct((1, width), F32)],
-        cost_estimate=cost(17),
+        cost_estimate=cost(16),
         name="outer_rows",
+        far_in=(1, 2, 3, 4),
+        near=(0, 1, 2, 3),
         operands=(me, left, left_other, right, right_other),
         after=after,
     )
 
 
 def outer_kernel(tiles, parts, *refs):
-    sides = refs[4 * len(parts) : 4 * len(parts) + 4]
-    grad_bias = refs[4 * len(parts) + 4]
+    sides, grad_bias = refs[-5:-1], refs[-1]
     step = pl.program_id(0)
-    for number, (begin, end) in enumerate(parts):
-        left, left_other, right, right_other = refs[4 * number : 4 * number + 4]
+    for begin, end, *places in parts:
+        left, left_other, right, right_other = [refs[place] for place in places]
         rows = left.shape[0] // (BLOCKS // 2)
 
         @pl.when((step >= begin) & (step < end))
@@ -692,16 +773,28 @@
 
 def outer(sets, tile_width, after=()):
     size, count = sets[0][0].shape
-    parts, tiles, in_specs = [], 0, []
-    for _, _, right, _ in sets:
+    parts, tiles, operands, in_specs = [], 0, [], []
+
+    def take(array, spec):
+        for place, known in enumerate(operands):
+            if known is array:
+                return place
+        operands.append(array)
+        in_specs.append(spec)
+        return len(operands) - 1
+
+    for left, left_other, right, right_other in sets:
         begin, end = tiles, tiles + right.shape[1] // tile_width
-        parts.append((begin, end))
+
+        def tile_of(step, begin=begin, end=end):
+            return 0, jnp.clip(step - begin, 0, end - begin - 1)
+
+        spec = pl.BlockSpec((count, tile_width), tile_of)
+        places = [take(each, fixed(size, count)) for each in (left, left_other)]
+        places += [take(each, spec) for each in (right, right_other)]
+        parts.append((begin, end, *places))
         tiles = end
 
-        def place(step, begin=begin, end=end):
-            return 0, jnp.clip(step - begin, 0, end - begin - 1)
-
-        in_specs += [fixed(size, count)] * 2 + [pl.BlockSpec((count, tile_width), place)] * 2
     width = tiles * tile_width
     block = (size // 2, tile_width)
     firsts = pl.BlockSpec(block, lambda step: (0, jnp.minimum(step, tiles // 2 - 1)))
@@ -715,7 +808,9 @@
         + [jax.ShapeDtypeStruct((1, width), F32)],
         cost_estimate=cost(4 * count * size * width / 0.55e9),
         name="outer",
-        operands=tuple(array for each in sets for array in each),
+        far_in=range(len(operands)),
+        near=(0, 1, 2, 3),
+        operands=tuple(operands),
         after=after,
     )
 
@@ -775,27 +870,36 @@
         ],
         cost_estimate=cost(21),
         name="branch_back",
+        far_in=(1, 2, 3, *range(5, 5 + len(pieces))),
+        near=(1, 2),
             operands=(me, grad_pre, resid, cotangent, table, *[array for _, _, array in pieces],),
         after=after,
     )
 
 
-def tokens_back_kernel(layout_of, chunks, me_ref, *rest):
+def tokens_back_kernel(layout_of, chunks, biases, me_ref, *rest):
     grads, rest = rest[:chunks], rest[chunks:]
-    tokens, grad_resid, table = rest[:3]
-    refs = rest[3 : 3 + len(layout_of)]
-    grad_tokens, grad_gain, grad_shift, weight, sem = rest[3 + len(layout_of) :]
+    qkv_biases, rest = rest[:biases], rest[biases:]
+    tokens, grad_resid, table, out_bias, up_bias, down_bias, gain_two, shift_two = rest[:8]
+    refs = rest[8 : 8 + len(layout_of)]
+    grad_tokens, grad_table, weight, sem = rest[8 + len(layout_of) :]
 
     @pl.when(pl.program_id(0) == 0)
     def _():
         fetch(me_ref[0], layout_of, refs, (0, 3 * D), weight, sem)
-        grad_gain[...] = jnp.zeros_like(grad_gain)
-        grad_shift[...] = jnp.zeros_like(grad_shift)
+        grad_table[...] = jnp.zeros_like(grad_table)
+        for ref, row in ((out_bias, OUT_B), (down_bias, DOWN_B), (gain_two, GAIN_TWO), (shift_two, SHIFT_TWO)):
+            grad_table[row : row + 1, :] = ref[...]
+        for part in range(FF // D):
+            grad_table[UP_B + part : UP_B + part + 1, :] = up_bias[:, part * D : (part + 1) * D]
+        groups = [(ref, begin) for ref in qkv_biases for begin in range(0, ref.shape[1], 3 * QUAD)]
+        for quad, (ref, begin) in enumerate(groups):
+            for part in range(3):
+                values = ref[:, begin + part * QUAD : begin + (part + 1) * QUAD]
+                grad_table[QKV_B + part : QKV_B + part + 1, quad * QUAD : (quad + 1) * QUAD] = values
         arrive(weight, sem)
 
-    quads = [
-        (ref, begin) for ref in grads for begin in range(0, ref.shape[1], 3 * QUAD)
-    ]
+    quads = [(ref, begin) for ref in grads for begin in range(0, ref.shape[1], 3 * QUAD)]
     ordered = jnp.concatenate(
         [ref[:, begin + part * QUAD : begin + (part + 1) * QUAD] for part in range(3) for ref, begin in quads], 1
     )
@@ -803,28 +907,71 @@
         tokens[...].astype(F32), line_of(table, GAIN_ONE), nt(ordered, weight[...])
     )
     grad_tokens[...] = (grad_resid[...] + back).astype(BF)
-    grad_gain[...] += gain_part
-    grad_shift[...] += shift_part
-
-
-def tokens_back(me, grads, tokens, grad_resid, table, pieces, after=()):
+    grad_table[GAIN_ONE : GAIN_ONE + 1, :] += gain_part
+    grad_table[SHIFT_ONE : SHIFT_ONE + 1, :] += shift_part
+
+
+def tokens_back(me, grads, qkv_biases, tokens, grad_resid, table, biases, pieces, after=()):
     count = tokens.shape[0]
     layout_of = describe(pieces)
     rows = pl.BlockSpec((ROWS, D), lambda step: (step, 0))
-    vector = jax.ShapeDtypeStruct((1, D), F32)
     return pallas(
-        functools.partial(tokens_back_kernel, layout_of, len(grads)),
+        functools.partial(tokens_back_kernel, layout_of, len(grads), len(qkv_biases)),
         grid=(count // ROWS,),
         in_specs=[SMEM]
         + [pl.BlockSpec((ROWS, part.shape[1]), lambda step: (step, 0)) for part in grads]
+        + [fixed(*part.shape) for part in qkv_biases]
         + [rows, rows, fixed(TABLE, D)]
+        + [fixed(*part.shape) for part in biases]
         + [ANY] * len(pieces),
-        out_specs=[rows, fixed(1, D), fixed(1, D)],
-        out_shape=[jax.ShapeDtypeStruct((count, D), BF), vector, vector],
+        out_specs=[rows, fixed(TABLE, D)],
+        out_shape=[jax.ShapeDtypeStruct((count, D), BF), jax.ShapeDtypeStruct((TABLE, D), F32)],
         scratch_shapes=[pltpu.VMEM((D, 3 * D), BF), pltpu.SemaphoreType.DMA],
         cost_estimate=cost(15),
         name="tokens_back",
-            operands=(me, *grads, tokens, grad_resid, table, *[array for _, _, array in pieces],),
+        far_in=range(len(grads) + len(qkv_biases) + 1, len(grads) + len(qkv_biases) + 3),
+        operands=(me, *grads, *qkv_biases, tokens, grad_resid, table, *biases, *[array for _, _, array in pieces]),
+        after=after,
+    )
+
+
+def finish_kernel(lengths, number, *refs):
+    weights, sums, outs = refs[:8], refs[8:12], refs[12:]
+    for chunk in range(2):
+        arrived = weights[4 * chunk : 4 * chunk + 4]
+        for half in range(2):
+            for part in range(3):
+                source = slice((3 * half + part) * QUAD, (3 * half + part + 1) * QUAD)
+                target = part * D + (2 * chunk + half) * QUAD
+                total = arrived[0][:, source]
+                for ref in arrived[1:]:
+                    total = total + ref[:, source].astype(F32)
+                outs[0][:, target : target + QUAD] = total
+    row = 0
+    for place, (length, lines) in enumerate(lengths):
+        place_in = number[0] * length
+        wide_row = jnp.concatenate(
+            [sum(line_of(ref, row + line) for ref in sums) for line in range(lines)], 1
+        )
+        wide_row = jnp.broadcast_to(wide_row, (8, lines * D))
+        turned = pltpu.roll(wide_row, lines * D - place_in, 1)
+        outs[1 + place][...] = turned[0:1, :length]
+        row += lines
+
+
+def finish(number, weights, total, sizes, count, after):
+    lengths = [(size // count, size // D) for size in sizes]
+    rows = weights[0].shape[0]
+    return pallas(
+        functools.partial(finish_kernel, lengths),
+        in_specs=[SMEM] + [fixed(*array.shape) for array in (*weights, *total)],
+        out_specs=[fixed(rows, 3 * D)] + [fixed(1, length) for length, _ in lengths],
+        out_shape=[jax.ShapeDtypeStruct((rows, 3 * D), F32)]
+        + [jax.ShapeDtypeStruct((1, length), F32) for length, _ in lengths],
+        cost_estimate=cost(3),
+        name="finish",
+        near="all",
+        operands=(number, *weights, *total),
         after=after,
     )
 
@@ -852,27 +999,26 @@
     for block in range(count // BQ):
         part = slice(block * BQ, (block + 1) * BQ)
         begin = jnp.min(first[:, part]) // BK
-        runs[0, block] = begin
-        runs[1, block] = (jnp.max(last[:, part]) + (BK - 1)) // BK - begin
+        needed = (jnp.max(last[:, part]) + (BK - 1)) // BK - begin
+        length = jnp.int32(LENGTHS_OF_RUNS[-1])
+        for size in LENGTHS_OF_RUNS[-2::-1]:
+            length = jnp.where(needed <= size, size, length)
+        runs[0, block] = jnp.minimum(begin, count // BK - length)
+        runs[1, block] = length
 
 
 def each_block(count, runs, work):
-    blocks = count // BQ
-
-    @pl.loop(0, 2 * blocks)
-    def _(index):
-        block = lax.rem(index, blocks)
-        pair = index // blocks
-        for size in range(1, count // BK + 1):
+    @pl.loop(0, count // BQ)
+    def _(block):
+        for size in LENGTHS_OF_RUNS:
 
             @pl.when(runs[1, block] == size)
             def _():
-                work(
-                    pair,
-                    pl.multiple_of(block * BQ, BQ),
-                    pl.multiple_of(runs[0, block] * BK, BK),
-                    size * BK,
-                )
+                work(pl.multiple_of(block * BQ, BQ), pl.multiple_of(runs[0, block] * BK, BK), size * BK)
+
+
+def pair_of(head):
+    return slice(head // 2 * LANES, (head // 2 + 1) * LANES)
 
 
 def one_head(pair_values, head):
@@ -890,22 +1036,24 @@
 
     turned[...] = values[...].T
 
-    def work(pair, row, key, size):
-        lanes = pl.ds(pl.multiple_of(pair * LANES, LANES), LANES)
-        rows = queries[pl.ds(row, BQ), lanes]
-        these = keys[pl.ds(key, size), lanes]
-        bias = mask[pl.ds(key, size), pl.ds(row, BQ)]
-        scores = [nt(these, one_head(rows, head)) + bias for head in range(2)]
+    heads = queries.shape[1] // HEAD
+
+    def work(row, key, size):
+        block, span = pl.ds(row, BQ), pl.ds(key, size)
+        bias = mask[span, block]
+        scores = [
+            nt(keys[span, pair_of(head)], one_head(queries[block, pair_of(head)], head % 2)) + bias
+            for head in range(heads)
+        ]
         results = []
-        for head in range(2):
+        for head in range(heads):
             highest = jnp.max(scores[head], axis=0, keepdims=True)
             expo = jnp.exp(scores[head] - highest)
             totals = jnp.sum(expo, axis=0, keepdims=True)
-            place = pl.multiple_of(pair * LANES + head * HEAD, HEAD)
-            result = nn(turned[pl.ds(place, HEAD), pl.ds(key, size)], expo.astype(BF))
+            result = nn(turned[head * HEAD : (head + 1) * HEAD, span], expo.astype(BF))
             results.append(result * (1.0 / totals))
-            log_totals[pl.ds(2 * pair + head, 1), pl.ds(row, BQ)] = highest + jnp.log(totals)
-        mixed[pl.ds(row, BQ), lanes] = jnp.concatenate(results, 0).T.astype(BF)
+            log_totals[head : head + 1, block] = highest + jnp.log(totals)
+        mixed[block, :] = jnp.concatenate(results, 0).T.astype(BF)
 
     each_block(count, runs, work)
 
@@ -914,29 +1062,32 @@
 QUADS = HEADS // 4
 
 
-def attend(frames, patches, qkv, begin, quads, before=(), after=()):
+def attend(frames, patches, qkv, after=()):
     count = qkv.shape[0]
+    groups, wide_block = QUADS // 2, 2 * QUAD
 
     def columns(part):
-        return pl.BlockSpec((count, QUAD), lambda step: (0, part * QUADS + begin + step))
-
-    return pallas(
+        return pl.BlockSpec((count, wide_block), lambda step: (0, part * groups + step))
+
+    (mixed, log_totals), token = pallas(
         attend_kernel,
-        grid=(quads,),
-        in_specs=[SMEM, SMEM, columns(0), columns(1), columns(2)] + [ANY] * len(before),
-        out_specs=[columns(0), pl.BlockSpec((None, 4, count), lambda step: (begin + step, 0, 0))],
-        out_shape=[jax.ShapeDtypeStruct((count, D), BF), jax.ShapeDtypeStruct((QUADS, 4, count), F32)],
+        grid=(groups,),
+        in_specs=[SMEM, SMEM, columns(0), columns(1), columns(2)],
+        out_specs=[columns(0), pl.BlockSpec((None, 8, count), lambda step: (step, 0, 0))],
+        out_shape=[jax.ShapeDtypeStruct((count, D), BF), jax.ShapeDtypeStruct((groups, 8, count), F32)],
         scratch_shapes=[
             pltpu.VMEM((count, count), F32),
-            pltpu.VMEM((QUAD, count), BF),
+            pltpu.VMEM((wide_block, count), BF),
             pltpu.SMEM((2, count // BQ), jnp.int32),
         ],
-        input_output_aliases={5 + place: place for place in range(len(before))},
-        cost_estimate=cost(9 * quads),
+        cost_estimate=cost(26 / 4),
         name="attend",
-            operands=(frames, patches, qkv, qkv, qkv, *before,),
+        far_in=(2, 3, 4),
+        vmem=ATTEND_BYTES,
+        operands=(frames, patches, qkv, qkv, qkv),
         after=after,
     )
+    return (mixed, log_totals.reshape(QUADS, 4, count)), token
 
 
 def attend_back_kernel(
@@ -975,28 +1126,28 @@
         own, product, (((1,), (1,)), ((), ())), precision=lax.Precision.HIGHEST, preferred_element_type=F32
     )
 
-    def work(pair, row, key, size):
-        lanes = pl.ds(pl.multiple_of(pair * LANES, LANES), LANES)
-        block = pl.ds(row, BQ)
-        span = pl.ds(key, size)
+    def work(row, key, size):
+        block, span = pl.ds(row, BQ), pl.ds(key, size)
         bias = mask[span, block]
-        these, those = keys[span, lanes], values[span, lanes]
-        rows = [one_head(queries[block, lanes], head) for head in range(2)]
-        rows_grads = [one_head(grads[block, lanes], head) for head in range(2)]
+        heads = range(QUAD // HEAD)
+        rows = [one_head(queries[block, pair_of(head)], head % 2) for head in heads]
+        rows_grads = [one_head(grads[block, pair_of(head)], head % 2) for head in heads]
+        shares = [nt(keys[span, pair_of(head)], rows[head]) + bias for head in heads]
+        changes = [nt(values[span, pair_of(head)], rows_grads[head]) for head in heads]
         probs, grad_scores, grad_rows = [], [], []
-        for head in range(2):
-            here = pl.ds(2 * pair + head, 1)
-            share = jnp.exp(nt(these, rows[head]) + bias - log_totals[here, block])
-            change = (share * (nt(those, rows_grads[head]) - inner[here, block])).astype(BF)
-            place = pl.multiple_of(pair * LANES + head * HEAD, HEAD)
-            grad_rows.append(nn(turned[pl.ds(place, HEAD), span], change))
+        for head in heads:
+            share = jnp.exp(shares[head] - log_totals[head : head + 1, block])
+            change = (share * (changes[head] - inner[head : head + 1, block])).astype(BF)
+            grad_rows.append(nn(turned[head * HEAD : (head + 1) * HEAD, span], change))
             probs.append(share.astype(BF))
             grad_scores.append(change)
-        grad_values[span, lanes] += nn(jnp.concatenate(probs, 1), jnp.concatenate(rows_grads, 0))
-        grad_keys[span, lanes] += nn(jnp.concatenate(grad_scores, 1), jnp.concatenate(rows, 0))
-        turned_back = jnp.concatenate(grad_rows, 0).T * HEAD**-0.5
-        turned_back = turned_back * cosine[block, :] - partner(turned_back) * sine[block, :]
-        grad_projected[block, lanes] = turned_back.astype(BF)
+        for pair in range(QUAD // LANES):
+            lanes, two = slice(pair * LANES, (pair + 1) * LANES), slice(2 * pair, 2 * pair + 2)
+            grad_values[span, lanes] += nn(jnp.concatenate(probs[two], 1), jnp.concatenate(rows_grads[two], 0))
+            grad_keys[span, lanes] += nn(jnp.concatenate(grad_scores[two], 1), jnp.concatenate(rows[two], 0))
+        back = jnp.concatenate(grad_rows, 0).T * HEAD**-0.5
+        back = back * wide(cosine[block, :], QUAD) - partner(back) * wide(sine[block, :], QUAD)
+        grad_projected[block, :QUAD] = back.astype(BF)
 
     each_block(count, runs, work)
     back = grad_keys[...] * wide(cosine[...], QUAD) - partner(grad_keys[...]) * wide(sine[...], QUAD)
@@ -1037,6 +1188,8 @@
         ],
         cost_estimate=cost(15 * quads),
         name="attend_back",
+        far_in=(2, 3, 4, 5),
+        near=(0,),
             operands=(frames, patches, qkv, qkv, qkv, mixed, grads, log_totals, cosine, sine,),
         after=after,
     )
@@ -1108,14 +1261,11 @@
     me_ref = net.me.reshape(1)
     small = (qkv_bias, out_bias, up_bias, down_bias, norm1_gain, norm1_shift, norm2_gain, norm2_shift)
     sizes = [item.shape[0] * count for item in small]
-    ends = list(np.cumsum(sizes))
     clips = (clip_frames, clip_patches)
 
-    shard = net.widen(qkv_weight)
-    lines = lines_of(net.me, [net.widen(values) for values in small])
-    first = Gather(net, jnp.concatenate([shard, lines, jnp.zeros_like(lines)], 1))
+    joined, _ = prepare(me_ref, net.widen(qkv_weight), [net.widen(values) for values in small])
+    first = Gather(net, joined)
     middle_shard = net.widen(jnp.concatenate([out_weight, up_weight], 1))
-    final_shard = net.widen(down_weight)
     cosine, sine = rotary_tables(positions_of(clip_frames[0], clip_patches[0]))
 
     def copy_of(shard):
@@ -1124,108 +1274,108 @@
 
         return put
 
-    made = advance([first], extra=copy_of(middle_shard))
+    made, _ = advance([first], extra=copy_of(middle_shard))
     middle = Gather(net, made[0])
-    made = advance([first])
-    made = advance([first, middle])
-    made = advance([middle], after=first.arrivals(), extra=copy_of(final_shard))
-    final = Gather(net, made[0])
-    normed_kept, normed_sent, qkv, table = project(me_ref, tokens, cosine, sine, first.pieces, after=made)
-    made = advance([middle, final], after=[qkv])
-    attended = attend(*clips, qkv, 0, QUADS // 2, after=made)
-    made = advance([final], after=[*attended, *middle.arrivals()])
+    advance([first], after=[middle.held[0][2]])
+    first.finish()
+    made, token = advance([middle], after=first.arrivals(), extra=copy_of(down_weight))
+    final = lax.all_gather(made[0], AXES, axis=0, tiled=True)
+    (normed_kept, normed_sent, qkv, table), token = project(
+        me_ref, tokens, cosine, sine, first.pieces, after=[token]
+    )
     normed_other = net.swap(normed_sent, 1)
-    mixed, log_totals = attend(*clips, qkv, QUADS // 2, QUADS // 2, attended, after=made)
-    made = advance([final], after=[mixed])
-    resid, normed_two, two_kept, two_sent, mixed_kept, mixed_sent = branch(
-        me_ref, mixed, tokens, table, middle.pieces, after=made
+    _, token = advance([middle], after=[token])
+    (mixed, log_totals), token = attend(*clips, qkv, after=[token])
+    token = middle.finish([token])
+    cotangent_other = net.swap(cotangent, 1)
+    (resid, normed_two, two_kept, two_sent, mixed_kept, mixed_sent), token = branch(
+        me_ref, mixed, tokens, table, [piece for piece in middle.pieces if piece[0] == 0], after=[token]
     )
     two_other, mixed_other = net.swap(two_sent, 1), net.swap(mixed_sent, 1)
-    cotangent_other = net.swap(cotangent, 1)
-    activ, slope, activ_kept, activ_sent = up(
-        me_ref, normed_two, table, middle.pieces, after=[*final.arrivals(), normed_other]
-    )
+    (activ, slope, activ_sent), token = up(me_ref, normed_two, table, middle.pieces, after=[token])
     activ_other = net.swap(activ_sent, 1)
-    output, grad_pre, grad_up_bias = down(
-        me_ref,
-        activ,
-        slope,
-        cotangent,
-        resid,
-        table,
-        final.pieces,
-        after=[activ_kept, two_other, mixed_other, cotangent_other],
-    )
+    (grad_pre, grad_up_bias), token = pre(slope, cotangent, final, after=[token])
     grad_pre_other = net.swap(grad_pre, 1)
-    *made, grad_down_bias = outer_rows(
-        me_ref, activ_kept, activ_other, cotangent, cotangent_other, after=[grad_pre]
-    )
-    moving_down = Scatter(net, by_side(made))
-    grad_resid, grad_branch, grad_mixed, grad_gain_two, grad_shift_two, grad_out_bias = branch_back(
-        me_ref, grad_pre, resid, cotangent, table, middle.pieces, after=[*made, grad_pre_other]
+    (*sides, grad_down_bias), token = outer_rows(
+        me_ref, activ, activ_other, cotangent, cotangent_other, after=[token]
+    )
+    moving_down = Scatter(net, by_side(sides))
+    (grad_resid, grad_branch, grad_mixed, grad_gain_two, grad_shift_two, grad_out_bias), token = branch_back(
+        me_ref, grad_pre, resid, cotangent, table, middle.pieces, after=[token]
     )
     grad_branch_other = net.swap(grad_branch, 1)
-    made = advance([moving_down], after=[grad_branch])
-    *made, _ = outer(
+    _, token = advance([moving_down], after=[token])
+    (*sides, _), token = outer(
         [(mixed_kept, mixed_other, grad_branch, grad_branch_other), (two_kept, two_other, grad_pre, grad_pre_other)],
         TILE,
-        after=made,
-    )
-    moving_up = Scatter(net, by_side(made))
+        after=[token],
+    )
+    moving_up = Scatter(net, by_side(sides), (D, FF))
     parts, others, grad_qkv_bias, moving_qkv = [], [], [], []
 
-    def back(quad, after):
-        parts.append(attend_back(*clips, qkv, mixed, grad_mixed, log_totals, cosine, sine, quad, 1, after=after))
-        others.append(net.swap(parts[-1], 1))
-        return [parts[-1]]
-
-    def weigh(quads, after):
+    def back(quad, token):
+        part, token = attend_back(
+            *clips, qkv, mixed, grad_mixed, log_totals, cosine, sine, quad, 1, after=[token]
+        )
+        parts.append(part)
+        others.append(net.swap(part, 1))
+        return token
+
+    def weigh(quads, token):
         sets = [(normed_kept, normed_other, parts[quad], others[quad]) for quad in quads]
-        *made, bias = outer(sets, 3 * QUAD // 2, after=after)
+        (*sides, bias), token = outer(sets, QUAD, after=[token])
         grad_qkv_bias.append(bias)
-        moving_qkv.append(Scatter(net, by_side(made)))
-        return made
-
-    made = back(0, made)
-    made = advance([moving_down], after=made)
-    made = back(1, made)
-    made = advance([moving_down, moving_up], after=made)
-    made = weigh([0, 1], made)
-    made = back(2, made)
-    made = advance([moving_up, moving_qkv[0]], after=[*made, moving_down.result])
-    made = back(3, made)
-    made = advance([moving_up, moving_qkv[0]], after=made)
-    made = weigh([2, 3], made)
-    grad_tokens, grad_gain_one, grad_shift_one = tokens_back(
-        me_ref, parts, tokens, grad_resid, table, first.pieces, after=made
-    )
-
-    def by_part(parts):
-        whole = jnp.concatenate(parts, 1)
-        return whole.reshape(-1, QUADS, 3, QUAD).transpose(0, 2, 1, 3).reshape(-1, 3 * D)
-
-    grads = [by_part(grad_qkv_bias), grad_out_bias, grad_up_bias, grad_down_bias]
-    grads += [grad_gain_one, grad_shift_one, grad_gain_two, grad_shift_two]
-    total = Sum(net, jnp.pad(jnp.concatenate(grads, 1).reshape(-1, D), ((0, TABLE - 13), (0, 0))))
-    made = advance([moving_qkv[1], moving_qkv[0], total], after=[grad_tokens])
-    made = advance([moving_qkv[1], total], after=made[:1])
-    made = advance([moving_qkv[1], total], after=made[:1])
-    summed = total.finish().reshape(-1)
-    own = [
-        lax.dynamic_slice_in_dim(summed, end - size + net.number * (size // count), size // count)
-        for size, end in zip(sizes, ends)
-    ]
-    out_up = moving_up.result
+        moving_qkv.append(Scatter(net, by_side(sides)))
+        return token
+
+    token = back(0, token)
+    _, token = advance([moving_down], after=[token])
+    token = back(1, token)
+    _, token = advance([moving_up], after=[token])
+    token = weigh([0, 1], token)
+    _, token = advance([moving_up], after=[token])
+    token = back(2, token)
+    _, token = advance([moving_down, moving_qkv[0]], after=[token])
+    token = back(3, token)
+    _, token = advance([moving_qkv[0]], after=[token])
+    token = weigh([2, 3], token)
+    (grad_tokens, grad_table), token = tokens_back(
+        me_ref,
+        parts,
+        grad_qkv_bias,
+        tokens,
+        grad_resid,
+        table,
+        (grad_out_bias, grad_up_bias, grad_down_bias, grad_gain_two, grad_shift_two),
+        first.pieces,
+        after=[token],
+    )
+    total = Sum(net, grad_table)
+    def rows_of(part, token, before=()):
+        return output_rows(activ, resid, table, final, part, 4, before, after=[token])
+
+    _, token = advance([moving_qkv[1], moving_up], after=[token, *moving_qkv[0].held[1:]])
+    output, token = rows_of(0, token)
+    _, token = advance([total], after=[token])
+    output, token = rows_of(1, token, [output])
+    _, token = advance([moving_qkv[1], total], after=[token])
+    output, token = rows_of(2, token, [output])
+    _, token = advance([total], after=[token])
+    output, token = rows_of(3, token, [output])
+    (grad_qkv_weight, *own), _ = finish(
+        net.number.reshape(1), (*moving_qkv[0].held, *moving_qkv[1].held), total.finish(), sizes, count, [token]
+    )
+    own = [values.reshape(-1) for values in own]
     return (
         output,
         grad_tokens,
-        by_part([each.result for each in moving_qkv]),
+        net.narrow(grad_qkv_weight),
         own[0],
-        out_up[:, :D],
+        moving_up.result[0],
         own[1],
-        out_up[:, D:],
+        moving_up.result[1],
         own[2],
-        moving_down.result,
+        moving_down.result[0],
         own[3],
         own[4],
         own[5],

time: 571 us -> 469 us (0.82)
  Pallas kernels: 344 us -> 301 us
  waiting for transfers between devices: 111 us -> 71.7 us
  local copies, waits for them, and re-layouts: 27.8 us -> 8.47 us
  between operations: 1.49 us -> 15.1 us
  other arithmetic: 13.1 us -> 3.43 us
    pallas_call x31 -> x36, Pallas kernels: 344 us -> 301 us  [pallas(): pl.pallas_call(body, in_specs=list(in_specs) + [ANY] * len(after), out_sp...]
    ppermute x70 -> x67, waiting for transfers between devices: 111 us -> 71.7 us  [permute(): lax.ppermute(value, AXES, [(number, number ^ mask) for number in range(se...]
    unnamed x102, local copies, waits for them, and re-layouts: 15.3 us -> 8.45 us
    dynamic_update_slice x8 -> x0, local copies, waits for them, and re-layouts: 6.69 us -> none  [lines_of(): flat = lax.dynamic_update_slice(flat, values, (place,))]
    ppermute x70 -> x67, starting transfers between devices: 64.7 us -> 60 us  [permute(): lax.ppermute(value, AXES, [(number, number ^ mask) for number in range(se...]
  transfers between devices with their start and end apart: 70 -> 68, of which waited for: 21 -> 14; matrix products, arithmetic and copies ran while one was open for 4% -> 1% of each run, Pallas kernels for 60% -> 64%
where the time goes in v2:
time: 469 us; the launch traced here: 460 us
  Pallas kernels  301 us (64%)
  waiting for transfers between devices  71.7 us (15%)
  starting transfers between devices  60 us (13%)
  between operations  15.1 us (3%)
  local copies, waits for them, and re-layouts  8.47 us (2%)
    pallas_call x36, Pallas kernels, pallas(): pl.pallas_call(body, in_specs=list(in_specs) + [ANY] * len(after), out_sp...  301 us
    ppermute x67, waiting for transfers between devices, permute(): lax.ppermute(value, AXES, [(number, number ^ mask) for number in range(se...  71.7 us
    ppermute x67, starting transfers between devices, permute(): lax.ppermute(value, AXES, [(number, number ^ mask) for number in range(se...  60 us
  transfers between devices with their start and end apart: 68, of which 14 were waited for; matrix products, arithmetic and copies ran while one was open for 1% of the time, Pallas kernels for 64%

profile of v2, /device:TPU:0, one launch (start us, length us, event | category | flops | bytes accessed | tf_op | source)
XLA Modules:
  0.0 459.8 jit_solution(6920206510595175094)
XLA Ops:
  20.2 11.9 %collective-permute-done.1.refs_3_ = bf16[32,3328]{1,0:T(8,128)(2,1)S(1)} collective-permute-done((bf16[32,3328]{1,0:T(8,128)(2,1)S(1)}, bf16[32,3328]{1,0:T(8,128)(2,1)S(1)}, u32[]{:S(2)}, u32[]{:S(2)}) %collective-permute-start.1) | collective-permute-done | bytes 213024 | tf_op jit(solution)/shard_map/ppermute | solution.py:153
  36.0 15.5 %collective-permute-done.5.refs_4_.refs_3_ = bf16[32,5120]{1,0:T(8,128)(2,1)S(1)} collective-permute-done((bf16[32,5120]{1,0:T(8,128)(2,1)S(1)}, bf16[32,5120]{1,0:T(8,128)(2,1)S(1)}, u32[]{:S(2)}, u32[]{:S(2)}) %collective-permute-start.5) | collective-permute-done | bytes 327712 | tf_op jit(solution)/shard_map/ppermute | solution.py:153
  61.5 7.2 %collective-permute-done.13.refs_4_ = bf16[32,5120]{1,0:T(8,128)(2,1)S(1)} collective-permute-done((bf16[32,5120]{1,0:T(8,128)(2,1)S(1)}, bf16[32,5120]{1,0:T(8,128)(2,1)S(1)}, u32[]{:S(2)}, u32[]{:S(2)}) %collective-permute-start.13) | collective-permute-done | bytes 327712 | tf_op jit(solution)/shard_map/ppermute | solution.py:153
  68.7 7.0 %collective-permute-done.7.refs_5_.refs_6_.refs_17_ = bf16[256,1664]{1,0:T(8,128)(2,1)} collective-permute-done((bf16[256,1664]{1,0:T(8,128)(2,1)S(1)}, bf16[256,1664]{1,0:T(8,128)(2,1)}, u32[]{:S(2)}, u32[]{:S(2)}) %collective-permute-start.7) | collective-permute-done | bytes 852000 | tf_op jit(solution)/shard_map/ppermute | solution.py:153
  79.8 17.5 %project.1 = (bf16[512,1024]{1,0:T(8,128)(2,1)}, bf16[512,1024]{1,0:T(8,128)(2,1)}, bf16[1024,3072]{1,0:T(8,128)(2,1)}, f32[16,1024]{1,0:T(8,128)S(1)}, f32[8,128]{1,0:T(8,128)S(1)}) custom-call(s32[1]{0:T(128)} %bitcast.refs_0_, bf16[1024,1024]{1,0:T(8,128)(2,1)} %refs_7_.1, f32[1024,128]{1,0:T(8,128)S(1)} %get-tuple-element.314.refs_2_.refs_8_, ...), custom_call_target="tpu_custom_call" | custom-call | flops 46000001024 | tf_op jit(solution)/shard_map/project/pallas_call | solution.py:77
  101.5 25.6 %attend.1 = (bf16[1024,1024]{1,0:T(8,128)(2,1)}, f32[2,8,1024]{2,1,0:T(8,128)}, f32[8,128]{1,0:T(8,128)S(1)}) custom-call(s32[1,4]{1,0:T(1,128)S(1)} %copy-done, s32[1,4]{1,0:T(1,128)S(1)} %copy-done.2, bf16[1024,3072]{1,0:T(8,128)(2,1)} %get-tuple-element.165.refs_2_.refs_3_.refs_4_, bf16[1024,3072]{1,0:T(8,128)(2,1)} %get-tuple-element.165.refs_2_.refs_3_.refs_4_, ...), custom_call_target="tpu_custom_call" | custom-call | flops 74750001152 | tf_op jit(solution)/shard_map/attend/pallas_call | solution.py:77
  127.1 8.7 %collective-permute-done.18.refs_1_.refs_9_.refs_11_ = bf16[256,2560]{1,0:T(8,128)(2,1)S(1)} collective-permute-done((bf16[256,2560]{1,0:T(8,128)(2,1)}, bf16[256,2560]{1,0:T(8,128)(2,1)S(1)}, u32[]{:S(2)}, u32[]{:S(2)}) %collective-permute-start.18) | collective-permute-done | bytes 1310752 | tf_op jit(solution)/shard_map/ppermute | solution.py:153
  145.2 12.1 %branch.1 = (f32[1024,1024]{1,0:T(8,128)}, bf16[1024,1024]{1,0:T(8,128)(2,1)S(1)}, bf16[512,1024]{1,0:T(8,128)(2,1)}, bf16[512,1024]{1,0:T(8,128)(2,1)S(1)}, bf1...) custom-call(s32[1]{0:T(128)} %bitcast.refs_0_, ...), custom_call_target="tpu_custom_call" | custom-call | flops 34500001792 | tf_op jit(solution)/shard_map/branch/pallas_call | solution.py:77
  158.6 29.5 %up.1 = (bf16[1024,4096]{1,0:T(8,128)(2,1)}, bf16[1024,4096]{1,0:T(8,128)(2,1)}, bf16[1024,2048]{1,0:T(8,128)(2,1)}, f32[8,128]{1,0:T(8,128)S(1)}) custom-call(s32[1]{0:T(128)} %bitcast.refs_0_, bf16[1024,1024]{1,0:T(8,128)(2,1)S(1)} %get-tuple-element.177.refs_1_, f32[16,1024]{1,0:T(8,128)S(1)} %get-tuple-element.171.refs_3_.refs_2_.refs_4_.refs_9_, ...), custom_call_target="tpu_custom_call" | custom-call | flops 100624998400 | tf_op jit(solution)/shard_map/up/pallas_call | solution.py:77
  188.3 16.8 %pre.1 = (bf16[1024,4096]{1,0:T(8,128)(2,1)}, f32[1,4096]{1,0:T(1,128)}, f32[8,128]{1,0:T(8,128)S(1)}) custom-call(bf16[1024,4096]{1,0:T(8,128)(2,1)} %get-tuple-element.185.refs_0_, bf16[1024,1024]{1,0:T(8,128)(2,1)} %refs_3_.3, bf16[4096,1024]{1,0:T(8,128)(2,1)} %all-gather.2.cloned.1.call-done.refs_2_.refs_3_, f32[8,128]{1,0:T(8,128)S(1)} %get-tuple-element.186.refs_3_), custom_call_target="tpu_custom_call" | custom-call | flops 184000004096 | tf_op jit(solution)/shard_map/pre/pallas_call | solution.py:77
  205.1 17.5 %outer_rows.1 = (f32[1024,512]{1,0:T(8,128)S(1)}, bf16[1024,512]{1,0:T(8,128)(2,1)}, f32[1024,512]{1,0:T(8,128)S(1)}, bf16[1024,512]{1,0:T(8,128)(2,1)}, f32[1,1024]{1,0:T(1,128)}, /*index=5*/f32[8,128]{1,0:T(8,128)S(1)}) custom-call(s32[1]{0:T(128)} %bitcast.refs_0_, bf16[1024,4096]{1,0:T(8,128)(2,1)} %get-tuple-element.180.refs_1_.refs_0_, ...), custom_call_target="tpu_custom_call" | custom-call | flops 184000004096 | tf_op jit(solution)/shard_map/outer_rows/pallas_call | solution.py:77
  225.9 20.9 %branch_back.1 = (f32[1024,1024]{1,0:T(8,128)}, bf16[1024,1024]{1,0:T(8,128)(2,1)S(1)}, bf16[1024,1024]{1,0:T(8,128)(2,1)S(1)}, f32[1,1024]{1,0:T(1,128)}, f32[1...) custom-call(s32[1]{0:T(128)} %bitcast.refs_0_, bf16[1024,4096]{1,0:T(8,128)(2,1)} %get-tuple-element.187.refs_1_.refs_6_, ...), custom_call_target="tpu_custom_call" | custom-call | flops 241499996160 | tf_op jit(solution)/shard_map/branch_back/pallas_call | solution.py:77
  256.6 20.4 %outer.3 = (f32[256,2560]{1,0:T(8,128)S(1)}, bf16[256,2560]{1,0:T(8,128)(2,1)}, f32[256,2560]{1,0:T(8,128)S(1)}, bf16[256,2560]{1,0:T(8,128)(2,1)}, f32[1,5120]{1,0:T(1,128)}, /*index=5*/f32[8,128]{1,0:T(8,128)S(1)}) custom-call(bf16[512,1024]{1,0:T(8,128)(2,1)} %get-tuple-element.193.refs_0_, bf16[512,1024]{1,0:T(8,128)(2,1)} %collective-permute-done.25.refs_1_, ...), custom_call_target="tpu_custom_call" | custom-call | flops 224509657088 | tf_op jit(solution)/shard_map/outer/pallas_call | solution.py:77
  279.1 13.6 %attend_back.4 = (bf16[1024,768]{1,0:T(8,128)(2,1)S(1)}, f32[8,128]{1,0:T(8,128)S(1)}) custom-call(s32[1,4]{1,0:T(1,128)S(1)} %copy-done.1, s32[1,4]{1,0:T(1,128)S(1)} %copy-done.3, bf16[1024,3072]{1,0:T(8,128)(2,1)} %get-tuple-element.165.refs_2_.refs_3_.refs_4_, bf16[1024,3072]{1,0:T(8,128)(2,1)} %get-tuple-element.165.refs_2_.refs_3_.refs_4_, ...), custom_call_target="tpu_custom_call" | custom-call | flops 172499992576 | tf_op jit(solution)/shard_map/attend_back/pallas_call | solution.py:77
  295.8 13.6 %attend_back.5 = (bf16[1024,768]{1,0:T(8,128)(2,1)S(1)}, f32[8,128]{1,0:T(8,128)S(1)}) custom-call(s32[1,4]{1,0:T(1,128)S(1)} %copy-done.1, s32[1,4]{1,0:T(1,128)S(1)} %copy-done.3, bf16[1024,3072]{1,0:T(8,128)(2,1)} %get-tuple-element.165.refs_2_.refs_3_.refs_4_, bf16[1024,3072]{1,0:T(8,128)(2,1)} %get-tuple-element.165.refs_2_.refs_3_.refs_4_, ...), custom_call_target="tpu_custom_call" | custom-call | flops 172499992576 | tf_op jit(solution)/shard_map/attend_back/pallas_call | solution.py:77
  318.6 9.4 %outer.4 = (f32[256,768]{1,0:T(8,128)S(1)}, bf16[256,768]{1,0:T(8,128)(2,1)}, f32[256,768]{1,0:T(8,128)S(1)}, bf16[256,768]{1,0:T(8,128)(2,1)}, f32[1,1536]{1,0:T(1,128)}, /*index=5*/f32[8,128]{1,0:T(8,128)S(1)}) custom-call(bf16[512,1024]{1,0:T(8,128)(2,1)} %get-tuple-element.183.refs_0_, bf16[512,1024]{1,0:T(8,128)(2,1)} %collective-permute-done.22.refs_1_, ...), custom_call_target="tpu_custom_call" | custom-call | flops 67352895488 | tf_op jit(solution)/shard_map/outer/pallas_call | solution.py:77
  336.1 13.4 %attend_back.6 = (bf16[1024,768]{1,0:T(8,128)(2,1)S(1)}, f32[8,128]{1,0:T(8,128)S(1)}) custom-call(s32[1,4]{1,0:T(1,128)S(1)} %copy-done.1, s32[1,4]{1,0:T(1,128)S(1)} %copy-done.3, bf16[1024,3072]{1,0:T(8,128)(2,1)} %get-tuple-element.165.refs_2_.refs_3_.refs_4_, bf16[1024,3072]{1,0:T(8,128)(2,1)} %get-tuple-element.165.refs_2_.refs_3_.refs_4_, ...), custom_call_target="tpu_custom_call" | custom-call | flops 172499992576 | tf_op jit(solution)/shard_map/attend_back/pallas_call | solution.py:77
  355.7 13.6 %attend_back.7 = (bf16[1024,768]{1,0:T(8,128)(2,1)S(1)}, f32[8,128]{1,0:T(8,128)S(1)}) custom-call(s32[1,4]{1,0:T(1,128)S(1)} %copy-done.1, s32[1,4]{1,0:T(1,128)S(1)} %copy-done.3, bf16[1024,3072]{1,0:T(8,128)(2,1)} %get-tuple-element.165.refs_2_.refs_3_.refs_4_, bf16[1024,3072]{1,0:T(8,128)(2,1)} %get-tuple-element.165.refs_2_.refs_3_.refs_4_, ...), custom_call_target="tpu_custom_call" | custom-call | flops 172499992576 | tf_op jit(solution)/shard_map/attend_back/pallas_call | solution.py:77
  377.5 10.0 %outer.5 = (f32[256,768]{1,0:T(8,128)S(1)}, bf16[256,768]{1,0:T(8,128)(2,1)}, f32[256,768]{1,0:T(8,128)S(1)}, bf16[256,768]{1,0:T(8,128)(2,1)}, f32[1,1536]{1,0:T(1,128)}, /*index=5*/f32[8,128]{1,0:T(8,128)S(1)}) custom-call(bf16[512,1024]{1,0:T(8,128)(2,1)} %get-tuple-element.183.refs_0_, bf16[512,1024]{1,0:T(8,128)(2,1)} %collective-permute-done.22.refs_1_, ...), custom_call_target="tpu_custom_call" | custom-call | flops 67352895488 | tf_op jit(solution)/shard_map/outer/pallas_call | solution.py:77
  392.3 14.1 %tokens_back.1 = (bf16[1024,1024]{1,0:T(8,128)(2,1)}, f32[16,1024]{1,0:T(8,128)}, f32[8,128]{1,0:T(8,128)S(1)}) custom-call(s32[1]{0:T(128)} %bitcast.refs_0_, bf16[1024,768]{1,0:T(8,128)(2,1)S(1)} %copy-done.6, bf16[1024,768]{1,0:T(8,128)(2,1)S(1)} %copy-done.8, bf16[1024,768]{1,0:T(8,128)(2,1)S(1)} %copy-done.10, bf16[1024,768]{1,0:T(8,128)(2,1)S(1)} %copy-done.12, ...), custom_call_target="tpu_custom_call" | custom-call | flops 172499992576 | tf_op jit(solution)/shard_map/tokens_back/pallas_call | solution.py:77
  410.7 7.1 %output.4 = (bf16[1024,1024]{1,0:T(8,128)(2,1)}, f32[8,128]{1,0:T(8,128)S(1)}) custom-call(bf16[1024,4096]{1,0:T(8,128)(2,1)} %get-tuple-element.180.refs_1_.refs_0_, f32[1024,1024]{1,0:T(8,128)} %get-tuple-element.181.refs_2_.refs_1_, f32[16,1024]{1,0:T(8,128)S(1)} %get-tuple-element.171.refs_3_.refs_2_.refs_4_.refs_9_, ...), custom_call_target="tpu_custom_call" | custom-call | flops 46000001024 | tf_op jit(solution)/shard_map/output/pallas_call | solution.py:77
  419.5 7.1 %output.5 = (bf16[1024,1024]{1,0:T(8,128)(2,1)}, f32[8,128]{1,0:T(8,128)S(1)}) custom-call(bf16[1024,4096]{1,0:T(8,128)(2,1)} %get-tuple-element.180.refs_1_.refs_0_, f32[1024,1024]{1,0:T(8,128)} %get-tuple-element.181.refs_2_.refs_1_, f32[16,1024]{1,0:T(8,128)S(1)} %get-tuple-element.171.refs_3_.refs_2_.refs_4_.refs_9_, ...), custom_call_target="tpu_custom_call", output_to_operand_aliasing={{0}: (4, {})} | custom-call | flops 46000001024 | tf_op jit(solution)/shard_map/output/pallas_call | solution.py:77
  432.1 7.1 %output.6 = (bf16[1024,1024]{1,0:T(8,128)(2,1)}, f32[8,128]{1,0:T(8,128)S(1)}) custom-call(bf16[1024,4096]{1,0:T(8,128)(2,1)} %get-tuple-element.180.refs_1_.refs_0_, f32[1024,1024]{1,0:T(8,128)} %get-tuple-element.181.refs_2_.refs_1_, f32[16,1024]{1,0:T(8,128)S(1)} %get-tuple-element.171.refs_3_.refs_2_.refs_4_.refs_9_, ...), custom_call_target="tpu_custom_call", output_to_operand_aliasing={{0}: (4, {})} | custom-call | flops 46000001024 | tf_op jit(solution)/shard_map/output/pallas_call | solution.py:77
  443.6 7.1 %output.7 = (bf16[1024,1024]{1,0:T(8,128)(2,1)}, f32[8,128]{1,0:T(8,128)S(1)}) custom-call(bf16[1024,4096]{1,0:T(8,128)(2,1)} %get-tuple-element.180.refs_1_.refs_0_, f32[1024,1024]{1,0:T(8,128)} %get-tuple-element.181.refs_2_.refs_1_, f32[16,1024]{1,0:T(8,128)S(1)} %get-tuple-element.171.refs_3_.refs_2_.refs_4_.refs_9_, ...), custom_call_target="tpu_custom_call", output_to_operand_aliasing={{0}: (4, {})} | custom-call | flops 46000001024 | tf_op jit(solution)/shard_map/output/pallas_call | solution.py:77
  (260 shorter events, 117.8 us)
Async XLA Ops:
  7.2 181.1 %all-gather.2.cloned.1.call-start = ((), (), s32[]{:S(2)}) async-start(), calls=%async_computation | async-start | bytes 8650752 | tf_op jit(solution)/shard_map/all_gather | solution.py:1282
  54.7 21.0 %collective-permute-start.7 = (bf16[256,1664]{1,0:T(8,128)(2,1)S(1)}, bf16[256,1664]{1,0:T(8,128)(2,1)}, u32[]{:S(2)}, u32[]{:S(2)}) collective-permute-start(bf16[256,1664]{1,0:T(8,128)(2,1)S(1)} %get-tuple-element.162.refs_4_.refs_15_), channel_id=1, source_target_pairs={{0,8},{1,9},{2,10},{3,11},{4,12},{5,13},{6,14},{7,15},{8,0},{9,1},... | collective-permute-start | bytes 2555912 | tf_op jit(solution)/shard_map/ppermute | solution.py:153
  55.3 20.7 %collective-permute-start.10 = (bf16[256,1664]{1,0:T(8,128)(2,1)S(1)}, bf16[256,1664]{1,0:T(8,128)(2,1)}, u32[]{:S(2)}, u32[]{:S(2)}) collective-permute-start(bf16[256,1664]{1,0:T(8,128)(2,1)S(1)} %get-tuple-element.163.refs_8_.refs_19_), channel_id=1, source_target_pairs={{0,16},{1,17},{2,18},{3,19},{4,20},{5,21},{6,22},{7,23},{8,24},{9,... | collective-permute-start | bytes 2555912 | tf_op jit(solution)/shard_map/ppermute | solution.py:153
  77.9 19.4 %collective-permute-start.14 = (bf16[128,2560]{1,0:T(8,128)(2,1)S(1)}, bf16[128,2560]{1,0:T(8,128)(2,1)S(1)}, u32[]{:S(2)}, u32[]{:S(2)}) collective-permute-start(bf16[128,2560]{1,0:T(8,128)(2,1)S(1)} %get-tuple-element.166.refs_0_), channel_id=1, source_target_pairs={{0,16},{1,17},{2,18},{3,19},{4,20},{5,21},{6,22},{7,23},{8,24},{9,... | collective-permute-start | bytes 1966088 | tf_op jit(solution)/shard_map/ppermute | solution.py:153
  98.6 40.6 %collective-permute-start.17 = (bf16[256,2560]{1,0:T(8,128)(2,1)S(1)}, bf16[256,2560]{1,0:T(8,128)(2,1)S(1)}, u32[]{:S(2)}, u32[]{:S(2)}) collective-permute-start(bf16[256,2560]{1,0:T(8,128)(2,1)S(1)} %get-tuple-element.172.refs_4_.refs_3_.refs_5_), channel_id=1, source_target_pairs={{0,8},{1,9},{2,10},{3,11},{4,12},{5,13},{6,14},{7,15},{8,0},{9,1},... | collective-permute-start | bytes 3932168 | tf_op jit(solution)/shard_map/ppermute | solution.py:153
  99.9 43.0 %collective-permute-start.16 = (bf16[256,2560]{1,0:T(8,128)(2,1)S(1)}, bf16[256,2560]{1,0:T(8,128)(2,1)}, u32[]{:S(2)}, u32[]{:S(2)}) collective-permute-start(bf16[256,2560]{1,0:T(8,128)(2,1)S(1)} %get-tuple-element.172.refs_4_.refs_3_.refs_5_), channel_id=1, source_target_pairs={{0,1},{1,0},{2,3},{3,2},{4,5},{5,4},{6,7},{7,6},{8,9},{9,8},{10,11... | collective-permute-start | bytes 3932168 | tf_op jit(solution)/shard_map/ppermute | solution.py:153
  99.9 35.8 %collective-permute-start.18 = (bf16[256,2560]{1,0:T(8,128)(2,1)}, bf16[256,2560]{1,0:T(8,128)(2,1)S(1)}, u32[]{:S(2)}, u32[]{:S(2)}) collective-permute-start(bf16[256,2560]{1,0:T(8,128)(2,1)} %get-tuple-element.173.refs_7_.refs_9_), channel_id=1, source_target_pairs={{0,16},{1,17},{2,18},{3,19},{4,20},{5,21},{6,22},{7,23},{8,24},{9,... | collective-permute-start | bytes 3932168 | tf_op jit(solution)/shard_map/ppermute | solution.py:153
  141.9 63.2 %collective-permute-start.24 = (bf16[1024,1024]{1,0:T(8,128)(2,1)}, bf16[1024,1024]{1,0:T(8,128)(2,1)}, u32[]{:S(2)}, u32[]{:S(2)}) collective-permute-start(bf16[1024,1024]{1,0:T(8,128)(2,1)} %refs_3_.3), channel_id=1, source_target_pairs={{0,1},{1,0},{2,3},{3,2},{4,5},{5,4},{6,7},{7,6},{8,9},{9,8},{10,11... | collective-permute-start | bytes 6291464 | tf_op jit(solution)/shard_map/ppermute | solution.py:153
  142.4 169.9 %collective-permute-start.22 = (bf16[512,1024]{1,0:T(8,128)(2,1)}, bf16[512,1024]{1,0:T(8,128)(2,1)}, u32[]{:S(2)}, u32[]{:S(2)}) collective-permute-start(bf16[512,1024]{1,0:T(8,128)(2,1)} %get-tuple-element.184), channel_id=1, source_target_pairs={{0,1},{1,0},{2,3},{3,2},{4,5},{5,4},{6,7},{7,6},{8,9},{9,8},{10,11... | collective-permute-start | bytes 3145736 | tf_op jit(solution)/shard_map/ppermute | solution.py:153
  157.4 95.4 %collective-permute-start.25 = (bf16[512,1024]{1,0:T(8,128)(2,1)}, bf16[512,1024]{1,0:T(8,128)(2,1)}, u32[]{:S(2)}, u32[]{:S(2)}) collective-permute-start(bf16[512,1024]{1,0:T(8,128)(2,1)} %get-tuple-element.194), channel_id=1, source_target_pairs={{0,1},{1,0},{2,3},{3,2},{4,5},{5,4},{6,7},{7,6},{8,9},{9,8},{10,11... | collective-permute-start | bytes 3145736 | tf_op jit(solution)/shard_map/ppermute | solution.py:153
  222.6 25.8 %collective-permute-start.29 = (bf16[1024,512]{1,0:T(8,128)(2,1)}, bf16[1024,512]{1,0:T(8,128)(2,1)}, u32[]{:S(2)}, u32[]{:S(2)}) collective-permute-start(bf16[1024,512]{1,0:T(8,128)(2,1)} %get-tuple-element.199), channel_id=1, source_target_pairs={{0,16},{1,17},{2,18},{3,19},{4,20},{5,21},{6,22},{7,23},{8,24},{9,... | collective-permute-start | bytes 3145736 | tf_op jit(solution)/shard_map/ppermute | solution.py:153
  224.1 25.5 %collective-permute-start.30 = (bf16[1024,512]{1,0:T(8,128)(2,1)}, bf16[1024,512]{1,0:T(8,128)(2,1)}, u32[]{:S(2)}, u32[]{:S(2)}) collective-permute-start(bf16[1024,512]{1,0:T(8,128)(2,1)} %get-tuple-element.201), channel_id=1, source_target_pairs={{0,8},{1,9},{2,10},{3,11},{4,12},{5,13},{6,14},{7,15},{8,0},{9,1},... | collective-permute-start | bytes 3145736 | tf_op jit(solution)/shard_map/ppermute | solution.py:153
  225.9 29.4 %collective-permute-start.28 = (bf16[1024,4096]{1,0:T(8,128)(2,1)}, bf16[1024,4096]{1,0:T(8,128)(2,1)}, u32[]{:S(2)}, u32[]{:S(2)}) collective-permute-start(bf16[1024,4096]{1,0:T(8,128)(2,1)} %get-tuple-element.187.refs_1_.refs_6_), channel_id=1, source_target_pairs={{0,1},{1,0},{2,3},{3,2},{4,5},{5,4},{6,7},{7,6},{8,9},{9,8},{10,11... | collective-permute-start | bytes 25165832 | tf_op jit(solution)/shard_map/ppermute | solution.py:153
  252.7 40.0 %collective-permute-start.33 = (bf16[512,512]{1,0:T(8,128)(2,1)}, bf16[512,512]{1,0:T(8,128)(2,1)}, u32[]{:S(2)}, u32[]{:S(2)}) collective-permute-start(bf16[512,512]{1,0:T(8,128)(2,1)} %get-tuple-element.209), channel_id=1, source_target_pairs={{0,8},{1,9},{2,10},{3,11},{4,12},{5,13},{6,14},{7,15},{8,0},{9,1},... | collective-permute-start | bytes 1572872 | tf_op jit(solution)/shard_map/ppermute | solution.py:153
  254.5 38.2 %collective-permute-start.34 = (bf16[512,512]{1,0:T(8,128)(2,1)}, bf16[512,512]{1,0:T(8,128)(2,1)}, u32[]{:S(2)}, u32[]{:S(2)}) collective-permute-start(bf16[512,512]{1,0:T(8,128)(2,1)} %get-tuple-element.211), channel_id=1, source_target_pairs={{0,16},{1,17},{2,18},{3,19},{4,20},{5,21},{6,22},{7,23},{8,24},{9,... | collective-permute-start | bytes 1572872 | tf_op jit(solution)/shard_map/ppermute | solution.py:153
  277.0 32.4 %collective-permute-start.31 = (bf16[256,2560]{1,0:T(8,128)(2,1)}, bf16[256,2560]{1,0:T(8,128)(2,1)}, u32[]{:S(2)}, u32[]{:S(2)}) collective-permute-start(bf16[256,2560]{1,0:T(8,128)(2,1)} %get-tuple-element.205), channel_id=1, source_target_pairs={{0,16},{1,17},{2,18},{3,19},{4,20},{5,21},{6,22},{7,23},{8,24},{9,... | collective-permute-start | bytes 3932168 | tf_op jit(solution)/shard_map/ppermute | solution.py:153
  278.3 31.3 %collective-permute-start.32 = (bf16[256,2560]{1,0:T(8,128)(2,1)}, bf16[256,2560]{1,0:T(8,128)(2,1)}, u32[]{:S(2)}, u32[]{:S(2)}) collective-permute-start(bf16[256,2560]{1,0:T(8,128)(2,1)} %get-tuple-element.207), channel_id=1, source_target_pairs={{0,8},{1,9},{2,10},{3,11},{4,12},{5,13},{6,14},{7,15},{8,0},{9,1},... | collective-permute-start | bytes 3932168 | tf_op jit(solution)/shard_map/ppermute | solution.py:153
  295.8 53.8 %collective-permute-start.40 = (bf16[128,1024]{1,0:T(8,128)(2,1)}, bf16[128,1024]{1,0:T(8,128)(2,1)}, u32[]{:S(2)}, u32[]{:S(2)}) collective-permute-start(bf16[128,1024]{1,0:T(8,128)(2,1)} %get-tuple-element.227), channel_id=1, source_target_pairs={{0,2},{1,3},{2,0},{3,1},{4,6},{5,7},{6,4},{7,5},{8,10},{9,11},{10,... | collective-permute-start | bytes 786440 | tf_op jit(solution)/shard_map/ppermute | solution.py:153
  295.8 53.8 %collective-permute-start.41 = (bf16[128,1024]{1,0:T(8,128)(2,1)}, bf16[128,1024]{1,0:T(8,128)(2,1)}, u32[]{:S(2)}, u32[]{:S(2)}) collective-permute-start(bf16[128,1024]{1,0:T(8,128)(2,1)} %get-tuple-element.228), channel_id=1, source_target_pairs={{0,4},{1,5},{2,6},{3,7},{4,0},{5,1},{6,2},{7,3},{8,12},{9,13},{10,... | collective-permute-start | bytes 786440 | tf_op jit(solution)/shard_map/ppermute | solution.py:153
  312.3 38.8 %collective-permute-start.42 = (bf16[128,1024]{1,0:T(8,128)(2,1)}, bf16[128,1024]{1,0:T(8,128)(2,1)}, u32[]{:S(2)}, u32[]{:S(2)}) collective-permute-start(bf16[128,1024]{1,0:T(8,128)(2,1)} %get-tuple-element.229), channel_id=1, source_target_pairs={{0,6},{1,7},{2,4},{3,5},{4,2},{5,3},{6,0},{7,1},{8,14},{9,15},{10,... | collective-permute-start | bytes 786440 | tf_op jit(solution)/shard_map/ppermute | solution.py:153
  349.6 56.8 %collective-permute-start.50 = (bf16[32,5120]{1,0:T(8,128)(2,1)}, bf16[32,5120]{1,0:T(8,128)(2,1)}, u32[]{:S(2)}, u32[]{:S(2)}) collective-permute-start(bf16[32,5120]{1,0:T(8,128)(2,1)} %get-tuple-element.248), channel_id=1, source_target_pairs={{0,2},{1,3},{2,0},{3,1},{4,6},{5,7},{6,4},{7,5},{8,10},{9,11},{10,... | collective-permute-start | bytes 983048 | tf_op jit(solution)/shard_map/ppermute | solution.py:153
  349.7 56.8 %collective-permute-start.51 = (bf16[32,5120]{1,0:T(8,128)(2,1)}, bf16[32,5120]{1,0:T(8,128)(2,1)}, u32[]{:S(2)}, u32[]{:S(2)}) collective-permute-start(bf16[32,5120]{1,0:T(8,128)(2,1)} %get-tuple-element.249), channel_id=1, source_target_pairs={{0,4},{1,5},{2,6},{3,7},{4,0},{5,1},{6,2},{7,3},{8,12},{9,13},{10,... | collective-permute-start | bytes 983048 | tf_op jit(solution)/shard_map/ppermute | solution.py:153
  427.7 23.1 %collective-permute-start.62 = (bf16[32,1536]{1,0:T(8,128)(2,1)S(1)}, bf16[32,1536]{1,0:T(8,128)(2,1)S(1)}, u32[]{:S(2)}, u32[]{:S(2)}) collective-permute-start(bf16[32,1536]{1,0:T(8,128)(2,1)S(1)} %get-tuple-element.286), channel_id=1, source_target_pairs={{0,4},{1,5},{2,6},{3,7},{4,0},{5,1},{6,2},{7,3},{8,12},{9,13},{10,... | collective-permute-start | bytes 294920 | tf_op jit(solution)/shard_map/ppermute | solution.py:153
  430.4 20.3 %collective-permute-start.63 = (bf16[32,1536]{1,0:T(8,128)(2,1)S(1)}, bf16[32,1536]{1,0:T(8,128)(2,1)S(1)}, u32[]{:S(2)}, u32[]{:S(2)}) collective-permute-start(bf16[32,1536]{1,0:T(8,128)(2,1)S(1)} %get-tuple-element.287), channel_id=1, source_target_pairs={{0,6},{1,7},{2,4},{3,5},{4,2},{5,3},{6,0},{7,1},{8,14},{9,15},{10,... | collective-permute-start | bytes 294920 | tf_op jit(solution)/shard_map/ppermute | solution.py:153
  (95 other events, 1127.4 us)
Sparse Core Ops, SparseCore 0:
  78.0 84.7 all-gather.1

commit v3 on v2

--- a/solution.py
+++ b/solution.py
@@ -23,7 +23,9 @@
 LENGTHS_OF_RUNS = (3, 4, 5, 7, 8)
 LANES = 128
 TILE = 512
+WIDE_TILE = 1024
 ROWS = 256
+UP_ROWS = 128
 F32 = jnp.float32
 BF = jnp.bfloat16
 VMEM_BYTES = 28 << 20
@@ -55,7 +57,7 @@
     return [pltpu.with_memory_space_constraint(array, pltpu.HBM) for array in arrays]
 
 
-def pallas(kernel, operands, in_specs, after=(), vmem=VMEM_BYTES, near=(), far_in=(), **kept):
+def pallas(kernel, operands, in_specs, after=(), vmem=VMEM_BYTES, near=(), far_in=(), prefetch=0, **kept):
     given = len(operands)
     shapes, specs = kept.pop("out_shape"), kept.pop("out_specs")
     single = not isinstance(shapes, (list, tuple))
@@ -74,15 +76,33 @@
         refs[outs + len(shapes)][...] = jnp.zeros((8, LANES), F32)
         kernel(*refs[:given], *refs[outs : outs + len(shapes)], *refs[outs + len(shapes) + 1 :])
 
+    places = dict(in_specs=list(in_specs) + [ANY] * len(after), out_specs=specs + [fixed(8, LANES)])
+    if prefetch:
+        places |= dict(grid=kept.pop("grid"), scratch_shapes=kept.pop("scratch_shapes", ()))
+        places = dict(grid_spec=pltpu.PrefetchScalarGridSpec(num_scalar_prefetch=prefetch, **places))
     *made, token = pl.pallas_call(
         body,
-        in_specs=list(in_specs) + [ANY] * len(after),
-        out_specs=specs + [fixed(8, LANES)],
+        **places,
         out_shape=shapes + [jax.ShapeDtypeStruct((8, LANES), F32)],
         compiler_params=pltpu.CompilerParams(vmem_limit_bytes=vmem),
         **kept,
     )(*operands, *waited)
     return (made[0] if single else made), token
+
+
+def hold(arrays, after):
+    return pallas(
+        lambda *refs: None,
+        arrays,
+        [ANY] * len(arrays),
+        after,
+        out_specs=[ANY] * len(arrays),
+        out_shape=[jax.ShapeDtypeStruct(array.shape, array.dtype) for array in arrays],
+        input_output_aliases={place: place for place in range(len(arrays))},
+        far_in=range(len(arrays)),
+        cost_estimate=cost(1),
+        name="hold",
+    )
 
 
 class Relay:
@@ -216,12 +236,9 @@
             self.kept = [self.net.swap(array, 1) for array in arrays]
 
     def finish(self, after=()):
-        sent = [come for _, come in self.held]
+        come, token = [come for _, come in self.held], None
         if after:
-            relay = Relay()
-            for array in sent:
-                relay.put(relay.make(*array.shape, BF), 0, 0, *array.shape, [(array, 0, 0)])
-            sent, token = relay.run(after, "hold")
+            come, token = hold(come, after)
         self.pieces = []
         for side in range(2):
             blocks = self.blocks[side]
@@ -229,10 +246,10 @@
             self.pieces += [
                 (side, blocks, self.held[side][0]),
                 (side, [block ^ 1 for block in blocks], self.kept[side]),
-                (side, others, self.held[side][1]),
-                (side, [block ^ 1 for block in others], self.net.swap(sent[side], 1)),
+                (side, others, come[side]),
+                (side, [block ^ 1 for block in others], self.net.swap(come[side], 1)),
             ]
-        return token if after else None
+        return token
 
     def arrivals(self):
         return [array for held in self.held for array in held[1:]]
@@ -287,7 +304,7 @@
     def __init__(self, net, value):
         self.net, self.value = net, value
         bits = [1 << place for place in range(net.count.bit_length() - 1)]
-        self.groups = [(1,)] + [(bit,) for bit in bits[3:]] + [(2, 4, 6)]
+        self.groups = [(1,), (2, 4, 6)] + [(bit,) for bit in bits[3:]]
         self.send()
 
     def send(self):
@@ -381,22 +398,14 @@
     return jnp.concatenate([table] * (width // LANES), 1)
 
 
-def turn_out(me, values, kept, sent):
-    turned = values.T
+def turn_out(me, values, kept, sent, turned):
+    turned[...] = values.T
     rows = D // BLOCKS
-    for number in range(BLOCKS):
-        place = (number ^ me) >> 1
-        block = turned[number * rows : (number + 1) * rows, :]
-        own = ((number ^ me) & 1) == 0
-        begin = pl.multiple_of(place * rows, rows)
-
-        @pl.when(own)
-        def _():
-            kept[pl.ds(begin, rows), :] = block
-
-        @pl.when(jnp.logical_not(own))
-        def _():
-            sent[pl.ds(begin, rows), :] = block
+    for place in range(BLOCKS // 2):
+        here = slice(place * rows, (place + 1) * rows)
+        for target, parity in ((kept, 0), (sent, 1)):
+            block = pl.multiple_of(((2 * place + parity) ^ me) * rows, rows)
+            target[here, :] = turned[pl.ds(block, rows), :]
 
 
 LINES = (3, 1, 1, 1, 1, 1, 1, 1)
@@ -405,9 +414,10 @@
 TABLE = 16
 
 
-def prepare_kernel(me_ref, shard, *rest):
+def prepare_kernel(me_ref, shard, second, *rest):
     small, (joined, row, rows) = rest[:-3], rest[-3:]
     joined[:, : 3 * D] = shard[...]
+    joined[:, 3 * D : 4 * D] = second[...]
     rows[...] = jnp.zeros_like(rows)
     line = 0
     for values, lines, length in zip(small, LINES, LENGTHS):
@@ -418,23 +428,23 @@
         for part in range(lines):
             rows[line + part : line + part + 1, :] = turned[0:1, part * LANES : (part + 1) * LANES]
         line += lines
-    joined[:, 3 * D : 3 * D + LANES] = rows[...].astype(BF)
-    joined[:, 3 * D + LANES :] = jnp.zeros((BLOCKS, LANES), BF)
-
-
-def prepare(me, shard, small):
+    joined[:, 4 * D : 4 * D + LANES] = rows[...].astype(BF)
+    joined[:, 4 * D + LANES :] = jnp.zeros((BLOCKS, LANES), BF)
+
+
+def prepare(me, shard, second, small):
     small = [values.reshape(1, -1) for values in small]
     return pallas(
         prepare_kernel,
-        in_specs=[SMEM, fixed(*shard.shape)] + [fixed(*values.shape) for values in small],
-        out_specs=fixed(BLOCKS, 3 * D + 2 * LANES),
-        out_shape=jax.ShapeDtypeStruct((BLOCKS, 3 * D + 2 * LANES), BF),
+        in_specs=[SMEM, fixed(*shard.shape), fixed(*second.shape)] + [fixed(*values.shape) for values in small],
+        out_specs=fixed(BLOCKS, 4 * D + 2 * LANES),
+        out_shape=jax.ShapeDtypeStruct((BLOCKS, 4 * D + 2 * LANES), BF),
         scratch_shapes=[pltpu.VMEM((8, 3 * LANES), F32), pltpu.VMEM((BLOCKS, LANES), F32)],
         cost_estimate=cost(2),
         name="prepare",
         near="all",
-        far_in=range(1, 10),
-        operands=(me, shard, *small),
+        far_in=range(1, 11),
+        operands=(me, shard, second, *small),
     )
 
 
@@ -459,12 +469,12 @@
 
 def project_kernel(layout_of, me_ref, tokens, cosine, sine, *rest):
     refs = rest[: len(layout_of)]
-    normed_kept, normed_sent, qkv_out, table, weight, lines, normed_out, sem, lines_sem = rest[len(layout_of) :]
+    normed_kept, normed_sent, qkv_out, table, weight, lines, normed_out, turned, sem, lines_sem = rest[len(layout_of) :]
     step = pl.program_id(0)
 
     @pl.when(step == 0)
     def _():
-        fetch(me_ref[0], layout_of, refs, (3 * D, 3 * D + LANES), lines, lines_sem)
+        fetch(me_ref[0], layout_of, refs, (4 * D, 4 * D + LANES), lines, lines_sem)
         fetch(me_ref[0], layout_of, refs, (0, 3 * D), weight, sem)
         arrive(lines, lines_sem)
         table_of(lines[...], table)
@@ -473,7 +483,7 @@
             part = slice(begin, begin + ROWS)
             unit, _ = normed(tokens[part, :].astype(F32))
             normed_out[part, :] = (unit * gain + shift).astype(BF)
-        turn_out(me_ref[0], normed_out[...], normed_kept, normed_sent)
+        turn_out(me_ref[0], normed_out[...], normed_kept, normed_sent, turned)
         arrive(weight, sem)
 
     column = pl.multiple_of(step * TILE, TILE)
@@ -509,6 +519,7 @@
             pltpu.VMEM((D, 3 * D), BF),
             pltpu.VMEM((D, LANES), BF),
             pltpu.VMEM((count, D), BF),
+            pltpu.VMEM((D, count), BF),
             pltpu.SemaphoreType.DMA,
             pltpu.SemaphoreType.DMA,
         ],
@@ -527,11 +538,11 @@
 
 def branch_kernel(layout_of, me_ref, mixed, tokens, table, *rest):
     refs = rest[: len(layout_of)]
-    resid, normed_two, normed_kept, normed_sent, mixed_kept, mixed_sent, weight, sem = rest[len(layout_of) :]
+    resid, normed_two, normed_kept, normed_sent, mixed_kept, mixed_sent, weight, turned, sem = rest[len(layout_of) :]
 
     @pl.when(pl.program_id(0) == 0)
     def _():
-        fetch(me_ref[0], layout_of, refs, (0, D), weight, sem)
+        fetch(me_ref[0], layout_of, refs, (3 * D, 4 * D), weight, sem)
         arrive(weight, sem)
 
     value = tokens[...].astype(F32) + (nn(mixed[...], weight[...]) + line_of(table, OUT_B))
@@ -539,8 +550,8 @@
     unit, _ = normed(value)
     low = (unit * line_of(table, GAIN_TWO) + line_of(table, SHIFT_TWO)).astype(BF)
     normed_two[...] = low
-    turn_out(me_ref[0], low, normed_kept, normed_sent)
-    turn_out(me_ref[0], mixed[...], mixed_kept, mixed_sent)
+    turn_out(me_ref[0], low, normed_kept, normed_sent, turned)
+    turn_out(me_ref[0], mixed[...], mixed_kept, mixed_sent, turned)
 
 
 def branch(me, mixed, tokens, table, pieces, after=()):
@@ -554,7 +565,7 @@
         out_specs=[rows, rows] + [pl.BlockSpec((D // 2, ROWS), lambda step: (0, step))] * 4,
         out_shape=[jax.ShapeDtypeStruct((count, D), F32), jax.ShapeDtypeStruct((count, D), BF)]
         + [jax.ShapeDtypeStruct((D // 2, count), BF)] * 4,
-        scratch_shapes=[pltpu.VMEM((D, D), BF), pltpu.SemaphoreType.DMA],
+        scratch_shapes=[pltpu.VMEM((D, D), BF), pltpu.VMEM((D, ROWS), BF), pltpu.SemaphoreType.DMA],
         cost_estimate=cost(12 / 4),
         name="branch",
         far_in=(1, 2, *range(4, 4 + len(pieces))),
@@ -581,21 +592,28 @@
 
     @pl.when(step == 0)
     def _():
-        fetch(me_ref[0], layout_of, refs, (D, D + FF), weight, sem)
+        fetch(me_ref[0], layout_of, refs, (0, FF), weight, sem)
         arrive(weight, sem)
 
     column = pl.multiple_of(step * TILE, TILE)
     tiles = D // TILE
     bias = table[pl.ds(UP_B + step // tiles, 1), pl.ds(pl.multiple_of(step % tiles * TILE, TILE), TILE)]
-    for begin in range(0, normed_two.shape[0], ROWS):
-        part = slice(begin, begin + ROWS)
-        value = nn(normed_two[part, :], weight[:, pl.ds(column, TILE)]) + bias
+    rows = FF // BLOCKS
+    odd = (me_ref[0] & 1) == 1
+    parts = [slice(begin, begin + UP_ROWS) for begin in range(0, normed_two.shape[0], UP_ROWS)]
+
+    def product(part):
+        return nn(normed_two[part, :], weight[:, pl.ds(column, TILE)])
+
+    ahead = product(parts[0])
+    for number, part in enumerate(parts):
+        value = ahead + bias
+        if number + 1 < len(parts):
+            ahead = product(parts[number + 1])
         share, density = gelu_parts(value)
         low = (value * share).astype(BF)
         activ[part, :] = low
         slope[part, :] = (share + value * density).astype(BF)
-        rows = FF // BLOCKS
-        odd = (me_ref[0] & 1) == 1
         pairs = [low[:, begin : begin + 2 * rows] for begin in range(0, TILE, 2 * rows)]
         sent = [jnp.where(odd, pair[:, :rows], pair[:, rows:]) for pair in pairs]
         activ_sent[part, :] = jnp.concatenate(sent, 1)
@@ -621,7 +639,7 @@
 
 
 def pre_kernel(slope, cotangent, weight, grad_pre, grad_bias):
-    sums = jnp.zeros((1, TILE), F32)
+    sums = jnp.zeros((1, WIDE_TILE), F32)
     for begin in range(0, slope.shape[0], ROWS):
         part = slice(begin, begin + ROWS)
         back = (nt(cotangent[part, :], weight[...]) * slope[part, :].astype(F32)).astype(BF)
@@ -632,14 +650,14 @@
 
 def pre(slope, cotangent, weight, after=()):
     count = slope.shape[0]
-    tile = pl.BlockSpec((count, TILE), lambda step: (0, step))
+    tile = pl.BlockSpec((count, WIDE_TILE), lambda step: (0, step))
     return pallas(
         pre_kernel,
-        grid=(FF // TILE,),
-        in_specs=[tile, fixed(count, D), pl.BlockSpec((TILE, D), lambda step: (step, 0))],
-        out_specs=[tile, pl.BlockSpec((1, TILE), lambda step: (0, step))],
+        grid=(FF // WIDE_TILE,),
+        in_specs=[tile, fixed(count, D), pl.BlockSpec((WIDE_TILE, D), lambda step: (step, 0))],
+        out_specs=[tile, pl.BlockSpec((1, WIDE_TILE), lambda step: (0, step))],
         out_shape=[jax.ShapeDtypeStruct((count, FF), BF), jax.ShapeDtypeStruct((1, FF), F32)],
-        cost_estimate=cost(16),
+        cost_estimate=cost(15),
         name="pre",
         far_in=(0, 1, 2),
         operands=(slope, cotangent, weight),
@@ -665,7 +683,7 @@
 def output_rows(activ, resid, table, weight, part, parts, before=(), after=()):
     count = activ.shape[0]
     rows = count // parts
-    wide_tile = 2 * TILE
+    wide_tile = WIDE_TILE
     mine = pl.BlockSpec((rows, D), lambda step: (part, 0))
     return pallas(
         output_kernel,
@@ -693,18 +711,15 @@
     return lax.dot_general(left, right, (((0,), (0,)), ((), ())), preferred_element_type=F32)
 
 
-def outer_rows_kernel(me_ref, left, left_other, right, right_other, *rest):
-    sides, grad_bias = rest[:4], rest[4]
+def outer_rows_kernel(me_ref, *refs):
+    own, other, (right, right_other), sides, grad_bias = refs[:4], refs[4:8], refs[8:10], refs[10:14], refs[14]
     step = pl.program_id(0)
-    rows = FF // BLOCKS
     half = right.shape[1] // 2
 
-    def group(ref, places):
-        return jnp.concatenate([ref[:, pl.ds(pl.multiple_of(place * rows, rows), rows)] for place in places], 1)
-
-    own = group(left, [me_ref[0] ^ (2 * (4 * step + z)) for z in range(4)])
-    other = group(left_other, [(me_ref[0] >> 1) ^ (4 * step + z) for z in range(4)])
-    product = tn(own, right[...]) + tn(other, right_other[...])
+    def group(blocks):
+        return jnp.concatenate([ref[...] for ref in blocks], 1)
+
+    product = tn(group(own), right[...]) + tn(group(other), right_other[...])
     for side in range(2):
         bit = (step >> (1 - side)) & 1
         values = product[:, side * half : (side + 1) * half]
@@ -725,25 +740,33 @@
 def outer_rows(me, left, left_other, right, right_other, after=()):
     count, size = left_other.shape
     width = right.shape[1]
-    block = (4 * FF // BLOCKS, width // 2)
+    rows = FF // BLOCKS
+    block = (4 * rows, width // 2)
+    own = [
+        pl.BlockSpec((count, rows), lambda step, me, z=z: (0, me[0] ^ (2 * (4 * step + z)))) for z in range(4)
+    ]
+    other = [
+        pl.BlockSpec((count, rows), lambda step, me, z=z: (0, (me[0] >> 1) ^ (4 * step + z))) for z in range(4)
+    ]
     return pallas(
         outer_rows_kernel,
         grid=(4,),
-        in_specs=[SMEM, fixed(count, 2 * size), fixed(count, size)] + [fixed(count, width)] * 2,
+        prefetch=1,
+        in_specs=own + other + [fixed(count, width)] * 2,
         out_specs=[
-            pl.BlockSpec(block, lambda step: (jnp.minimum(step, 1), 0)),
-            pl.BlockSpec(block, lambda step: (jnp.maximum(step - 2, 0), 0)),
-            pl.BlockSpec(block, lambda step: (step // 2, 0)),
-            pl.BlockSpec(block, lambda step: (step // 2, 0)),
+            pl.BlockSpec(block, lambda step, me: (jnp.minimum(step, 1), 0)),
+            pl.BlockSpec(block, lambda step, me: (jnp.maximum(step - 2, 0), 0)),
+            pl.BlockSpec(block, lambda step, me: (step // 2, 0)),
+            pl.BlockSpec(block, lambda step, me: (step // 2, 0)),
             fixed(1, width),
         ],
         out_shape=[jax.ShapeDtypeStruct((size // 2, width // 2), kind) for kind in (F32, BF, F32, BF)]
         + [jax.ShapeDtypeStruct((1, width), F32)],
         cost_estimate=cost(16),
         name="outer_rows",
-        far_in=(1, 2, 3, 4),
+        far_in=range(1, 11),
         near=(0, 1, 2, 3),
-        operands=(me, left, left_other, right, right_other),
+        operands=(me, *[left] * 4, *[left_other] * 4, right, right_other),
         after=after,
     )
 
@@ -771,7 +794,7 @@
             grad_bias[...] = jnp.sum(right[...].astype(F32), axis=0, keepdims=True)
 
 
-def outer(sets, tile_width, after=()):
+def outer(sets, tile_width, after=(), free=()):
     size, count = sets[0][0].shape
     parts, tiles, operands, in_specs = [], 0, [], []
 
@@ -808,28 +831,26 @@
         + [jax.ShapeDtypeStruct((1, width), F32)],
         cost_estimate=cost(4 * count * size * width / 0.55e9),
         name="outer",
-        far_in=range(len(operands)),
+        far_in=[place for place, array in enumerate(operands) if not any(array is each for each in free)],
         near=(0, 1, 2, 3),
         operands=tuple(operands),
         after=after,
     )
 
 
-def branch_back_kernel(layout_of, me_ref, grad_pre, resid, cotangent, table, *rest):
-    refs = rest[: len(layout_of)]
-    grad_resid, grad_branch, grad_mixed, grad_gain, grad_shift, grad_bias, up_weight, out_weight, up_sem, out_sem = rest[
-        len(layout_of) :
-    ]
+def branch_back_kernel(layout_of, out_layout, me_ref, grad_pre, resid, cotangent, table, *rest):
+    refs, rest = rest[: len(layout_of)], rest[len(layout_of) :]
+    out_refs, rest = rest[: len(out_layout)], rest[len(out_layout) :]
+    grad_resid, grad_branch, grad_mixed, grad_gain, grad_shift, grad_bias, up_weight, out_weight, up_sem, out_sem = rest
 
     @pl.when(pl.program_id(0) == 0)
     def _():
-        fetch(me_ref[0], layout_of, refs, (D, D + FF), up_weight, up_sem)
-        fetch(me_ref[0], layout_of, refs, (0, D), out_weight, out_sem)
+        fetch(me_ref[0], layout_of, refs, (0, FF), up_weight, up_sem)
+        fetch(me_ref[0], out_layout, out_refs, (3 * D, 4 * D), out_weight, out_sem)
         grad_gain[...] = jnp.zeros_like(grad_gain)
         grad_shift[...] = jnp.zeros_like(grad_shift)
         grad_bias[...] = jnp.zeros_like(grad_bias)
         arrive(up_weight, up_sem)
-        arrive(out_weight, out_sem)
 
     upstream = nt(grad_pre[...], up_weight[...])
     back, gain_part, shift_part = norm_back(resid[...], line_of(table, GAIN_TWO), upstream)
@@ -840,19 +861,24 @@
     grad_gain[...] += gain_part
     grad_shift[...] += shift_part
     grad_bias[...] += jnp.sum(low.astype(F32), axis=0, keepdims=True)
+
+    @pl.when(pl.program_id(0) == 0)
+    def _():
+        arrive(out_weight, out_sem)
+
     grad_mixed[...] = nt(low, out_weight[...]).astype(BF)
 
 
-def branch_back(me, grad_pre, resid, cotangent, table, pieces, after=()):
+def branch_back(me, grad_pre, resid, cotangent, table, pieces, out_pieces, after=()):
     count = resid.shape[0]
-    layout_of = describe(pieces)
+    layout_of, out_layout = describe(pieces), describe(out_pieces)
     rows = pl.BlockSpec((ROWS, D), lambda step: (step, 0))
     vector = jax.ShapeDtypeStruct((1, D), F32)
     return pallas(
-        functools.partial(branch_back_kernel, layout_of),
+        functools.partial(branch_back_kernel, layout_of, out_layout),
         grid=(count // ROWS,),
         in_specs=[SMEM, pl.BlockSpec((ROWS, FF), lambda step: (step, 0)), rows, rows, fixed(TABLE, D)]
-        + [ANY] * len(pieces),
+        + [ANY] * (len(pieces) + len(out_pieces)),
         out_specs=[rows, rows, rows] + [fixed(1, D)] * 3,
         out_shape=[
             jax.ShapeDtypeStruct((count, D), F32),
@@ -870,16 +896,15 @@
         ],
         cost_estimate=cost(21),
         name="branch_back",
-        far_in=(1, 2, 3, *range(5, 5 + len(pieces))),
+        far_in=(1, 2, 3, *range(5, 5 + len(pieces) + len(out_pieces))),
         near=(1, 2),
-            operands=(me, grad_pre, resid, cotangent, table, *[array for _, _, array in pieces],),
+            operands=(me, grad_pre, resid, cotangent, table, *[array for _, _, array in (*pieces, *out_pieces)],),
         after=after,
     )
 
 
-def tokens_back_kernel(layout_of, chunks, biases, me_ref, *rest):
+def tokens_back_kernel(layout_of, chunks, me_ref, *rest):
     grads, rest = rest[:chunks], rest[chunks:]
-    qkv_biases, rest = rest[:biases], rest[biases:]
     tokens, grad_resid, table, out_bias, up_bias, down_bias, gain_two, shift_two = rest[:8]
     refs = rest[8 : 8 + len(layout_of)]
     grad_tokens, grad_table, weight, sem = rest[8 + len(layout_of) :]
@@ -892,17 +917,15 @@
             grad_table[row : row + 1, :] = ref[...]
         for part in range(FF // D):
             grad_table[UP_B + part : UP_B + part + 1, :] = up_bias[:, part * D : (part + 1) * D]
-        groups = [(ref, begin) for ref in qkv_biases for begin in range(0, ref.shape[1], 3 * QUAD)]
-        for quad, (ref, begin) in enumerate(groups):
-            for part in range(3):
-                values = ref[:, begin + part * QUAD : begin + (part + 1) * QUAD]
-                grad_table[QKV_B + part : QKV_B + part + 1, quad * QUAD : (quad + 1) * QUAD] = values
         arrive(weight, sem)
 
     quads = [(ref, begin) for ref in grads for begin in range(0, ref.shape[1], 3 * QUAD)]
     ordered = jnp.concatenate(
         [ref[:, begin + part * QUAD : begin + (part + 1) * QUAD] for part in range(3) for ref, begin in quads], 1
     )
+    for part in range(3):
+        sums = jnp.sum(ordered[:, part * D : (part + 1) * D].astype(F32), axis=0, keepdims=True)
+        grad_table[QKV_B + part : QKV_B + part + 1, :] += sums
     back, gain_part, shift_part = norm_back(
         tokens[...].astype(F32), line_of(table, GAIN_ONE), nt(ordered, weight[...])
     )
@@ -911,16 +934,15 @@
     grad_table[SHIFT_ONE : SHIFT_ONE + 1, :] += shift_part
 
 
-def tokens_back(me, grads, qkv_biases, tokens, grad_resid, table, biases, pieces, after=()):
+def tokens_back(me, grads, tokens, grad_resid, table, biases, pieces, after=()):
     count = tokens.shape[0]
     layout_of = describe(pieces)
     rows = pl.BlockSpec((ROWS, D), lambda step: (step, 0))
     return pallas(
-        functools.partial(tokens_back_kernel, layout_of, len(grads), len(qkv_biases)),
+        functools.partial(tokens_back_kernel, layout_of, len(grads)),
         grid=(count // ROWS,),
         in_specs=[SMEM]
         + [pl.BlockSpec((ROWS, part.shape[1]), lambda step: (step, 0)) for part in grads]
-        + [fixed(*part.shape) for part in qkv_biases]
         + [rows, rows, fixed(TABLE, D)]
         + [fixed(*part.shape) for part in biases]
         + [ANY] * len(pieces),
@@ -929,14 +951,14 @@
         scratch_shapes=[pltpu.VMEM((D, 3 * D), BF), pltpu.SemaphoreType.DMA],
         cost_estimate=cost(15),
         name="tokens_back",
-        far_in=range(len(grads) + len(qkv_biases) + 1, len(grads) + len(qkv_biases) + 3),
-        operands=(me, *grads, *qkv_biases, tokens, grad_resid, table, *biases, *[array for _, _, array in pieces]),
+        far_in=range(len(grads) + 1, len(grads) + 3),
+        operands=(me, *grads, tokens, grad_resid, table, *biases, *[array for _, _, array in pieces]),
         after=after,
     )
 
 
-def finish_kernel(lengths, number, *refs):
-    weights, sums, outs = refs[:8], refs[8:12], refs[12:]
+def finish_kernel(lengths, terms, number, *refs):
+    weights, sums, outs = refs[:8], refs[8 : 8 + terms], refs[8 + terms :]
     for chunk in range(2):
         arrived = weights[4 * chunk : 4 * chunk + 4]
         for half in range(2):
@@ -963,7 +985,7 @@
     lengths = [(size // count, size // D) for size in sizes]
     rows = weights[0].shape[0]
     return pallas(
-        functools.partial(finish_kernel, lengths),
+        functools.partial(finish_kernel, lengths, len(total)),
         in_specs=[SMEM] + [fixed(*array.shape) for array in (*weights, *total)],
         out_specs=[fixed(rows, 3 * D)] + [fixed(1, length) for length, _ in lengths],
         out_shape=[jax.ShapeDtypeStruct((rows, 3 * D), F32)]
@@ -1263,9 +1285,9 @@
     sizes = [item.shape[0] * count for item in small]
     clips = (clip_frames, clip_patches)
 
-    joined, _ = prepare(me_ref, net.widen(qkv_weight), [net.widen(values) for values in small])
+    joined, _ = prepare(me_ref, net.widen(qkv_weight), net.widen(out_weight), [net.widen(values) for values in small])
     first = Gather(net, joined)
-    middle_shard = net.widen(jnp.concatenate([out_weight, up_weight], 1))
+    middle_shard = net.widen(up_weight)
     cosine, sine = rotary_tables(positions_of(clip_frames[0], clip_patches[0]))
 
     def copy_of(shard):
@@ -1276,7 +1298,7 @@
 
     made, _ = advance([first], extra=copy_of(middle_shard))
     middle = Gather(net, made[0])
-    advance([first], after=[middle.held[0][2]])
+    advance([first], after=[middle.held[0][1]])
     first.finish()
     made, token = advance([middle], after=first.arrivals(), extra=copy_of(down_weight))
     final = lax.all_gather(made[0], AXES, axis=0, tiled=True)
@@ -1286,11 +1308,11 @@
     normed_other = net.swap(normed_sent, 1)
     _, token = advance([middle], after=[token])
     (mixed, log_totals), token = attend(*clips, qkv, after=[token])
-    token = middle.finish([token])
     cotangent_other = net.swap(cotangent, 1)
     (resid, normed_two, two_kept, two_sent, mixed_kept, mixed_sent), token = branch(
-        me_ref, mixed, tokens, table, [piece for piece in middle.pieces if piece[0] == 0], after=[token]
-    )
+        me_ref, mixed, tokens, table, [piece for piece in first.pieces if piece[0] == 1], after=[token]
+    )
+    token = middle.finish([token])
     two_other, mixed_other = net.swap(two_sent, 1), net.swap(mixed_sent, 1)
     (activ, slope, activ_sent), token = up(me_ref, normed_two, table, middle.pieces, after=[token])
     activ_other = net.swap(activ_sent, 1)
@@ -1301,7 +1323,7 @@
     )
     moving_down = Scatter(net, by_side(sides))
     (grad_resid, grad_branch, grad_mixed, grad_gain_two, grad_shift_two, grad_out_bias), token = branch_back(
-        me_ref, grad_pre, resid, cotangent, table, middle.pieces, after=[token]
+        me_ref, grad_pre, resid, cotangent, table, middle.pieces, first.pieces[4:], after=[token]
     )
     grad_branch_other = net.swap(grad_branch, 1)
     _, token = advance([moving_down], after=[token])
@@ -1309,9 +1331,10 @@
         [(mixed_kept, mixed_other, grad_branch, grad_branch_other), (two_kept, two_other, grad_pre, grad_pre_other)],
         TILE,
         after=[token],
+        free=(grad_branch, grad_branch_other),
     )
     moving_up = Scatter(net, by_side(sides), (D, FF))
-    parts, others, grad_qkv_bias, moving_qkv = [], [], [], []
+    parts, others, moving_qkv = [], [], []
 
     def back(quad, token):
         part, token = attend_back(
@@ -1323,8 +1346,7 @@
 
     def weigh(quads, token):
         sets = [(normed_kept, normed_other, parts[quad], others[quad]) for quad in quads]
-        (*sides, bias), token = outer(sets, QUAD, after=[token])
-        grad_qkv_bias.append(bias)
+        (*sides, _), token = outer(sets, 3 * QUAD, after=[token], free=(*parts, *others))
         moving_qkv.append(Scatter(net, by_side(sides)))
         return token
 
@@ -1332,17 +1354,14 @@
     _, token = advance([moving_down], after=[token])
     token = back(1, token)
     _, token = advance([moving_up], after=[token])
+    token = back(2, token)
+    _, token = advance([moving_up, moving_down], after=[token])
     token = weigh([0, 1], token)
-    _, token = advance([moving_up], after=[token])
-    token = back(2, token)
-    _, token = advance([moving_down, moving_qkv[0]], after=[token])
     token = back(3, token)
     _, token = advance([moving_qkv[0]], after=[token])
-    token = weigh([2, 3], token)
     (grad_tokens, grad_table), token = tokens_back(
         me_ref,
         parts,
-        grad_qkv_bias,
         tokens,
         grad_resid,
         table,
@@ -1351,17 +1370,14 @@
         after=[token],
     )
     total = Sum(net, grad_table)
-    def rows_of(part, token, before=()):
-        return output_rows(activ, resid, table, final, part, 4, before, after=[token])
-
-    _, token = advance([moving_qkv[1], moving_up], after=[token, *moving_qkv[0].held[1:]])
-    output, token = rows_of(0, token)
-    _, token = advance([total], after=[token])
-    output, token = rows_of(1, token, [output])
+    _, token = advance([moving_qkv[0], moving_up], after=[token])
+    token = weigh([2, 3], token)
+    _, token = advance([total], after=[token, *moving_qkv[0].held[1:]])
+    output, token = output_rows(activ, resid, table, final, 0, 2, after=[token])
     _, token = advance([moving_qkv[1], total], after=[token])
-    output, token = rows_of(2, token, [output])
-    _, token = advance([total], after=[token])
-    output, token = rows_of(3, token, [output])
+    output, token = output_rows(activ, resid, table, final, 2, 4, [output], after=[token])
+    _, token = advance([moving_qkv[1], total], after=[token])
+    output, token = output_rows(activ, resid, table, final, 3, 4, [output], after=[token])
     (grad_qkv_weight, *own), _ = finish(
         net.number.reshape(1), (*moving_qkv[0].held, *moving_qkv[1].held), total.finish(), sizes, count, [token]
     )

time: 469 us -> 435 us (0.928)
  Pallas kernels: 301 us -> 280 us
  waiting for transfers between devices: 71.7 us -> 60.1 us
    pallas_call x36 -> x34, Pallas kernels: 301 us -> 280 us  [pallas(): pl.pallas_call(body, **places, out_shape=shapes + [jax.ShapeDtypeStruct((...]
    ppermute x67, waiting for transfers between devices: 71.7 us -> 60 us  [permute(): lax.ppermute(value, AXES, [(number, number ^ mask) for number in range(se...]
  transfers between devices with their start and end apart: 68 -> 68, of which waited for: 14 -> 12; matrix products, arithmetic and copies ran while one was open for 1% -> 1% of each run, Pallas kernels for 64% -> 65%
where the time goes in v3:
time: 435 us; the launch traced here: 427 us
  Pallas kernels  280 us (64%)
  starting transfers between devices  62.2 us (14%)
  waiting for transfers between devices  60.1 us (14%)
  between operations  15 us (3%)
  local copies, waits for them, and re-layouts  5.97 us (1%)
    pallas_call x34, Pallas kernels, pallas(): pl.pallas_call(body, **places, out_shape=shapes + [jax.ShapeDtypeStruct((...  280 us
    ppermute x67, starting transfers between devices, permute(): lax.ppermute(value, AXES, [(number, number ^ mask) for number in range(se...  62.2 us
    ppermute x67, waiting for transfers between devices, permute(): lax.ppermute(value, AXES, [(number, number ^ mask) for number in range(se...  60 us
  transfers between devices with their start and end apart: 68, of which 12 were waited for; matrix products, arithmetic and copies ran while one was open for 1% of the time, Pallas kernels for 65%

profile of v3, /device:TPU:0, one launch (start us, length us, event | category | flops | bytes accessed | tf_op | source)
XLA Modules:
  0.0 427.2 jit_solution(1739515353695091170)
XLA Ops:
  8.9 5.0 %collective-permute-start.2 = (bf16[32,4352]{1,0:T(8,128)(2,1)S(1)}, bf16[32,4352]{1,0:T(8,128)(2,1)S(1)}, u32[]{:S(2)}, u32[]{:S(2)}) collective-permute-start(bf16[32,4352]{1,0:T(8,128)(2,1)S(1)} %get-tuple-element.153.refs_1_), channel_id=1, source_target_pairs={{0,6},{1,7},{2,4},{3,5},{4,2},{5,3},{6,0},{7,1},{8,14},{9,15},{10,... | collective-permute-start | bytes 835592 | tf_op jit(solution)/shard_map/ppermute | solution.py:173
  14.5 7.1 %collective-permute-done.2.refs_4_ = bf16[32,4352]{1,0:T(8,128)(2,1)S(1)} collective-permute-done((bf16[32,4352]{1,0:T(8,128)(2,1)S(1)}, bf16[32,4352]{1,0:T(8,128)(2,1)S(1)}, u32[]{:S(2)}, u32[]{:S(2)}) %collective-permute-start.2) | collective-permute-done | bytes 278560 | tf_op jit(solution)/shard_map/ppermute | solution.py:173
  21.6 16.1 %collective-permute-done.1.refs_3_ = bf16[32,4352]{1,0:T(8,128)(2,1)S(1)} collective-permute-done((bf16[32,4352]{1,0:T(8,128)(2,1)S(1)}, bf16[32,4352]{1,0:T(8,128)(2,1)S(1)}, u32[]{:S(2)}, u32[]{:S(2)}) %collective-permute-start.1) | collective-permute-done | bytes 278560 | tf_op jit(solution)/shard_map/ppermute | solution.py:173
  41.5 6.8 %collective-permute-done.5.refs_4_.refs_2_ = bf16[32,4096]{1,0:T(8,128)(2,1)S(1)} collective-permute-done((bf16[32,4096]{1,0:T(8,128)(2,1)S(1)}, bf16[32,4096]{1,0:T(8,128)(2,1)S(1)}, u32[]{:S(2)}, u32[]{:S(2)}) %collective-permute-start.5) | collective-permute-done | bytes 262176 | tf_op jit(solution)/shard_map/ppermute | solution.py:173
  62.0 5.1 %collective-permute-done.13.refs_4_ = bf16[32,4096]{1,0:T(8,128)(2,1)S(1)} collective-permute-done((bf16[32,4096]{1,0:T(8,128)(2,1)S(1)}, bf16[32,4096]{1,0:T(8,128)(2,1)S(1)}, u32[]{:S(2)}, u32[]{:S(2)}) %collective-permute-start.13) | collective-permute-done | bytes 262176 | tf_op jit(solution)/shard_map/ppermute | solution.py:173
  67.0 11.5 %collective-permute-done.7.refs_5_.refs_6_.refs_15_ = bf16[256,2176]{1,0:T(8,128)(2,1)} collective-permute-done((bf16[256,2176]{1,0:T(8,128)(2,1)S(1)}, bf16[256,2176]{1,0:T(8,128)(2,1)}, u32[]{:S(2)}, u32[]{:S(2)}) %collective-permute-start.7) | collective-permute-done | bytes 1114144 | tf_op jit(solution)/shard_map/ppermute | solution.py:173
  83.7 17.0 %project.1 = (bf16[512,1024]{1,0:T(8,128)(2,1)}, bf16[512,1024]{1,0:T(8,128)(2,1)S(1)}, bf16[1024,3072]{1,0:T(8,128)(2,1)}, f32[16,1024]{1,0:T(8,128)S(1)}, f32[8,128]{1,0:T(8,128)S(1)}) custom-call(s32[1]{0:T(128)} %bitcast.refs_0_, bf16[1024,1024]{1,0:T(8,128)(2,1)} %refs_5_.1, f32[1024,128]{1,0:T(8,128)S(1)} %get-tuple-element.304.refs_2_.refs_8_, ...), custom_call_target="tpu_custom_call" | custom-call | flops 46000001024 | tf_op jit(solution)/shard_map/project/pallas_call | solution.py:83
  105.0 24.6 %attend.1 = (bf16[1024,1024]{1,0:T(8,128)(2,1)}, f32[2,8,1024]{2,1,0:T(8,128)}, f32[8,128]{1,0:T(8,128)S(1)}) custom-call(s32[1,4]{1,0:T(1,128)S(1)} %copy-done, s32[1,4]{1,0:T(1,128)S(1)} %copy-done.2, bf16[1024,3072]{1,0:T(8,128)(2,1)} %get-tuple-element.160.refs_2_.refs_3_.refs_4_, bf16[1024,3072]{1,0:T(8,128)(2,1)} %get-tuple-element.160.refs_2_.refs_3_.refs_4_, ...), custom_call_target="tpu_custom_call" | custom-call | flops 74750001152 | tf_op jit(solution)/shard_map/attend/pallas_call | solution.py:83
  129.7 9.5 %branch.1 = (f32[1024,1024]{1,0:T(8,128)}, bf16[1024,1024]{1,0:T(8,128)(2,1)S(1)}, bf16[512,1024]{1,0:T(8,128)(2,1)}, bf16[512,1024]{1,0:T(8,128)(2,1)}, bf16[51...) custom-call(s32[1]{0:T(128)} %bitcast.refs_0_, ...), custom_call_target="tpu_custom_call" | custom-call | flops 34500001792 | tf_op jit(solution)/shard_map/branch/pallas_call | solution.py:83
  147.3 28.6 %up.1 = (bf16[1024,4096]{1,0:T(8,128)(2,1)}, bf16[1024,4096]{1,0:T(8,128)(2,1)}, bf16[1024,2048]{1,0:T(8,128)(2,1)}, f32[8,128]{1,0:T(8,128)S(1)}) custom-call(s32[1]{0:T(128)} %bitcast.refs_0_, bf16[1024,1024]{1,0:T(8,128)(2,1)S(1)} %copy-done.29, f32[16,1024]{1,0:T(8,128)S(1)} %get-tuple-element.166.refs_3_.refs_2_.refs_4_.refs_7_, ...), custom_call_target="tpu_custom_call" | custom-call | flops 100624998400 | tf_op jit(solution)/shard_map/up/pallas_call | solution.py:83
  176.1 15.8 %pre.1 = (bf16[1024,4096]{1,0:T(8,128)(2,1)}, f32[1,4096]{1,0:T(1,128)}, f32[8,128]{1,0:T(8,128)S(1)}) custom-call(bf16[1024,4096]{1,0:T(8,128)(2,1)} %get-tuple-element.178.refs_0_, bf16[1024,1024]{1,0:T(8,128)(2,1)} %refs_3_.1, bf16[4096,1024]{1,0:T(8,128)(2,1)} %all-gather.2.cloned.1.call-done.refs_2_.refs_3_, f32[8,128]{1,0:T(8,128)S(1)} %get-tuple-element.179.refs_3_), custom_call_target="tpu_custom_call" | custom-call | flops 172499992576 | tf_op jit(solution)/shard_map/pre/pallas_call | solution.py:83
  191.9 15.1 %outer_rows.1 = (f32[1024,512]{1,0:T(8,128)S(1)}, bf16[1024,512]{1,0:T(8,128)(2,1)}, f32[1024,512]{1,0:T(8,128)S(1)}, bf16[1024,512]{1,0:T(8,128)(2,1)}, f32[1,1024]{1,0:T(1,128)}, /*index=5*/f32[8,128]{1,0:T(8,128)S(1)}) custom-call(s32[1]{0:T(128)} %bitcast.refs_0_, bf16[1024,4096]{1,0:T(8,128)(2,1)} %get-tuple-element.175.refs_1_.refs_2_.refs_3_.refs_4_.refs_0_, ...), custom_call_target="tpu_custom_call" | custom-call | flops 184000004096 | tf_op jit(solution)/shard_map/outer_rows/pallas_call | solution.py:83
  209.8 21.5 %branch_back.1 = (f32[1024,1024]{1,0:T(8,128)}, bf16[1024,1024]{1,0:T(8,128)(2,1)S(1)}, bf16[1024,1024]{1,0:T(8,128)(2,1)S(1)}, f32[1,1024]{1,0:T(1,128)}, f32[1...) custom-call(s32[1]{0:T(128)} %bitcast.refs_0_, bf16[1024,4096]{1,0:T(8,128)(2,1)} %get-tuple-element.180.refs_1_.refs_6_, ...), custom_call_target="tpu_custom_call" | custom-call | flops 241499996160 | tf_op jit(solution)/shard_map/branch_back/pallas_call | solution.py:83
  238.9 19.7 %outer.3 = (f32[256,2560]{1,0:T(8,128)S(1)}, bf16[256,2560]{1,0:T(8,128)(2,1)}, f32[256,2560]{1,0:T(8,128)S(1)}, bf16[256,2560]{1,0:T(8,128)(2,1)}, f32[1,5120]{1,0:T(1,128)}, /*index=5*/f32[8,128]{1,0:T(8,128)S(1)}) custom-call(bf16[512,1024]{1,0:T(8,128)(2,1)} %get-tuple-element.186.refs_0_, bf16[512,1024]{1,0:T(8,128)(2,1)} %collective-permute-done.24.refs_1_, ...), custom_call_target="tpu_custom_call" | custom-call | flops 224509657088 | tf_op jit(solution)/shard_map/outer/pallas_call | solution.py:83
  262.0 13.2 %attend_back.4 = (bf16[1024,768]{1,0:T(8,128)(2,1)S(1)}, f32[8,128]{1,0:T(8,128)S(1)}) custom-call(s32[1,4]{1,0:T(1,128)S(1)} %copy-done.1, s32[1,4]{1,0:T(1,128)S(1)} %copy-done.3, bf16[1024,3072]{1,0:T(8,128)(2,1)} %get-tuple-element.160.refs_2_.refs_3_.refs_4_, bf16[1024,3072]{1,0:T(8,128)(2,1)} %get-tuple-element.160.refs_2_.refs_3_.refs_4_, ...), custom_call_target="tpu_custom_call" | custom-call | flops 172499992576 | tf_op jit(solution)/shard_map/attend_back/pallas_call | solution.py:83
  282.7 13.1 %attend_back.5 = (bf16[1024,768]{1,0:T(8,128)(2,1)S(1)}, f32[8,128]{1,0:T(8,128)S(1)}) custom-call(s32[1,4]{1,0:T(1,128)S(1)} %copy-done.1, s32[1,4]{1,0:T(1,128)S(1)} %copy-done.3, bf16[1024,3072]{1,0:T(8,128)(2,1)} %get-tuple-element.160.refs_2_.refs_3_.refs_4_, bf16[1024,3072]{1,0:T(8,128)(2,1)} %get-tuple-element.160.refs_2_.refs_3_.refs_4_, ...), custom_call_target="tpu_custom_call" | custom-call | flops 172499992576 | tf_op jit(solution)/shard_map/attend_back/pallas_call | solution.py:83
  301.8 12.9 %attend_back.6 = (bf16[1024,768]{1,0:T(8,128)(2,1)S(1)}, f32[8,128]{1,0:T(8,128)S(1)}) custom-call(s32[1,4]{1,0:T(1,128)S(1)} %copy-done.1, s32[1,4]{1,0:T(1,128)S(1)} %copy-done.3, bf16[1024,3072]{1,0:T(8,128)(2,1)} %get-tuple-element.160.refs_2_.refs_3_.refs_4_, bf16[1024,3072]{1,0:T(8,128)(2,1)} %get-tuple-element.160.refs_2_.refs_3_.refs_4_, ...), custom_call_target="tpu_custom_call" | custom-call | flops 172499992576 | tf_op jit(solution)/shard_map/attend_back/pallas_call | solution.py:83
  323.0 7.4 %outer.4 = (f32[256,768]{1,0:T(8,128)S(1)}, bf16[256,768]{1,0:T(8,128)(2,1)}, f32[256,768]{1,0:T(8,128)S(1)}, bf16[256,768]{1,0:T(8,128)(2,1)}, f32[1,1536]{1,0:T(1,128)}, /*index=5*/f32[8,128]{1,0:T(8,128)S(1)}) custom-call(bf16[512,1024]{1,0:T(8,128)(2,1)} %get-tuple-element.213.refs_0_, bf16[512,1024]{1,0:T(8,128)(2,1)} %copy-done.39, ...), custom_call_target="tpu_custom_call" | custom-call | flops 67352895488 | tf_op jit(solution)/shard_map/outer/pallas_call | solution.py:83
  333.3 12.9 %attend_back.7 = (bf16[1024,768]{1,0:T(8,128)(2,1)S(1)}, f32[8,128]{1,0:T(8,128)S(1)}) custom-call(s32[1,4]{1,0:T(1,128)S(1)} %copy-done.1, s32[1,4]{1,0:T(1,128)S(1)} %copy-done.3, bf16[1024,3072]{1,0:T(8,128)(2,1)} %get-tuple-element.160.refs_2_.refs_3_.refs_4_, bf16[1024,3072]{1,0:T(8,128)(2,1)} %get-tuple-element.160.refs_2_.refs_3_.refs_4_, ...), custom_call_target="tpu_custom_call" | custom-call | flops 172499992576 | tf_op jit(solution)/shard_map/attend_back/pallas_call | solution.py:83
  350.5 14.4 %tokens_back.1 = (bf16[1024,1024]{1,0:T(8,128)(2,1)}, f32[16,1024]{1,0:T(8,128)}, f32[8,128]{1,0:T(8,128)S(1)}) custom-call(s32[1]{0:T(128)} %bitcast.refs_0_, bf16[1024,768]{1,0:T(8,128)(2,1)S(1)} %copy-done.5, bf16[1024,768]{1,0:T(8,128)(2,1)S(1)} %copy-done.7, bf16[1024,768]{1,0:T(8,128)(2,1)S(1)} %get-tuple-element.212.refs_3_.refs_2_, ...), custom_call_target="tpu_custom_call" | custom-call | flops 172499992576 | tf_op jit(solution)/shard_map/tokens_back/pallas_call | solution.py:83
  372.3 6.6 %outer.5 = (f32[256,768]{1,0:T(8,128)S(1)}, bf16[256,768]{1,0:T(8,128)(2,1)S(1)}, f32[256,768]{1,0:T(8,128)S(1)}, bf16[256,768]{1,0:T(8,128)(2,1)S(1)}, f32[1,1536]{1,0:T(1,128)}, /*index=5*/f32[8,128]{1,0:T(8,128)S(1)}) custom-call(bf16[512,1024]{1,0:T(8,128)(2,1)} %get-tuple-element.213.refs_0_, bf16[512,1024]{1,0:T(8,128)(2,1)} %copy-done.39, ...), custom_call_target="tpu_custom_call" | custom-call | flops 67352895488 | tf_op jit(solution)/shard_map/outer/pallas_call | solution.py:83
  386.3 9.6 %output.3 = (bf16[1024,1024]{1,0:T(8,128)(2,1)}, f32[8,128]{1,0:T(8,128)S(1)}) custom-call(bf16[1024,4096]{1,0:T(8,128)(2,1)} %get-tuple-element.175.refs_1_.refs_2_.refs_3_.refs_4_.refs_0_, f32[1024,1024]{1,0:T(8,128)} %get-tuple-element.176.refs_2_.refs_1_, f32[16,1024]{1,0:T(8,128)S(1)} %get-tuple-element.166.refs_3_.refs_2_.refs_4_.refs_7_, ...), custom_call_target="tpu_custom_call" | custom-call | flops 92000002048 | tf_op jit(solution)/shard_map/output/pallas_call | solution.py:83
  400.1 7.1 %output.4 = (bf16[1024,1024]{1,0:T(8,128)(2,1)}, f32[8,128]{1,0:T(8,128)S(1)}) custom-call(bf16[1024,4096]{1,0:T(8,128)(2,1)} %get-tuple-element.175.refs_1_.refs_2_.refs_3_.refs_4_.refs_0_, f32[1024,1024]{1,0:T(8,128)} %get-tuple-element.176.refs_2_.refs_1_, ...), custom_call_target="tpu_custom_call", output_to_operand_aliasing={{0}: (4, {})} | custom-call | flops 46000001024 | tf_op jit(solution)/shard_map/output/pallas_call | solution.py:83
  411.9 7.1 %output.5 = (bf16[1024,1024]{1,0:T(8,128)(2,1)}, f32[8,128]{1,0:T(8,128)S(1)}) custom-call(bf16[1024,4096]{1,0:T(8,128)(2,1)} %get-tuple-element.175.refs_1_.refs_2_.refs_3_.refs_4_.refs_0_, f32[1024,1024]{1,0:T(8,128)} %get-tuple-element.176.refs_2_.refs_1_, ...), custom_call_target="tpu_custom_call", output_to_operand_aliasing={{0}: (4, {})} | custom-call | flops 46000001024 | tf_op jit(solution)/shard_map/output/pallas_call | solution.py:83
  (239 shorter events, 104.2 us)
Async XLA Ops:
  7.2 168.9 %all-gather.2.cloned.1.call-start = ((), (), s32[]{:S(2)}) async-start(), calls=%async_computation | async-start | bytes 8650752 | tf_op jit(solution)/shard_map/all_gather | solution.py:1304
  14.0 23.7 %collective-permute-start = (bf16[32,4352]{1,0:T(8,128)(2,1)S(1)}, bf16[32,4352]{1,0:T(8,128)(2,1)S(1)}, u32[]{:S(2)}, u32[]{:S(2)}) collective-permute-start(bf16[32,4352]{1,0:T(8,128)(2,1)S(1)} %get-tuple-element.153.refs_1_), channel_id=1, source_target_pairs={{0,2},{1,3},{2,0},{3,1},{4,6},{5,7},{6,4},{7,5},{8,10},{9,11},{10,... | collective-permute-start | bytes 835592 | tf_op jit(solution)/shard_map/ppermute | solution.py:173
  54.0 24.5 %collective-permute-start.7 = (bf16[256,2176]{1,0:T(8,128)(2,1)S(1)}, bf16[256,2176]{1,0:T(8,128)(2,1)}, u32[]{:S(2)}, u32[]{:S(2)}) collective-permute-start(bf16[256,2176]{1,0:T(8,128)(2,1)S(1)} %get-tuple-element.157.refs_4_.refs_13_), channel_id=1, source_target_pairs={{0,8},{1,9},{2,10},{3,11},{4,12},{5,13},{6,14},{7,15},{8,0},{9,1},... | collective-permute-start | bytes 3342344 | tf_op jit(solution)/shard_map/ppermute | solution.py:173
  55.5 24.2 %collective-permute-start.10 = (bf16[256,2176]{1,0:T(8,128)(2,1)S(1)}, bf16[256,2176]{1,0:T(8,128)(2,1)}, u32[]{:S(2)}, u32[]{:S(2)}) collective-permute-start(bf16[256,2176]{1,0:T(8,128)(2,1)S(1)} %get-tuple-element.158.refs_8_.refs_4_.refs_13_.refs_17_), channel_id=1, source_target_pairs={{0,16},{1,17},{2,18},{3,19},{4,20},{5,21},{6,22},{7,23},{8,24},{9,... | collective-permute-start | bytes 3342344 | tf_op jit(solution)/shard_map/ppermute | solution.py:173
  101.9 37.4 %collective-permute-start.17 = (bf16[256,2048]{1,0:T(8,128)(2,1)S(1)}, bf16[256,2048]{1,0:T(8,128)(2,1)S(1)}, u32[]{:S(2)}, u32[]{:S(2)}) collective-permute-start(bf16[256,2048]{1,0:T(8,128)(2,1)S(1)} %get-tuple-element.169.refs_3_.refs_5_), channel_id=1, source_target_pairs={{0,8},{1,9},{2,10},{3,11},{4,12},{5,13},{6,14},{7,15},{8,0},{9,1},... | collective-permute-start | bytes 3145736 | tf_op jit(solution)/shard_map/ppermute | solution.py:173
  103.1 38.7 %collective-permute-start.16 = (bf16[256,2048]{1,0:T(8,128)(2,1)S(1)}, bf16[256,2048]{1,0:T(8,128)(2,1)}, u32[]{:S(2)}, u32[]{:S(2)}) collective-permute-start(bf16[256,2048]{1,0:T(8,128)(2,1)S(1)} %get-tuple-element.169.refs_3_.refs_5_), channel_id=1, source_target_pairs={{0,1},{1,0},{2,3},{3,2},{4,5},{5,4},{6,7},{7,6},{8,9},{9,8},{10,11... | collective-permute-start | bytes 3145736 | tf_op jit(solution)/shard_map/ppermute | solution.py:173
  103.1 39.3 %collective-permute-start.20 = (bf16[256,2048]{1,0:T(8,128)(2,1)}, bf16[256,2048]{1,0:T(8,128)(2,1)}, u32[]{:S(2)}, u32[]{:S(2)}) collective-permute-start(bf16[256,2048]{1,0:T(8,128)(2,1)} %get-tuple-element.170.refs_7_.refs_9_), channel_id=1, source_target_pairs={{0,1},{1,0},{2,3},{3,2},{4,5},{5,4},{6,7},{7,6},{8,9},{9,8},{10,11... | collective-permute-start | bytes 3145736 | tf_op jit(solution)/shard_map/ppermute | solution.py:173
  103.6 35.7 %collective-permute-start.18 = (bf16[256,2048]{1,0:T(8,128)(2,1)}, bf16[256,2048]{1,0:T(8,128)(2,1)S(1)}, u32[]{:S(2)}, u32[]{:S(2)}) collective-permute-start(bf16[256,2048]{1,0:T(8,128)(2,1)} %get-tuple-element.170.refs_7_.refs_9_), channel_id=1, source_target_pairs={{0,16},{1,17},{2,18},{3,19},{4,20},{5,21},{6,22},{7,23},{8,24},{9,... | collective-permute-start | bytes 3145736 | tf_op jit(solution)/shard_map/ppermute | solution.py:173
  141.7 50.2 %collective-permute-start.23 = (bf16[1024,1024]{1,0:T(8,128)(2,1)}, bf16[1024,1024]{1,0:T(8,128)(2,1)}, u32[]{:S(2)}, u32[]{:S(2)}) collective-permute-start(bf16[1024,1024]{1,0:T(8,128)(2,1)} %refs_3_.1), channel_id=1, source_target_pairs={{0,1},{1,0},{2,3},{3,2},{4,5},{5,4},{6,7},{7,6},{8,9},{9,8},{10,11... | collective-permute-start | bytes 6291464 | tf_op jit(solution)/shard_map/ppermute | solution.py:173
  141.8 96.7 %collective-permute-start.24 = (bf16[512,1024]{1,0:T(8,128)(2,1)}, bf16[512,1024]{1,0:T(8,128)(2,1)}, u32[]{:S(2)}, u32[]{:S(2)}) collective-permute-start(bf16[512,1024]{1,0:T(8,128)(2,1)} %get-tuple-element.187), channel_id=1, source_target_pairs={{0,1},{1,0},{2,3},{3,2},{4,5},{5,4},{6,7},{7,6},{8,9},{9,8},{10,11... | collective-permute-start | bytes 3145736 | tf_op jit(solution)/shard_map/ppermute | solution.py:173
  142.4 96.5 %collective-permute-start.26 = (bf16[512,1024]{1,0:T(8,128)(2,1)}, bf16[512,1024]{1,0:T(8,128)(2,1)}, u32[]{:S(2)}, u32[]{:S(2)}) collective-permute-start(bf16[512,1024]{1,0:T(8,128)(2,1)} %get-tuple-element.190), channel_id=1, source_target_pairs={{0,1},{1,0},{2,3},{3,2},{4,5},{5,4},{6,7},{7,6},{8,9},{9,8},{10,11... | collective-permute-start | bytes 3145736 | tf_op jit(solution)/shard_map/ppermute | solution.py:173
  207.1 26.6 %collective-permute-start.28 = (bf16[1024,512]{1,0:T(8,128)(2,1)}, bf16[1024,512]{1,0:T(8,128)(2,1)}, u32[]{:S(2)}, u32[]{:S(2)}) collective-permute-start(bf16[1024,512]{1,0:T(8,128)(2,1)} %get-tuple-element.192), channel_id=1, source_target_pairs={{0,16},{1,17},{2,18},{3,19},{4,20},{5,21},{6,22},{7,23},{8,24},{9,... | collective-permute-start | bytes 3145736 | tf_op jit(solution)/shard_map/ppermute | solution.py:173
  209.8 25.4 %collective-permute-start.29 = (bf16[1024,512]{1,0:T(8,128)(2,1)}, bf16[1024,512]{1,0:T(8,128)(2,1)}, u32[]{:S(2)}, u32[]{:S(2)}) collective-permute-start(bf16[1024,512]{1,0:T(8,128)(2,1)} %get-tuple-element.194), channel_id=1, source_target_pairs={{0,8},{1,9},{2,10},{3,11},{4,12},{5,13},{6,14},{7,15},{8,0},{9,1},... | collective-permute-start | bytes 3145736 | tf_op jit(solution)/shard_map/ppermute | solution.py:173
  209.8 29.1 %collective-permute-start.27 = (bf16[1024,4096]{1,0:T(8,128)(2,1)}, bf16[1024,4096]{1,0:T(8,128)(2,1)}, u32[]{:S(2)}, u32[]{:S(2)}) collective-permute-start(bf16[1024,4096]{1,0:T(8,128)(2,1)} %get-tuple-element.180.refs_1_.refs_6_), channel_id=1, source_target_pairs={{0,1},{1,0},{2,3},{3,2},{4,5},{5,4},{6,7},{7,6},{8,9},{9,8},{10,11... | collective-permute-start | bytes 25165832 | tf_op jit(solution)/shard_map/ppermute | solution.py:173
  238.2 36.9 %collective-permute-start.30 = (bf16[512,512]{1,0:T(8,128)(2,1)}, bf16[512,512]{1,0:T(8,128)(2,1)}, u32[]{:S(2)}, u32[]{:S(2)}) collective-permute-start(bf16[512,512]{1,0:T(8,128)(2,1)} %get-tuple-element.200), channel_id=1, source_target_pairs={{0,8},{1,9},{2,10},{3,11},{4,12},{5,13},{6,14},{7,15},{8,0},{9,1},... | collective-permute-start | bytes 1572872 | tf_op jit(solution)/shard_map/ppermute | solution.py:173
  238.5 36.7 %collective-permute-start.31 = (bf16[512,512]{1,0:T(8,128)(2,1)}, bf16[512,512]{1,0:T(8,128)(2,1)}, u32[]{:S(2)}, u32[]{:S(2)}) collective-permute-start(bf16[512,512]{1,0:T(8,128)(2,1)} %get-tuple-element.202), channel_id=1, source_target_pairs={{0,16},{1,17},{2,18},{3,19},{4,20},{5,21},{6,22},{7,23},{8,24},{9,... | collective-permute-start | bytes 1572872 | tf_op jit(solution)/shard_map/ppermute | solution.py:173
  258.6 37.3 %collective-permute-start.32 = (bf16[256,2560]{1,0:T(8,128)(2,1)}, bf16[256,2560]{1,0:T(8,128)(2,1)}, u32[]{:S(2)}, u32[]{:S(2)}) collective-permute-start(bf16[256,2560]{1,0:T(8,128)(2,1)} %get-tuple-element.207), channel_id=1, source_target_pairs={{0,16},{1,17},{2,18},{3,19},{4,20},{5,21},{6,22},{7,23},{8,24},{9,... | collective-permute-start | bytes 3932168 | tf_op jit(solution)/shard_map/ppermute | solution.py:173
  260.2 35.7 %collective-permute-start.33 = (bf16[256,2560]{1,0:T(8,128)(2,1)}, bf16[256,2560]{1,0:T(8,128)(2,1)}, u32[]{:S(2)}, u32[]{:S(2)}) collective-permute-start(bf16[256,2560]{1,0:T(8,128)(2,1)} %get-tuple-element.209), channel_id=1, source_target_pairs={{0,8},{1,9},{2,10},{3,11},{4,12},{5,13},{6,14},{7,15},{8,0},{9,1},... | collective-permute-start | bytes 3932168 | tf_op jit(solution)/shard_map/ppermute | solution.py:173
  278.4 36.4 %collective-permute-start.39 = (bf16[128,1024]{1,0:T(8,128)(2,1)}, bf16[128,1024]{1,0:T(8,128)(2,1)}, u32[]{:S(2)}, u32[]{:S(2)}) collective-permute-start(bf16[128,1024]{1,0:T(8,128)(2,1)} %get-tuple-element.220), channel_id=1, source_target_pairs={{0,2},{1,3},{2,0},{3,1},{4,6},{5,7},{6,4},{7,5},{8,10},{9,11},{10,... | collective-permute-start | bytes 786440 | tf_op jit(solution)/shard_map/ppermute | solution.py:173
  278.4 36.5 %collective-permute-start.40 = (bf16[128,1024]{1,0:T(8,128)(2,1)}, bf16[128,1024]{1,0:T(8,128)(2,1)}, u32[]{:S(2)}, u32[]{:S(2)}) collective-permute-start(bf16[128,1024]{1,0:T(8,128)(2,1)} %get-tuple-element.221), channel_id=1, source_target_pairs={{0,4},{1,5},{2,6},{3,7},{4,0},{5,1},{6,2},{7,3},{8,12},{9,13},{10,... | collective-permute-start | bytes 786440 | tf_op jit(solution)/shard_map/ppermute | solution.py:173
  278.4 37.0 %collective-permute-start.41 = (bf16[128,1024]{1,0:T(8,128)(2,1)}, bf16[128,1024]{1,0:T(8,128)(2,1)}, u32[]{:S(2)}, u32[]{:S(2)}) collective-permute-start(bf16[128,1024]{1,0:T(8,128)(2,1)} %get-tuple-element.222), channel_id=1, source_target_pairs={{0,6},{1,7},{2,4},{3,5},{4,2},{5,3},{6,0},{7,1},{8,14},{9,15},{10,... | collective-permute-start | bytes 786440 | tf_op jit(solution)/shard_map/ppermute | solution.py:173
  318.6 46.4 %collective-permute-start.49 = (bf16[32,5120]{1,0:T(8,128)(2,1)}, bf16[32,5120]{1,0:T(8,128)(2,1)}, u32[]{:S(2)}, u32[]{:S(2)}) collective-permute-start(bf16[32,5120]{1,0:T(8,128)(2,1)} %get-tuple-element.245), channel_id=1, source_target_pairs={{0,2},{1,3},{2,0},{3,1},{4,6},{5,7},{6,4},{7,5},{8,10},{9,11},{10,... | collective-permute-start | bytes 983048 | tf_op jit(solution)/shard_map/ppermute | solution.py:173
  318.6 46.4 %collective-permute-start.50 = (bf16[32,5120]{1,0:T(8,128)(2,1)}, bf16[32,5120]{1,0:T(8,128)(2,1)}, u32[]{:S(2)}, u32[]{:S(2)}) collective-permute-start(bf16[32,5120]{1,0:T(8,128)(2,1)} %get-tuple-element.246), channel_id=1, source_target_pairs={{0,4},{1,5},{2,6},{3,7},{4,0},{5,1},{6,2},{7,3},{8,12},{9,13},{10,... | collective-permute-start | bytes 983048 | tf_op jit(solution)/shard_map/ppermute | solution.py:173
  319.6 45.9 %collective-permute-start.51 = (bf16[32,5120]{1,0:T(8,128)(2,1)}, bf16[32,5120]{1,0:T(8,128)(2,1)}, u32[]{:S(2)}, u32[]{:S(2)}) collective-permute-start(bf16[32,5120]{1,0:T(8,128)(2,1)} %get-tuple-element.247), channel_id=1, source_target_pairs={{0,6},{1,7},{2,4},{3,5},{4,2},{5,3},{6,0},{7,1},{8,14},{9,15},{10,... | collective-permute-start | bytes 983048 | tf_op jit(solution)/shard_map/ppermute | solution.py:173
  (86 other events, 970.4 us)
Sparse Core Ops, SparseCore 0:
  82.3 84.6 all-gather.1
